TPU v7x, 128 devices: a whole 4x4x4 slice. The times are simulated.
128 devices in a mesh: aux: 16 (over x, y), orb: 8 (over z, core).
Axes of the slice: x: 4, y: 4, z: 4, core: 2. Of those that a mesh axis runs over, the one named last changes fastest.
Arguments:
- tensor: bfloat16 [24, 1024, 32, 256], P('orb', 'aux'), may hold values from -0.41992188 to 0.41992188
- mu_block: int32 [24, 8], P('orb'), may hold values from 0 to 23, as said below
- green_occ: bfloat16 [768, 768], replicated, may hold values from -0.21875 to 0.21875
- green_virt: bfloat16 [768, 768], replicated, may hold values from -0.21875 to 0.21875
Outputs:
- polarizability: float32 [1024, 1024], P('aux', 'orb')
Inputs may be any that keep to these rules, and one draw needn't show every extreme that they name: `mu_block`: row n holds 8 different molecule blocks.
All inputs are finite; a program needn't handle non-finite values.
Results may differ from a plain program's by a relative error of at most 0.0041.
Values may be sent and summed in bfloat16 or wider, within the bound.
No kernel may reach another device: no remote copies, remote signals or barrier semaphores. Data moves between devices by JAX's collectives and lax.ppermute only.
A program may use at most 192 MiB of HBM per device.

v0:
```python
import jax
import jax.numpy as jnp
from jax import lax
from jax.sharding import PartitionSpec as P


def shards(tensor, mu_block, green_occ, green_virt):
    local_blocks, aux_local, width, pair_width = tensor.shape
    orbitals = green_occ.shape[0]
    mol_total = orbitals // width
    virt_cols = green_virt.reshape(orbitals, mol_total, width)[:, mu_block].reshape(
        mol_total, width, local_blocks, pair_width
    )
    occ_rows = green_occ.reshape(mol_total, width, orbitals)[mu_block].reshape(
        local_blocks, pair_width, orbitals
    )
    partial_value = lax.dot_general(
        tensor, occ_rows, (((3,), (1,)), ((0,), (0,))), preferred_element_type=jnp.float32
    )
    partial_value = partial_value.astype(jnp.bfloat16)
    m_part = lax.all_to_all(partial_value, "orb", split_axis=3, concat_axis=0, tiled=True)
    item_count = m_part.shape[1]
    grouped = m_part.reshape(mol_total, item_count, width, local_blocks, width)
    paired_part = lax.dot_general(
        grouped, virt_cols, (((0, 2), (0, 1)), ((3,), (2,))), preferred_element_type=jnp.float32
    )
    paired = paired_part.astype(jnp.bfloat16)
    partial_chi = lax.dot_general(
        paired,
        lax.all_gather(tensor, "aux", axis=1, tiled=True),
        (((0, 2, 3), (0, 2, 3)), ((), ())),
        preferred_element_type=jnp.float32,
    )
    return lax.psum_scatter(partial_chi, "orb", scatter_dimension=1, tiled=True)


def solution(mesh):
    return jax.shard_map(
        shards,
        mesh=mesh,
        in_specs=(P("orb", "aux", None, None), P("orb", None), P(), P()),
        out_specs=P("aux", "orb"),
        check_vma=False,
    )
```

profile of v0, /device:TPU:0, one launch (start us, length us, event | category | flops | bytes accessed | tf_op | source)
XLA Modules:
  0.0 366.6 jit_solution(13873832361434610053)
XLA Ops:
  6.5 0.0 copy-start
  6.5 0.0 all-gather.2.cloned.1.call-start
  6.5 5.4 %copy.18 = bf16[3,64,32,256]{3,1,2,0:T(8,128)(2,1)} copy(bf16[3,64,32,256]{3,2,1,0:T(8,128)(2,1)} %param.4) | data formatting | bytes 6291456 | tf_op args[0]
  11.9 0.0 copy-start.3
  11.9 0.0 all-gather.2.cloned.1.call-update
  12.0 0.7 copy-done.3
  12.6 0.1 reshape.23
  12.7 0.0 copy-done
  12.7 0.6 gather_fusion
  13.4 9.6 %convert_bitcast_fusion = bf16[3,64,32,768]{3,1,2,0:T(8,128)(2,1)} fusion(bf16[3,256,768,1]{2,1,3,0:T(8,128)(2,1)S(1)} %bitcast.47, bf16[3,64,32,256]{3,2,1,0:T(8,128)(2,1)} %param.4), kind=kOutput, calls=%fused_computation.4 | convolution fusion | flops 2420637696 | bytes 13762560 | tf_op jit(solution)/shard_map/dot_general | solution.py:17
  22.9 27.1 %copy.19 = bf16[3,64,32,768]{1,2,0,3:T(8,128)(2,1)} copy(bf16[3,64,32,768]{3,1,2,0:T(8,128)(2,1)} %convert_bitcast_fusion) | data formatting | bytes 18874368 | tf_op jit(solution)/shard_map/convert_element_type | solution.py:20
  50.0 18.5 %reshape.47 = bf16[8,2,294912]{2,1,0:T(2,128)(2,1)} reshape(bf16[768,3,32,64]{3,2,1,0:T(8,128)(2,1)} %bitcast.42) | data formatting | bytes 18874368
  68.5 0.0 copy-start.2
  68.5 5.4 %all-to-all-start = ((bf16[8,2,294912]{2,1,0:T(2,128)(2,1)}), bf16[8,2,294912]{2,1,0:T(2,128)(2,1)}, u32[]{:S(2)}, u32[]{:S(2)}) async-start(bf16[8,2,294912]{2,1,0:T(2,128)(2,1)} %reshape.47), calls=%async_computation | async-start | bytes 18874368 | tf_op jit(solution)/shard_map/all_to_all | solution.py:21
  73.9 0.2 reduce-scatter.2.cloned.1.call-start
  74.1 0.0 copy-done.2
  74.2 0.6 copy.22
  74.8 0.6 gather_fusion.1
  75.4 4.6 %copy.23 = bf16[3,8,768,32]{3,1,2,0:T(8,128)(2,1)} copy(bf16[3,8,768,32]{2,3,1,0:T(8,128)(2,1)S(1)} %bitcast.45) | data formatting | bytes 2359296 | tf_op jit(solution)/shard_map/gather | solution.py:11
  80.1 5.8 %reshape.43 = bf16[24,32,3,256,1]{3,1,0,2,4:T(8,128)(2,1)S(1)} reshape(bf16[768,3,8,32]{3,2,0,1:T(8,128)(2,1)} %bitcast.46) | data formatting | bytes 2359296 | tf_op jit(solution)/shard_map/reshape | solution.py:11
  85.8 94.0 %all-to-all-done = bf16[8,2,294912]{2,1,0:T(2,128)(2,1)} async-done(((bf16[8,2,294912]{2,1,0:T(2,128)(2,1)}), bf16[8,2,294912]{2,1,0:T(2,128)(2,1)}, u32[]{:S(2)}, u32[]{:S(2)}) %all-to-all-start) | async-done | bytes 9437216 | tf_op jit(solution)/shard_map/all_to_all | solution.py:21
  179.9 18.1 %reshape.48 = bf16[768,3,32,64]{3,2,1,0:T(8,128)(2,1)} reshape(bf16[8,2,294912]{2,1,0:T(2,128)(2,1)} %all-to-all-done) | data formatting | bytes 18874368
  198.0 21.3 %copy.21 = bf16[8,3,64,32,96]{2,4,3,1,0:T(8,128)(2,1)} copy(bf16[8,3,64,32,96]{2,3,1,4,0:T(8,128)(2,1)} %bitcast.43) | data formatting | bytes 18874368 | tf_op jit(solution)/shard_map/all_to_all | solution.py:21
  219.3 78.0 %all-gather.2.cloned.1.call-done = bf16[3,1024,32,256]{3,1,2,0:T(8,128)(2,1)} async-done(((bf16[3,64,32,256]{3,1,2,0:T(8,128)(2,1)}), bf16[3,1024,32,256]{3,1,2,0:T(8,128)(2,1)}) %all-gather.2.cloned.1.call-update) | async-done | bytes 50331664 | tf_op jit(solution)/shard_map/all_gather | solution.py:30
  297.3 0.0 copy-start.1
  297.3 31.8 %fusion.9 = f32[64,1024]{1,0:T(8,128)} fusion(bf16[3,1024,32,256]{3,1,2,0:T(8,128)(2,1)} %all-gather.2.cloned.1.call-done, bf16[24,64,32,3,32]{1,4,3,2,0:T(8,128)(2,1)} %bitcast.41, bf16[24,32,3,256,1]{3,1,0,2,4:T(8,128)(2,1)S(1)} %reshape.43), kind=kOutput, calls=%fused_computation.8 | convolution fusion | flops 5638717440 | bytes 61210624 | tf_op jit(solution)/shard_map/dot_general | solution.py:28
  329.1 0.0 reduce-scatter.2.cloned.1.call-update
  329.1 30.6 %reduce-scatter.2.cloned.1.call-done = f32[64,128]{1,0:T(8,128)} async-done(((f32[64,1024]{1,0:T(8,128)}), f32[64,128]{1,0:T(8,128)}) %reduce-scatter.2.cloned.1.call-update) | async-done | bytes 32784 | tf_op jit(solution)/shard_map/reduce_scatter | solution.py:34
  359.7 0.0 copy-done.1
  (2 shorter events, 0.0 us)
Async XLA Ops:
  6.5 6.2 %copy-start = (bf16[768,768]{1,0:T(8,128)(2,1)S(1)}, bf16[768,768]{1,0:T(8,128)(2,1)}, u32[]{:S(2)}) copy-start(bf16[768,768]{1,0:T(8,128)(2,1)} %param.6) | copy-start | bytes 3538948
  6.5 290.8 %all-gather.2.cloned.1.call-start = ((), (), s32[]{:S(2)}) async-start(), calls=%async_computation.2 | async-start | bytes 53477376 | tf_op jit(solution)/shard_map/all_gather | solution.py:30
  11.9 0.7 copy-start.3
  68.5 5.6 %copy-start.2 = (bf16[768,768]{1,0:T(8,128)(2,1)S(1)}, bf16[768,768]{1,0:T(8,128)(2,1)}, u32[]{:S(2)}) copy-start(bf16[768,768]{1,0:T(8,128)(2,1)} %param.7) | copy-start | bytes 3538948
  68.5 111.4 %all-to-all-start = ((bf16[8,2,294912]{2,1,0:T(2,128)(2,1)}), bf16[8,2,294912]{2,1,0:T(2,128)(2,1)}, u32[]{:S(2)}, u32[]{:S(2)}) async-start(bf16[8,2,294912]{2,1,0:T(2,128)(2,1)} %reshape.47), calls=%async_computation | async-start | bytes 18874368 | tf_op jit(solution)/shard_map/all_to_all | solution.py:21
  73.9 285.8 %reduce-scatter.2.cloned.1.call-start = ((), (), s32[]{:S(2)}) async-start(), calls=%async_computation.3 | async-start | bytes 294912 | tf_op jit(solution)/shard_map/reduce_scatter | solution.py:34
  297.3 62.4 %copy-start.1 = (bf16[768,768]{1,0:T(8,128)(2,1)S(1)}, bf16[768,768]{1,0:T(8,128)(2,1)}, u32[]{:S(2)}) copy-start(bf16[768,768]{1,0:T(8,128)(2,1)} %param.6) | copy-start | bytes 3538948
Sparse Core Ops, SparseCore 0:
  12.1 285.1 all-gather.1
  329.2 30.4 reduce-scatter.1
where the time goes:
time: 368 us; the launch traced here: 367 us
  waiting for transfers between devices  203 us (55%)
  local copies, waits for them, and re-layouts  103 us (28%)
  matrix products  41.3 us (11%)
  between operations  13.5 us (4%)
  starting transfers between devices  5.62 us (2%)
    all_to_all x1, waiting for transfers between devices, shards(): lax.all_to_all(partial_value, 'orb', split_axis=3, concat_axis=0, tiled=T...  94 us
    all_gather x1, waiting for transfers between devices, shards(): lax.all_gather(tensor, 'aux', axis=1, tiled=True)  78 us
    unnamed x12, local copies, waits for them, and re-layouts  43.4 us
    dot_general x1, matrix products, shards(): lax.dot_general(paired, lax.all_gather(tensor, 'aux', axis=1, tiled=True)...  31.8 us
    reduce_scatter x1, waiting for transfers between devices, shards(): return lax.psum_scatter(partial_chi, 'orb', scatter_dimension=1, tiled=True)  30.6 us
    convert_element_type x1, local copies, waits for them, and re-layouts, shards(): partial_value = partial_value.astype(jnp.bfloat16)  27.1 us
    all_to_all x1, local copies, waits for them, and re-layouts, shards(): lax.all_to_all(partial_value, 'orb', split_axis=3, concat_axis=0, tiled=T...  21.3 us
    dot_general x1, matrix products, shards(): lax.dot_general(tensor, occ_rows, (((3,), (1,)), ((0,), (0,))), preferred...  9.56 us
  transfers between devices with their start and end apart: 3, of which 3 were waited for; matrix products, arithmetic and copies ran while one was open for 29% of the time, Pallas kernels for 0%

commit v1 on v0

v1 whole, which is shorter than its diff:
```python
import functools

import jax
import jax.numpy as jnp
from jax import lax
from jax.experimental import pallas as pl
from jax.experimental.pallas import tpu as pltpu
from jax.sharding import Mesh
from jax.sharding import PartitionSpec as P

NX, NY, NZ, NC = 4, 4, 4, 2
NXY = NX * NY
BF, F32 = jnp.bfloat16, jnp.float32
LIMIT = 56 * 1024 * 1024


def swap_matrix(outer, inner):
    n = outer * inner
    row = lax.broadcasted_iota(jnp.int32, (n, n), 0)
    col = lax.broadcasted_iota(jnp.int32, (n, n), 1)
    source = (row % outer) * inner + row // outer
    return jnp.where(col == source, 1.0, 0.0).astype(BF)


def regroup_kernel(tensor_ref, swap_ref, out_ref):
    rows = tensor_ref[0].reshape(-1, tensor_ref.shape[-1])
    got = jnp.dot(swap_ref[...], rows, preferred_element_type=F32).astype(BF)
    out_ref[...] = got.reshape(out_ref.shape)


def regroup(tensor, swap):
    blocks, aux, width, pair = tensor.shape
    return pl.pallas_call(
        regroup_kernel,
        grid=(blocks, aux // 16),
        in_specs=[
            pl.BlockSpec((1, 16, width, pair), lambda m, g: (m, g, 0, 0)),
            pl.BlockSpec(swap.shape, lambda m, g: (0, 0)),
        ],
        out_specs=pl.BlockSpec((NXY, 1, 2, 16, pair), lambda m, g: (0, m, 0, g, 0)),
        out_shape=jax.ShapeDtypeStruct((NXY, blocks, 2, aux, pair), BF),
        compiler_params=pltpu.CompilerParams(vmem_limit_bytes=LIMIT),
    )(tensor, swap)


def pair_kernel(mu_nu, mu_lam, *refs):
    pieces = refs[:8]
    occ_ref, virt_ref, swap_ref, out_ref, turned, stage = refs[8:]
    per = mu_nu.shape[1]
    half = occ_ref.shape[1]
    width, pair = 32, 256
    for g in range(6):
        for q in range(4):
            t = g * 4 + q
            piece, m = divmod(t, 3)
            rows = pieces[piece][m].reshape(16 * width, pair)
            occ = jnp.concatenate(
                [
                    occ_ref[pl.ds(pl.multiple_of(mu_nu[t, k] * width, width), width), :]
                    for k in range(per)
                ],
                axis=0,
            )
            got = jnp.dot(rows, occ, preferred_element_type=F32).astype(BF)
            stage[:, q * width : (q + 1) * width, :] = got.reshape(16, width, half)
        for p in range(16):
            turned[p, :, g * 128 : (g + 1) * 128] = stage[p].T

    @pl.loop(0, 4)
    def _(z):
        for m in range(3):
            lam = z * 3 + m
            left = turned[:, pl.ds(pl.multiple_of(lam * width, width), width), :]
            left = left.reshape(16 * width, -1)
            virt = jnp.concatenate(
                [
                    virt_ref[pl.ds(pl.multiple_of(mu_lam[lam, k] * width, width), width), :]
                    for k in range(per)
                ],
                axis=0,
            )
            got = lax.dot_general(
                left, virt, (((1,), (1,)), ((), ())), preferred_element_type=F32
            ).astype(BF)
            got = jnp.dot(swap_ref[...], got, preferred_element_type=F32).astype(BF)
            out_ref[:, z, m, :, :] = got.reshape(16, 32, pair)


def make_paired(mu_nu, mu_lam, pieces, occ, virt, swap):
    orbitals, half = occ.shape
    vmem = pl.BlockSpec(memory_space=pltpu.VMEM)
    smem = pl.BlockSpec(memory_space=pltpu.SMEM)
    return pl.pallas_call(
        pair_kernel,
        in_specs=[smem, smem] + [vmem] * 11,
        out_specs=vmem,
        out_shape=jax.ShapeDtypeStruct((NXY, NZ, 3, 32, 256), BF),
        scratch_shapes=[
            pltpu.VMEM((16, half, orbitals), BF),
            pltpu.VMEM((16, 128, half), BF),
        ],
        compiler_params=pltpu.CompilerParams(vmem_limit_bytes=LIMIT),
    )(mu_nu, mu_lam, *pieces, occ, virt, swap)


def chi_kernel(core, a_ref, b_ref, out_ref):
    @pl.when(pl.program_id(0) == 0)
    def _():
        out_ref[...] = jnp.zeros_like(out_ref)

    for r in range(2):
        a = a_ref[:, 0, r * 16 : (r + 1) * 16, :].reshape(-1, a_ref.shape[-1])
        for z in range(4):
            b = b_ref[z, 0, :, 0, r].reshape(-1, b_ref.shape[-1])
            out_ref[:, z, :] += lax.dot_general(
                a, b, (((1,), (1,)), ((), ())), preferred_element_type=F32
            )


def chi_half(core, a, b):
    return pl.pallas_call(
        chi_kernel,
        grid_spec=pltpu.PrefetchScalarGridSpec(
            num_scalar_prefetch=1,
            grid=(3,),
            in_specs=[
                pl.BlockSpec((64, 1, 32, 256), lambda m, core: (0, m, 0, 0)),
                pl.BlockSpec(
                    (4, 1, 2, 1, 2, 64, 256), lambda m, core: (0, core[0], 0, m, 0, 0, 0)
                ),
            ],
            out_specs=pl.BlockSpec((1024, 4, 128), lambda m, core: (0, 0, 0)),
        ),
        out_shape=jax.ShapeDtypeStruct((1024, 4, 128), F32),
        compiler_params=pltpu.CompilerParams(vmem_limit_bytes=LIMIT),
    )(core, a, b)


def shards(tensor, mu_block, green_occ, green_virt):
    z, core = lax.axis_index("z"), lax.axis_index("core")
    orbitals = green_occ.shape[0]
    other = [(0, 1), (1, 0)]
    swap = swap_matrix(16, 32)

    by_z = tensor.reshape(3, NZ, 16, 32, 256)
    arrived = []
    for s in range(NZ):
        block = lax.dynamic_index_in_dim(by_z, (z + s) % NZ, 1, keepdims=False)
        if s:
            block = lax.ppermute(block, "z", [(i, (i + s) % NZ) for i in range(NZ)])
        arrived.append(block)
    pieces = []
    for block in arrived:
        pieces += [block, lax.ppermute(block, "core", other)]

    q_side = lax.all_to_all(
        regroup(tensor, swap), ("x", "y"), split_axis=0, concat_axis=0, tiled=True
    )

    mu_all = lax.all_gather(mu_block, ("z", "core"), axis=0, tiled=True)
    order = jnp.stack(
        [((z - s) % NZ) * NC + c for s in range(NZ) for c in (core, 1 - core)]
    )
    mu_nu = mu_all.reshape(NZ * NC, 3, -1)[order].reshape(NZ * NC * 3, -1)
    mu_lam = lax.dynamic_index_in_dim(
        mu_all.reshape(NZ, NC, 3, -1), core, 1, keepdims=False
    ).reshape(NZ * 3, -1)
    occ = lax.dynamic_index_in_dim(
        green_occ.reshape(orbitals, NZ, NC, -1), core, 2, keepdims=False
    ).reshape(orbitals, -1)
    virt = green_virt.reshape(NZ * NC, -1, orbitals)[order].reshape(orbitals, orbitals).T

    paired = make_paired(mu_nu, mu_lam, pieces, occ, virt, swap)
    p_side = lax.all_to_all(
        paired.reshape(NXY * NZ, 3, 32, 256), ("x", "y", "z"), 0, 0, tiled=True
    )
    q_side = q_side.reshape(4, 2, 2, 3, 2, 64, 256)
    given = chi_half((1 - core).reshape(1), p_side, q_side)
    kept = chi_half(core.reshape(1), p_side, q_side)
    chi = kept + lax.ppermute(given, "core", other)

    chi = chi.reshape(NXY, 64, NZ, 128).transpose(0, 2, 1, 3).reshape(NXY * NZ, 64, 128)
    shares = lax.all_to_all(chi, ("x", "y", "z"), 0, 0, tiled=True)
    return shares.reshape(NXY * NZ, 64, 128).sum(0)


def solution(mesh):
    mesh = Mesh(mesh.devices.reshape(NX, NY, NZ, NC), ("x", "y", "z", "core"))
    return jax.shard_map(
        shards,
        mesh=mesh,
        in_specs=(P(("z", "core"), ("x", "y"), None, None), P(("z", "core"), None), P(), P()),
        out_specs=P(("x", "y"), ("z", "core")),
        check_vma=False,
    )
```

time: 368 us -> 222 us (0.60)
  waiting for transfers between devices: 203 us -> 35.1 us
  blocking collectives: 0 us -> 97.6 us
  local copies, waits for them, and re-layouts: 103 us -> 11.1 us
  Pallas kernels: 0 us -> 60.6 us
  matrix products: 41.3 us -> 0 us
  between operations: 13.5 us -> 0.16 us
  starting transfers between devices: 5.62 us -> 13 us
  other arithmetic: 0.01 us -> 4.26 us
    all_to_all x1, waiting for transfers between devices: 94 us -> 0.01 us  [shards(): lax.all_to_all(regroup(tensor, swap), ('x', 'y'), split_axis=0, concat_ax...]
    all_to_all x0 -> x2, blocking collectives: none -> 86.3 us  [the longest x1 51.2 us: shards(): lax.all_to_all(paired.reshape(NXY * NZ, 3, 32, 256), ('x', 'y', 'z'), 0,...]
    all_gather x1 -> x0, waiting for transfers between devices: 78 us -> none  [shards(): lax.all_gather(tensor, 'aux', axis=1, tiled=True)]
    pallas_call x0 -> x4, Pallas kernels: none -> 60.6 us  [the longest x2 33.7 us: chi_half(): pl.pallas_call(chi_kernel, grid_spec=pltpu.PrefetchScalarGridSpec(num_sca...]
    unnamed x12 -> x8, local copies, waits for them, and re-layouts: 43.4 us -> 1.58 us
    dot_general x2 -> x0, matrix products: 41.3 us -> none  [the longest x1 31.8 us: shards(): lax.dot_general(paired, lax.all_gather(tensor, 'aux', axis=1, tiled=True)...]
    ppermute x0 -> x8, waiting for transfers between devices: none -> 35.1 us  [the longest x3 35.1 us: shards(): block = lax.ppermute(block, 'z', [(i, (i + s) % NZ) for i in range(NZ)])]
    reduce_scatter x1 -> x0, waiting for transfers between devices: 30.6 us -> none  [shards(): return lax.psum_scatter(partial_chi, 'orb', scatter_dimension=1, tiled=True)]
  transfers between devices with their start and end apart: 3 -> 9, of which waited for: 3 -> 2; matrix products, arithmetic and copies ran while one was open for 29% -> 5% of each run, Pallas kernels for 0% -> 15%
where the time goes in v1:
time: 222 us
  blocking collectives  97.6 us (44%)
  Pallas kernels  60.6 us (27%)
  waiting for transfers between devices  35.1 us (16%)
  starting transfers between devices  13 us (6%)
  local copies, waits for them, and re-layouts  11.1 us (5%)
  other arithmetic  4.26 us (2%)
    all_to_all x1, blocking collectives, shards(): lax.all_to_all(paired.reshape(NXY * NZ, 3, 32, 256), ('x', 'y', 'z'), 0,...  51.2 us
    all_to_all x1, blocking collectives, shards(): shares = lax.all_to_all(chi, ('x', 'y', 'z'), 0, 0, tiled=True)  35.2 us
    ppermute x3, waiting for transfers between devices, shards(): block = lax.ppermute(block, 'z', [(i, (i + s) % NZ) for i in range(NZ)])  35.1 us
    pallas_call x2, Pallas kernels, chi_half(): pl.pallas_call(chi_kernel, grid_spec=pltpu.PrefetchScalarGridSpec(num_sca...  33.7 us
    pallas_call x1, Pallas kernels, make_paired(): pl.pallas_call(pair_kernel, in_specs=[smem, smem] + [vmem] * 11, out_spec...  17.1 us
    all_gather x1, blocking collectives, shards(): mu_all = lax.all_gather(mu_block, ('z', 'core'), axis=0, tiled=True)  11.2 us
    pallas_call x1, Pallas kernels, regroup(): pl.pallas_call(regroup_kernel, grid=(blocks, aux // 16), in_specs=[pl.Blo...  9.67 us
    all_to_all x1, starting transfers between devices, shards(): lax.all_to_all(regroup(tensor, swap), ('x', 'y'), split_axis=0, concat_ax...  7.17 us
  transfers between devices with their start and end apart: 9, of which 2 were waited for; matrix products, arithmetic and copies ran while one was open for 5% of the time, Pallas kernels for 15%

profile of v1, /device:TPU:0, one launch (start us, length us, event | category | flops | bytes accessed | tf_op | source)
XLA Modules:
  0.0 221.8 jit_solution(11885753543774343069)
XLA Ops:
  0.0 0.0 copy-start
  0.0 1.3 select_convert_fusion.refs_10_.swap_ref
  1.4 9.7 %shard_map.47 = bf16[16,3,2,64,256]{4,3,2,1,0:T(8,128)(2,1)} custom-call(bf16[3,64,32,256]{3,2,1,0:T(8,128)(2,1)} %tensor_ref.1, bf16[512,512]{1,0:T(8,128)(2,1)} %select_convert_fusion.refs_10_.swap_ref), custom_call_target="tpu_custom_call" | custom-call | tf_op jit(solution)/shard_map/pallas_call | solution.py:33
  11.0 7.2 %all-to-all-start.1 = ((bf16[16,3,2,64,256]{4,3,2,1,0:T(8,128)(2,1)}), bf16[16,3,2,64,256]{4,3,2,1,0:T(8,128)(2,1)}, u32[]{:S(2)}, u32[]{:S(2)}) async-start(bf16[16,3,2,64,256]{4,3,2,1,0:T(8,128)(2,1)} %shard_map.47), calls=%async_computation.1 | async-start | bytes 6291456 | tf_op jit(solution)/shard_map/all_to_all | solution.py:156
  18.3 0.0 copy-start.2
  18.3 2.2 dynamic-slice_bitcast_fusion
  20.5 0.0 copy-start.1
  20.5 4.1 %collective-permute-start.5 = (bf16[3,16,32,256]{3,2,1,0:T(8,128)(2,1)S(1)}, bf16[3,16,32,256]{3,2,1,0:T(8,128)(2,1)}, u32[]{:S(2)}, u32[]{:S(2)}) collective-permute-start(bf16[3,16,32,256]{3,2,1,0:T(8,128)(2,1)S(1)} %get-tuple-element.5), channel_id=1, source_target_pairs={{0,6},{2,0},{4,2},{6,4},{1,7},{3,1},{5,3},{7,5},{8,14},{10,8},{12,... | collective-permute-start | bytes 2359304 | tf_op jit(solution)/shard_map/ppermute | solution.py:150
  24.6 0.0 collective-permute-start.3
  24.6 1.3 collective-permute-start.1
  25.9 0.0 collective-permute-start
  25.9 32.1 %collective-permute-done.5.refs_6_ = bf16[3,16,32,256]{3,2,1,0:T(8,128)(2,1)} collective-permute-done((bf16[3,16,32,256]{3,2,1,0:T(8,128)(2,1)S(1)}, bf16[3,16,32,256]{3,2,1,0:T(8,128)(2,1)}, u32[]{:S(2)}, u32[]{:S(2)}) %collective-permute-start.5) | collective-permute-done | bytes 786464 | tf_op jit(solution)/shard_map/ppermute | solution.py:150
  58.0 0.0 collective-permute-start.6
  58.0 0.0 collective-permute-done.3.refs_4_
  58.0 0.5 collective-permute-start.4
  58.5 3.0 %collective-permute-done.1.refs_2_ = bf16[3,16,32,256]{3,2,1,0:T(8,128)(2,1)} collective-permute-done((bf16[3,16,32,256]{3,2,1,0:T(8,128)(2,1)S(1)}, bf16[3,16,32,256]{3,2,1,0:T(8,128)(2,1)}, u32[]{:S(2)}, u32[]{:S(2)}) %collective-permute-start.1) | collective-permute-done | bytes 786464 | tf_op jit(solution)/shard_map/ppermute | solution.py:150
  61.5 0.0 collective-permute-start.2
  61.5 0.0 copy-done.2
  61.5 11.2 %all-gather = s32[8,3,8]{2,1,0:T(4,128)S(1)} all-gather(s32[1,3,8]{2,1,0:T(4,128)S(1)} %bitcast.56), channel_id=1, replica_groups=mesh['x'=4,'y'=4,'z'=4,'core'=2] {'z','core'}, dimensions={0}, use_global_device_ids=true | all-gather | bytes 864 | tf_op jit(solution)/shard_map/all_gather | solution.py:160
  72.7 0.6 reshape.364.mu_lam
  73.3 0.1 stack.35
  73.5 0.6 gather_fusion
  74.0 0.6 reshape.362.mu_nu
  74.6 0.0 copy-done
  74.7 0.6 gather_fusion.1
  75.3 1.5 copy.26
  76.8 0.0 copy-done.1
  76.8 1.6 copy.25
  78.3 0.9 constant_dynamic-slice_fusion
  79.2 2.1 copy.27.refs_8_
  81.3 0.0 collective-permute-done.refs_1_
  81.3 0.0 collective-permute-done.6.refs_7_
  81.3 0.0 collective-permute-done.4.refs_5_
  81.3 0.0 collective-permute-done.2.refs_3_
  81.4 17.1 %shard_map.46 = bf16[16,4,3,32,256]{4,3,2,1,0:T(8,128)(2,1)} custom-call(s32[24,8]{1,0:T(8,128)} %reshape.362.mu_nu, s32[12,8]{1,0:T(8,128)} %reshape.364.mu_lam, bf16[3,16,32,256]{3,2,1,0:T(8,128)(2,1)} %copy-done.1, bf16[3,16,32,256]{3,2,1,0:T(8,128)(2,1)} %collective-permute-done.refs_1_, bf16[3,16,32,256]{3,2,1,0:T(8,128)(2,1)} %collective-permute-done.1.refs_2_, ...), custom_call_target="tpu_custom_call" | custom-call | tf_op jit(solution)/shard_map/pallas_call | solution.py:93
  98.5 0.0 all-to-all-done.1
  98.5 51.2 %all_to_all.15.a_ref = bf16[64,3,32,256]{3,2,1,0:T(8,128)(2,1)} all-to-all(bf16[64,3,32,256]{3,2,1,0:T(8,128)(2,1)} %bitcast.48), channel_id=1, replica_groups=mesh['x'=4,'y'=4,'z'=4,'core'=2] {'x','y','z'}, dimensions={0} | all-to-all | bytes 6291456 | tf_op jit(solution)/shard_map/all_to_all | solution.py:174
  149.7 16.9 %shard_map.49 = f32[1024,4,128]{2,1,0:T(4,128)} custom-call(s32[1]{0:T(128)} %bitcast.24.core, bf16[64,3,32,256]{3,2,1,0:T(8,128)(2,1)} %all_to_all.15.a_ref, bf16[4,2,2,3,2,64,256]{6,5,4,3,2,1,0:T(8,128)(2,1)} %bitcast.23.b_ref), custom_call_target="tpu_custom_call" | custom-call | tf_op jit(solution)/shard_map/pallas_call | solution.py:121
  166.5 0.0 collective-permute-start.7
  166.5 16.9 %shard_map.48 = f32[1024,4,128]{2,1,0:T(4,128)} custom-call(s32[1]{0:T(128)} %bitcast.core, bf16[64,3,32,256]{3,2,1,0:T(8,128)(2,1)} %all_to_all.15.a_ref, bf16[4,2,2,3,2,64,256]{6,5,4,3,2,1,0:T(8,128)(2,1)} %bitcast.23.b_ref), custom_call_target="tpu_custom_call" | custom-call | tf_op jit(solution)/shard_map/pallas_call | solution.py:121
  183.4 0.0 collective-permute-done.7
  183.4 2.1 add.138
  185.6 0.3 copy.28
  185.9 35.2 %all_to_all.16 = f32[64,64,128]{2,1,0:T(8,128)S(1)} all-to-all(f32[64,64,128]{2,1,0:T(8,128)S(1)} %bitcast.50), channel_id=1, replica_groups=mesh['x'=4,'y'=4,'z'=4,'core'=2] {'x','y','z'}, dimensions={0} | all-to-all | bytes 4194304 | tf_op jit(solution)/shard_map/all_to_all | solution.py:183
  221.0 0.8 reduce_sum.9
  (6 shorter events, 0.0 us)
Async XLA Ops:
  0.0 74.7 %copy-start = (bf16[768,768]{1,0:T(8,128)(2,1)S(1)}, bf16[768,768]{1,0:T(8,128)(2,1)}, u32[]{:S(2)}) copy-start(bf16[768,768]{1,0:T(8,128)(2,1)} %param.7) | copy-start | bytes 3538948
  11.0 87.5 %all-to-all-start.1 = ((bf16[16,3,2,64,256]{4,3,2,1,0:T(8,128)(2,1)}), bf16[16,3,2,64,256]{4,3,2,1,0:T(8,128)(2,1)}, u32[]{:S(2)}, u32[]{:S(2)}) async-start(bf16[16,3,2,64,256]{4,3,2,1,0:T(8,128)(2,1)} %shard_map.47), calls=%async_computation.1 | async-start | bytes 6291456 | tf_op jit(solution)/shard_map/all_to_all | solution.py:156
  18.3 43.2 %copy-start.2 = (s32[3,8]{1,0:T(4,128)S(1)}, s32[3,8]{1,0:T(4,128)}, u32[]{:S(2)}) copy-start(s32[3,8]{1,0:T(4,128)} %param.5) | copy-start | bytes 292
  20.5 56.3 %copy-start.1 = (bf16[3,16,32,256]{3,2,1,0:T(8,128)(2,1)}, bf16[3,16,32,256]{3,2,1,0:T(8,128)(2,1)S(1)}, u32[]{:S(2)}) copy-start(bf16[3,16,32,256]{3,2,1,0:T(8,128)(2,1)S(1)} %get-tuple-element.8.refs_0_) | copy-start | bytes 2359300
  20.5 37.5 %collective-permute-start.5 = (bf16[3,16,32,256]{3,2,1,0:T(8,128)(2,1)S(1)}, bf16[3,16,32,256]{3,2,1,0:T(8,128)(2,1)}, u32[]{:S(2)}, u32[]{:S(2)}) collective-permute-start(bf16[3,16,32,256]{3,2,1,0:T(8,128)(2,1)S(1)} %get-tuple-element.5), channel_id=1, source_target_pairs={{0,6},{2,0},{4,2},{6,4},{1,7},{3,1},{5,3},{7,5},{8,14},{10,8},{12,... | collective-permute-start | bytes 2359304 | tf_op jit(solution)/shard_map/ppermute | solution.py:150
  24.6 33.4 %collective-permute-start.3 = (bf16[3,16,32,256]{3,2,1,0:T(8,128)(2,1)S(1)}, bf16[3,16,32,256]{3,2,1,0:T(8,128)(2,1)}, u32[]{:S(2)}, u32[]{:S(2)}) collective-permute-start(bf16[3,16,32,256]{3,2,1,0:T(8,128)(2,1)S(1)} %get-tuple-element.6), channel_id=1, source_target_pairs={{0,4},{2,6},{4,0},{6,2},{1,5},{3,7},{5,1},{7,3},{8,12},{10,14},{12... | collective-permute-start | bytes 2359304 | tf_op jit(solution)/shard_map/ppermute | solution.py:150
  24.6 36.9 %collective-permute-start.1 = (bf16[3,16,32,256]{3,2,1,0:T(8,128)(2,1)S(1)}, bf16[3,16,32,256]{3,2,1,0:T(8,128)(2,1)}, u32[]{:S(2)}, u32[]{:S(2)}) collective-permute-start(bf16[3,16,32,256]{3,2,1,0:T(8,128)(2,1)S(1)} %get-tuple-element.7), channel_id=1, source_target_pairs={{0,2},{2,4},{4,6},{6,0},{1,3},{3,5},{5,7},{7,1},{8,10},{10,12},{12... | collective-permute-start | bytes 2359304 | tf_op jit(solution)/shard_map/ppermute | solution.py:150
  25.9 55.5 %collective-permute-start = (bf16[3,16,32,256]{3,2,1,0:T(8,128)(2,1)S(1)}, bf16[3,16,32,256]{3,2,1,0:T(8,128)(2,1)}, u32[]{:S(2)}, u32[]{:S(2)}) collective-permute-start(bf16[3,16,32,256]{3,2,1,0:T(8,128)(2,1)S(1)} %get-tuple-element.8.refs_0_), channel_id=1, source_target_pairs={{0,1},{1,0},{2,3},{3,2},{4,5},{5,4},{6,7},{7,6},{8,9},{9,8},{10,11... | collective-permute-start | bytes 2359304 | tf_op jit(solution)/shard_map/ppermute | solution.py:154
  58.0 23.4 %collective-permute-start.6 = (bf16[3,16,32,256]{3,2,1,0:T(8,128)(2,1)}, bf16[3,16,32,256]{3,2,1,0:T(8,128)(2,1)}, u32[]{:S(2)}, u32[]{:S(2)}) collective-permute-start(bf16[3,16,32,256]{3,2,1,0:T(8,128)(2,1)} %collective-permute-done.5.refs_6_), channel_id=1, source_target_pairs={{0,1},{1,0},{2,3},{3,2},{4,5},{5,4},{6,7},{7,6},{8,9},{9,8},{10,11... | collective-permute-start | bytes 2359304 | tf_op jit(solution)/shard_map/ppermute | solution.py:154
  58.0 23.4 %collective-permute-start.4 = (bf16[3,16,32,256]{3,2,1,0:T(8,128)(2,1)}, bf16[3,16,32,256]{3,2,1,0:T(8,128)(2,1)}, u32[]{:S(2)}, u32[]{:S(2)}) collective-permute-start(bf16[3,16,32,256]{3,2,1,0:T(8,128)(2,1)} %collective-permute-done.3.refs_4_), channel_id=1, source_target_pairs={{0,1},{1,0},{2,3},{3,2},{4,5},{5,4},{6,7},{7,6},{8,9},{9,8},{10,11... | collective-permute-start | bytes 2359304 | tf_op jit(solution)/shard_map/ppermute | solution.py:154
  61.5 19.9 %collective-permute-start.2 = (bf16[3,16,32,256]{3,2,1,0:T(8,128)(2,1)}, bf16[3,16,32,256]{3,2,1,0:T(8,128)(2,1)}, u32[]{:S(2)}, u32[]{:S(2)}) collective-permute-start(bf16[3,16,32,256]{3,2,1,0:T(8,128)(2,1)} %collective-permute-done.1.refs_2_), channel_id=1, source_target_pairs={{0,1},{1,0},{2,3},{3,2},{4,5},{5,4},{6,7},{7,6},{8,9},{9,8},{10,11... | collective-permute-start | bytes 2359304 | tf_op jit(solution)/shard_map/ppermute | solution.py:154
  166.5 16.9 %collective-permute-start.7 = (f32[1024,4,128]{2,1,0:T(4,128)}, f32[1024,4,128]{2,1,0:T(4,128)S(1)}, u32[]{:S(2)}, u32[]{:S(2)}) collective-permute-start(f32[1024,4,128]{2,1,0:T(4,128)} %shard_map.49), channel_id=1, source_target_pairs={{0,1},{1,0},{2,3},{3,2},{4,5},{5,4},{6,7},{7,6},{8,9},{9,8},{10,11... | collective-permute-start | bytes 6291464 | tf_op jit(solution)/shard_map/ppermute | solution.py:180

commit v2 on v1

v2 whole, which is shorter than its diff:
```python
import jax
import jax.numpy as jnp
from jax import lax
from jax.experimental import pallas as pl
from jax.experimental.pallas import tpu as pltpu
from jax.sharding import Mesh
from jax.sharding import PartitionSpec as P

NX, NY, NZ, NC = 4, 4, 4, 2
NXY = NX * NY
BF, F32 = jnp.bfloat16, jnp.float32
LIMIT = 56 * 1024 * 1024


def regroup_kernel(tensor_ref, out_ref):
    out_ref[:, 0] = jnp.swapaxes(tensor_ref[0], 0, 1).reshape(
        NXY, 2, tensor_ref.shape[1], tensor_ref.shape[3]
    )


def regroup(tensor):
    blocks, aux, width, pair = tensor.shape
    return pl.pallas_call(
        regroup_kernel,
        grid=(blocks,),
        in_specs=[pl.BlockSpec((1, aux, width, pair), lambda m: (m, 0, 0, 0))],
        out_specs=pl.BlockSpec((NXY, 1, 2, aux, pair), lambda m: (0, m, 0, 0, 0)),
        out_shape=jax.ShapeDtypeStruct((NXY, blocks, 2, aux, pair), BF),
        compiler_params=pltpu.CompilerParams(vmem_limit_bytes=LIMIT),
        cost_estimate=pl.CostEstimate(
            flops=1000, bytes_accessed=1000, transcendentals=0
        ),
    )(tensor)


def gathered(ref, mu, t, per, width):
    return jnp.concatenate(
        [ref[pl.ds(pl.multiple_of(mu[t, k] * width, width), width), :] for k in range(per)],
        axis=0,
    )


def pair_kernel(z_ref, *refs):
    mus, pieces = refs[:4], refs[4:12]
    occ_ref, virt_ref, out_ref, turned, stage = refs[12:]
    per, half, width, pair = mus[0].shape[1], occ_ref.shape[1], 32, 256
    for g in range(6):
        for q in range(4):
            piece, m = divmod(g * 4 + q, 3)
            rows = pieces[piece][m].reshape(16 * width, pair)
            occ = gathered(occ_ref, mus[piece // 2], piece % 2 * 3 + m, per, width)
            got = jnp.dot(rows, occ, preferred_element_type=F32).astype(BF)
            stage[:, q * width : (q + 1) * width, :] = got.reshape(16, width, half)
        for p in range(16):
            turned[p, :, g * 128 : (g + 1) * 128] = stage[p].T

    for s in range(NZ):
        z = lax.rem(z_ref[0] - s + NZ, NZ)
        for m in range(3):
            lam = pl.multiple_of((z * 3 + m) * width, width)
            left = turned[:, pl.ds(lam, width), :].reshape(16 * width, -1)
            virt = gathered(virt_ref, mus[s], m, per, width)
            got = lax.dot_general(
                left, virt, (((1,), (1,)), ((), ())), preferred_element_type=F32
            ).astype(BF)
            got = jnp.swapaxes(got.reshape(16, width, pair), 0, 1)
            out_ref[:, z, m, :, :] = got.reshape(NXY, 32, pair)


def make_paired(z, mus, pieces, occ, virt):
    orbitals, half = occ.shape
    vmem = pl.BlockSpec(memory_space=pltpu.VMEM)
    smem = pl.BlockSpec(memory_space=pltpu.SMEM)
    return pl.pallas_call(
        pair_kernel,
        in_specs=[smem] * 5 + [vmem] * 10,
        out_specs=vmem,
        out_shape=jax.ShapeDtypeStruct((NXY, NZ, 3, 32, 256), BF),
        scratch_shapes=[
            pltpu.VMEM((16, half, orbitals), BF),
            pltpu.VMEM((16, 128, half), BF),
        ],
        compiler_params=pltpu.CompilerParams(vmem_limit_bytes=LIMIT),
        cost_estimate=pl.CostEstimate(
            flops=22_000_000_000, bytes_accessed=12_000_000, transcendentals=0
        ),
    )(z, *mus, *pieces, occ, virt)


def chi_kernel(core, a_ref, b_ref, out_ref):
    pair = a_ref.shape[-1]
    a = jnp.concatenate(
        [a_ref[:, 0, r * 16 : (r + 1) * 16, :].reshape(-1, pair) for r in range(2)], axis=1
    )
    b = jnp.concatenate([b_ref[:, 0, :, 0, r].reshape(-1, pair) for r in range(2)], axis=1)
    got = lax.dot_general(a, b, (((1,), (1,)), ((), ())), preferred_element_type=F32)
    first = pl.program_id(0) == 0

    @pl.when(first)
    def _():
        for z in range(NZ):
            out_ref[:, z] = got[:, z * 128 : (z + 1) * 128].reshape(NXY, 64, 128)

    @pl.when(jnp.logical_not(first))
    def _():
        for z in range(NZ):
            out_ref[:, z] += got[:, z * 128 : (z + 1) * 128].reshape(NXY, 64, 128)


def chi_half(core, a, b):
    return pl.pallas_call(
        chi_kernel,
        grid_spec=pltpu.PrefetchScalarGridSpec(
            num_scalar_prefetch=1,
            grid=(3,),
            in_specs=[
                pl.BlockSpec((64, 1, 32, 256), lambda m, core: (0, m, 0, 0)),
                pl.BlockSpec(
                    (4, 1, 2, 1, 2, 64, 256), lambda m, core: (0, core[0], 0, m, 0, 0, 0)
                ),
            ],
            out_specs=pl.BlockSpec((NXY, NZ, 64, 128), lambda m, core: (0, 0, 0, 0)),
        ),
        out_shape=jax.ShapeDtypeStruct((NXY, NZ, 64, 128), F32),
        compiler_params=pltpu.CompilerParams(vmem_limit_bytes=LIMIT),
        cost_estimate=pl.CostEstimate(
            flops=1_700_000_000, bytes_accessed=7_000_000, transcendentals=0
        ),
    )(core, a, b)


def shards(tensor, mu_block, green_occ, green_virt):
    z, core = lax.axis_index("z"), lax.axis_index("core")
    orbitals = green_occ.shape[0]
    other = [(0, 1), (1, 0)]
    around = [[(i, (i + s) % NZ) for i in range(NZ)] for s in range(NZ)]

    by_z = tensor.reshape(3, NZ, 16, 32, 256)
    blocks = [
        lax.dynamic_index_in_dim(by_z, (z + s) % NZ, 1, keepdims=False) for s in range(NZ)
    ]
    mu_pair = jnp.concatenate([mu_block, lax.ppermute(mu_block, "core", other)], axis=0)
    mus = [lax.ppermute(mu_pair, "z", around[s]) for s in range(1, NZ)]
    mus, blocks = lax.optimization_barrier((mus, blocks))
    arrived = [lax.ppermute(blocks[s], "z", around[s]) for s in range(1, NZ)]
    own_other = lax.ppermute(blocks[0], "core", other)

    occ = lax.dynamic_index_in_dim(
        green_occ.reshape(orbitals, NZ, NC, -1), core, 2, keepdims=False
    ).reshape(orbitals, -1)
    order = jnp.stack(
        [((z - s) % NZ) * NC + c for s in range(NZ) for c in (core, 1 - core)]
    )
    virt = green_virt.reshape(NZ * NC, -1, orbitals)[order].reshape(orbitals, orbitals).T
    held, own_other, occ, virt = lax.optimization_barrier((tensor, own_other, occ, virt))
    q_side = lax.all_to_all(
        regroup(held), ("x", "y"), split_axis=0, concat_axis=0, tiled=True
    )


    pieces = [blocks[0], own_other]
    for block in arrived:
        pieces += [block, lax.ppermute(block, "core", other)]
    paired = make_paired(z.reshape(1), [mu_pair, *mus], pieces, occ, virt)
    p_side = lax.all_to_all(
        paired.reshape(NXY * NZ, 3, 32, 256), ("x", "y", "z"), 0, 0, tiled=True
    )
    q_side = q_side.reshape(4, 2, 2, 3, 2, 64, 256)
    given = chi_half((1 - core).reshape(1), p_side, q_side)
    kept = chi_half(core.reshape(1), p_side, q_side)
    chi = (kept + lax.ppermute(given, "core", other)).astype(BF)
    shares = lax.all_to_all(
        chi.reshape(NXY * NZ, 64, 128), ("x", "y", "z"), 0, 0, tiled=True
    )
    return shares.astype(F32).sum(0)


def solution(mesh):
    mesh = Mesh(mesh.devices.reshape(NX, NY, NZ, NC), ("x", "y", "z", "core"))
    return jax.shard_map(
        shards,
        mesh=mesh,
        in_specs=(P(("z", "core"), ("x", "y"), None, None), P(("z", "core"), None), P(), P()),
        out_specs=P(("x", "y"), ("z", "core")),
        check_vma=False,
    )
```

time: 222 us -> 162 us (0.73)
  Pallas kernels: 60.6 us -> 28.8 us
  blocking collectives: 97.6 us -> 72.2 us
  starting transfers between devices: 13 us -> 17.5 us
  waiting for transfers between devices: 35.1 us -> 31.2 us
  local copies, waits for them, and re-layouts: 11.1 us -> 8.56 us
    pallas_call x2, Pallas kernels: 33.7 us -> 12.1 us  [chi_half(): pl.pallas_call(chi_kernel, grid_spec=pltpu.PrefetchScalarGridSpec(num_sca...]
    ppermute x4 -> x9, waiting for transfers between devices: 35.1 us -> 19.9 us  [the longest x3 18.3 us: shards(): arrived = [lax.ppermute(blocks[s], 'z', around[s]) for s in range(1, NZ)]]
    all_gather x1 -> x0, blocking collectives: 11.2 us -> none  [shards(): mu_all = lax.all_gather(mu_block, ('z', 'core'), axis=0, tiled=True)]
    all_to_all x1, blocking collectives: 35.2 us -> 24.4 us  [shards(): lax.all_to_all(chi.reshape(NXY * NZ, 64, 128), ('x', 'y', 'z'), 0, 0, til...]
    pallas_call x2, Pallas kernels: 26.8 us -> 16.7 us  [the longest x1 11.9 us: make_paired(): pl.pallas_call(pair_kernel, in_specs=[smem] * 5 + [vmem] * 10, out_specs=...]
    all_to_all x1, waiting for transfers between devices: 0.01 us -> 9.24 us  [shards(): lax.all_to_all(regroup(held), ('x', 'y'), split_axis=0, concat_axis=0, ti...]
    ppermute x4 -> x9, starting transfers between devices: 5.36 us -> 10.4 us  [the longest x3 5.44 us: shards(): mus = [lax.ppermute(mu_pair, 'z', around[s]) for s in range(1, NZ)]]
    reshape x4 -> x0, local copies, waits for them, and re-layouts: 3.63 us -> none  [the longest x1 2.12 us: shards(): occ = lax.dynamic_index_in_dim(green_occ.reshape(orbitals, NZ, NC, -1), c...]
  transfers between devices with their start and end apart: 9 -> 13, of which waited for: 2 -> 8; matrix products, arithmetic and copies ran while one was open for 5% -> 5% of each run, Pallas kernels for 15% -> 14%
where the time goes in v2:
time: 162 us
  blocking collectives  72.2 us (45%)
  waiting for transfers between devices  31.2 us (19%)
  Pallas kernels  28.8 us (18%)
  starting transfers between devices  17.5 us (11%)
  local copies, waits for them, and re-layouts  8.56 us (5%)
  other arithmetic  3.54 us (2%)
    all_to_all x1, blocking collectives, shards(): lax.all_to_all(paired.reshape(NXY * NZ, 3, 32, 256), ('x', 'y', 'z'), 0,...  47.7 us
    all_to_all x1, blocking collectives, shards(): lax.all_to_all(chi.reshape(NXY * NZ, 64, 128), ('x', 'y', 'z'), 0, 0, til...  24.4 us
    ppermute x3, waiting for transfers between devices, shards(): arrived = [lax.ppermute(blocks[s], 'z', around[s]) for s in range(1, NZ)]  18.3 us
    pallas_call x2, Pallas kernels, chi_half(): pl.pallas_call(chi_kernel, grid_spec=pltpu.PrefetchScalarGridSpec(num_sca...  12.1 us
    pallas_call x1, Pallas kernels, make_paired(): pl.pallas_call(pair_kernel, in_specs=[smem] * 5 + [vmem] * 10, out_specs=...  11.9 us
    all_to_all x1, waiting for transfers between devices, shards(): lax.all_to_all(regroup(held), ('x', 'y'), split_axis=0, concat_axis=0, ti...  9.24 us
    all_to_all x1, starting transfers between devices, shards(): lax.all_to_all(regroup(held), ('x', 'y'), split_axis=0, concat_axis=0, ti...  7.08 us
    ppermute x3, starting transfers between devices, shards(): mus = [lax.ppermute(mu_pair, 'z', around[s]) for s in range(1, NZ)]  5.44 us
  transfers between devices with their start and end apart: 13, of which 8 were waited for; matrix products, arithmetic and copies ran while one was open for 5% of the time, Pallas kernels for 14%

profile of v2, /device:TPU:0, one launch (start us, length us, event | category | flops | bytes accessed | tf_op | source)
XLA Modules:
  0.0 161.9 jit_solution(2037455309733869568)
XLA Ops:
  0.0 0.0 copy-start
  0.0 0.0 collective-permute-start
  0.0 1.4 collective-permute-done
  1.4 0.7 pad_add_fusion.refs_0_
  2.1 4.2 %collective-permute-start.3 = (s32[6,8]{1,0:T(8,128)S(1)}, s32[6,8]{1,0:T(8,128)S(1)}, u32[]{:S(2)}, u32[]{:S(2)}) collective-permute-start(s32[6,8]{1,0:T(8,128)S(1)} %pad_add_fusion.refs_0_), channel_id=1, source_target_pairs={{0,6},{2,0},{4,2},{6,4},{1,7},{3,1},{5,3},{7,5},{8,14},{10,8},{12,... | collective-permute-start | bytes 584 | tf_op jit(solution)/shard_map/ppermute | solution.py:143
  6.2 0.0 collective-permute-start.2
  6.2 1.3 collective-permute-start.1
  7.5 3.6 %dynamic-slice_bitcast_fusion = (bf16[3,16,32,256]{3,2,1,0:T(8,128)(2,1)}, bf16[3,16,32,256]{3,2,1,0:T(8,128)(2,1)}, bf16[3,16,32,256]{3,2,1,0:T(8,128)(2,1)}, bf16[3,16,32,256]{3,2,1,0:T(8,128)(2,1)}) fusion(bf16[3,4,16,32,256]{4,3,2,1,0:T(8,128)(2,1)} %bitcast.39, s32[]{:T(128)S(6)} %select_n.75, s32[]{:T(128)S(6)} %select_n.73, s32[]{:T(128)S(6)} %select_n.71, ...), kind=kLoop, calls=%fused_computation.3 | loop fusion | bytes 6291472 | tf_op jit(solution)/shard_map/jit(dynamic_index_in_dim)/squeeze | solution.py:140
  11.1 0.0 copy-done.1
  11.1 0.0 collective-permute-done.3.refs_3_
  11.1 0.0 copy-start.4
  11.2 0.2 collective-permute-done.2.refs_2_
  11.4 0.0 collective-permute-done.1.refs_1_
  11.4 0.1 collective-permute-start.4
  11.5 2.1 %collective-permute-start.5 = (bf16[3,16,32,256]{3,2,1,0:T(8,128)(2,1)}, bf16[3,16,32,256]{3,2,1,0:T(8,128)(2,1)}, u32[]{:S(2)}, u32[]{:S(2)}) collective-permute-start(bf16[3,16,32,256]{3,2,1,0:T(8,128)(2,1)} %get-tuple-element.21), channel_id=1, source_target_pairs={{0,2},{2,4},{4,6},{6,0},{1,3},{3,5},{5,7},{7,1},{8,10},{10,12},{12... | collective-permute-start | bytes 2359304 | tf_op jit(solution)/shard_map/ppermute | solution.py:145
  13.6 1.2 collective-permute-start.7
  14.8 1.6 collective-permute-start.9
  16.4 0.1 stack.35
  16.5 0.0 copy-done
  16.5 0.6 gather_fusion
  17.1 1.5 copy.15
  18.6 0.0 copy-done.4
  18.6 0.0 copy-done.5
  18.6 0.0 copy-done.6
  18.6 1.6 copy.14
  20.2 0.0 collective-permute-done.4.refs_5_
  20.2 4.8 %shard_map.47 = bf16[16,3,2,64,256]{4,3,2,1,0:T(8,128)(2,1)} custom-call(bf16[3,64,32,256]{3,2,1,0:T(8,128)(2,1)} %tensor_ref), custom_call_target="tpu_custom_call" | custom-call | flops 1000 | bytes 1000 | tf_op jit(solution)/shard_map/pallas_call | solution.py:23
  25.0 7.1 %all-to-all-start.1 = ((bf16[16,3,2,64,256]{4,3,2,1,0:T(8,128)(2,1)}), bf16[16,3,2,64,256]{4,3,2,1,0:T(8,128)(2,1)}, u32[]{:S(2)}, u32[]{:S(2)}) async-start(bf16[16,3,2,64,256]{4,3,2,1,0:T(8,128)(2,1)} %shard_map.47), calls=%async_computation.1 | async-start | bytes 6291456 | tf_op jit(solution)/shard_map/all_to_all | solution.py:156
  32.1 1.2 collective-permute-done.5.refs_6_
  33.4 0.0 collective-permute-start.6
  33.4 16.5 %collective-permute-done.7.refs_8_ = bf16[3,16,32,256]{3,2,1,0:T(8,128)(2,1)} collective-permute-done((bf16[3,16,32,256]{3,2,1,0:T(8,128)(2,1)}, bf16[3,16,32,256]{3,2,1,0:T(8,128)(2,1)}, u32[]{:S(2)}, u32[]{:S(2)}) %collective-permute-start.7) | collective-permute-done | bytes 786464 | tf_op jit(solution)/shard_map/ppermute | solution.py:145
  49.8 0.0 collective-permute-start.8
  49.8 0.6 collective-permute-done.9.refs_10_
  50.4 0.0 collective-permute-start.10
  50.4 1.1 copy.16.refs_12_
  51.5 0.0 collective-permute-done.6.refs_7_
  51.5 0.8 collective-permute-done.8.refs_9_
  52.3 1.3 collective-permute-done.10.refs_11_
  53.6 11.9 %shard_map.46 = bf16[16,4,3,32,256]{4,3,2,1,0:T(8,128)(2,1)} custom-call(s32[1]{0:T(128)} %bitcast.1.z_ref, s32[6,8]{1,0:T(8,128)} %copy-done.1, s32[6,8]{1,0:T(8,128)} %copy-done.6, s32[6,8]{1,0:T(8,128)} %copy-done.5, s32[6,8]{1,0:T(8,128)} %copy-done.4, bf16[3,16,32,256]{3,2,1,0:T(8,128)(2,1)} %get-tuple-element.19.refs_4_, ...), custom_call_target="tpu_custom_call" | custom-call | flops 22000001024 | bytes 12000000 | tf_op jit(solution)/shard_map/pallas_call | solution.py:74
  65.5 9.2 %all-to-all-done.1 = bf16[16,3,2,64,256]{4,3,2,1,0:T(8,128)(2,1)} async-done(((bf16[16,3,2,64,256]{4,3,2,1,0:T(8,128)(2,1)}), bf16[16,3,2,64,256]{4,3,2,1,0:T(8,128)(2,1)}, u32[]{:S(2)}, u32[]{:S(2)}) %all-to-all-start.1) | async-done | bytes 3145760 | tf_op jit(solution)/shard_map/all_to_all | solution.py:156
  74.7 47.7 %all_to_all.15.a_ref = bf16[64,3,32,256]{3,2,1,0:T(8,128)(2,1)} all-to-all(bf16[64,3,32,256]{3,2,1,0:T(8,128)(2,1)} %bitcast.42), channel_id=1, replica_groups=mesh['x'=4,'y'=4,'z'=4,'core'=2] {'x','y','z'}, dimensions={0} | all-to-all | bytes 6291456 | tf_op jit(solution)/shard_map/all_to_all | solution.py:165
  122.5 6.1 %shard_map.49 = f32[16,4,64,128]{3,2,1,0:T(8,128)} custom-call(s32[1]{0:T(128)} %bitcast.23.core, bf16[64,3,32,256]{3,2,1,0:T(8,128)(2,1)} %all_to_all.15.a_ref, bf16[4,2,2,3,2,64,256]{6,5,4,3,2,1,0:T(8,128)(2,1)} %bitcast.22.b_ref), custom_call_target="tpu_custom_call" | custom-call | flops 1700000000 | bytes 7000000 | tf_op jit(solution)/shard_map/pallas_call | solution.py:111
  128.5 0.0 collective-permute-start.11
  128.5 6.1 %shard_map.48 = f32[16,4,64,128]{3,2,1,0:T(8,128)} custom-call(s32[1]{0:T(128)} %bitcast.core, bf16[64,3,32,256]{3,2,1,0:T(8,128)(2,1)} %all_to_all.15.a_ref, bf16[4,2,2,3,2,64,256]{6,5,4,3,2,1,0:T(8,128)(2,1)} %bitcast.22.b_ref), custom_call_target="tpu_custom_call" | custom-call | flops 1700000000 | bytes 7000000 | tf_op jit(solution)/shard_map/pallas_call | solution.py:111
  134.6 0.0 collective-permute-done.11
  134.6 2.1 %add_convert_fusion = bf16[16,4,64,128]{3,2,1,0:T(8,128)(2,1)S(1)} fusion(f32[16,4,64,128]{3,2,1,0:T(8,128)} %shard_map.48, f32[16,4,64,128]{3,2,1,0:T(8,128)S(1)} %collective-permute-done.11), kind=kLoop, calls=%fused_computation.2 | loop fusion | flops 1048576 | bytes 5242880 | tf_op jit(solution)/shard_map/convert_element_type | solution.py:171
  136.7 24.4 %all_to_all.16 = bf16[64,64,128]{2,1,0:T(8,128)(2,1)S(1)} all-to-all(bf16[64,64,128]{2,1,0:T(8,128)(2,1)S(1)} %bitcast.41), channel_id=1, replica_groups=mesh['x'=4,'y'=4,'z'=4,'core'=2] {'x','y','z'}, dimensions={0} | all-to-all | bytes 2097152 | tf_op jit(solution)/shard_map/all_to_all | solution.py:172
  161.1 0.8 convert_reduce_fusion
  (10 shorter events, 0.1 us)
Async XLA Ops:
  0.0 16.5 %copy-start = (bf16[768,768]{1,0:T(8,128)(2,1)S(1)}, bf16[768,768]{1,0:T(8,128)(2,1)}, u32[]{:S(2)}) copy-start(bf16[768,768]{1,0:T(8,128)(2,1)} %param.7) | copy-start | bytes 3538948
  0.0 1.4 collective-permute-start
  2.1 9.1 %copy-start.1 = (s32[6,8]{1,0:T(8,128)}, s32[6,8]{1,0:T(8,128)S(1)}, u32[]{:S(2)}) copy-start(s32[6,8]{1,0:T(8,128)S(1)} %pad_add_fusion.refs_0_) | copy-start | bytes 580
  2.1 9.1 %collective-permute-start.3 = (s32[6,8]{1,0:T(8,128)S(1)}, s32[6,8]{1,0:T(8,128)S(1)}, u32[]{:S(2)}, u32[]{:S(2)}) collective-permute-start(s32[6,8]{1,0:T(8,128)S(1)} %pad_add_fusion.refs_0_), channel_id=1, source_target_pairs={{0,6},{2,0},{4,2},{6,4},{1,7},{3,1},{5,3},{7,5},{8,14},{10,8},{12,... | collective-permute-start | bytes 584 | tf_op jit(solution)/shard_map/ppermute | solution.py:143
  6.2 5.1 %collective-permute-start.2 = (s32[6,8]{1,0:T(8,128)S(1)}, s32[6,8]{1,0:T(8,128)S(1)}, u32[]{:S(2)}, u32[]{:S(2)}) collective-permute-start(s32[6,8]{1,0:T(8,128)S(1)} %pad_add_fusion.refs_0_), channel_id=1, source_target_pairs={{0,4},{2,6},{4,0},{6,2},{1,5},{3,7},{5,1},{7,3},{8,12},{10,14},{12... | collective-permute-start | bytes 584 | tf_op jit(solution)/shard_map/ppermute | solution.py:143
  6.2 5.1 %collective-permute-start.1 = (s32[6,8]{1,0:T(8,128)S(1)}, s32[6,8]{1,0:T(8,128)S(1)}, u32[]{:S(2)}, u32[]{:S(2)}) collective-permute-start(s32[6,8]{1,0:T(8,128)S(1)} %pad_add_fusion.refs_0_), channel_id=1, source_target_pairs={{0,2},{2,4},{4,6},{6,0},{1,3},{3,5},{5,7},{7,1},{8,10},{10,12},{12... | collective-permute-start | bytes 584 | tf_op jit(solution)/shard_map/ppermute | solution.py:143
  11.1 7.5 %copy-start.4 = (s32[6,8]{1,0:T(8,128)}, s32[6,8]{1,0:T(8,128)S(1)}, u32[]{:S(2)}) copy-start(s32[6,8]{1,0:T(8,128)S(1)} %collective-permute-done.3.refs_3_) | copy-start | bytes 580
  11.4 7.2 %copy-start.5 = (s32[6,8]{1,0:T(8,128)}, s32[6,8]{1,0:T(8,128)S(1)}, u32[]{:S(2)}) copy-start(s32[6,8]{1,0:T(8,128)S(1)} %collective-permute-done.2.refs_2_) | copy-start | bytes 580
  11.4 7.2 %copy-start.6 = (s32[6,8]{1,0:T(8,128)}, s32[6,8]{1,0:T(8,128)S(1)}, u32[]{:S(2)}) copy-start(s32[6,8]{1,0:T(8,128)S(1)} %collective-permute-done.1.refs_1_) | copy-start | bytes 580
  11.4 8.9 %collective-permute-start.4 = (bf16[3,16,32,256]{3,2,1,0:T(8,128)(2,1)}, bf16[3,16,32,256]{3,2,1,0:T(8,128)(2,1)}, u32[]{:S(2)}, u32[]{:S(2)}) collective-permute-start(bf16[3,16,32,256]{3,2,1,0:T(8,128)(2,1)} %get-tuple-element.19.refs_4_), channel_id=1, source_target_pairs={{0,1},{1,0},{2,3},{3,2},{4,5},{5,4},{6,7},{7,6},{8,9},{9,8},{10,11... | collective-permute-start | bytes 2359304 | tf_op jit(solution)/shard_map/ppermute | solution.py:146
  11.5 21.9 %collective-permute-start.5 = (bf16[3,16,32,256]{3,2,1,0:T(8,128)(2,1)}, bf16[3,16,32,256]{3,2,1,0:T(8,128)(2,1)}, u32[]{:S(2)}, u32[]{:S(2)}) collective-permute-start(bf16[3,16,32,256]{3,2,1,0:T(8,128)(2,1)} %get-tuple-element.21), channel_id=1, source_target_pairs={{0,2},{2,4},{4,6},{6,0},{1,3},{3,5},{5,7},{7,1},{8,10},{10,12},{12... | collective-permute-start | bytes 2359304 | tf_op jit(solution)/shard_map/ppermute | solution.py:145
  13.6 36.2 %collective-permute-start.7 = (bf16[3,16,32,256]{3,2,1,0:T(8,128)(2,1)}, bf16[3,16,32,256]{3,2,1,0:T(8,128)(2,1)}, u32[]{:S(2)}, u32[]{:S(2)}) collective-permute-start(bf16[3,16,32,256]{3,2,1,0:T(8,128)(2,1)} %get-tuple-element.22), channel_id=1, source_target_pairs={{0,4},{2,6},{4,0},{6,2},{1,5},{3,7},{5,1},{7,3},{8,12},{10,14},{12... | collective-permute-start | bytes 2359304 | tf_op jit(solution)/shard_map/ppermute | solution.py:145
  14.8 35.6 %collective-permute-start.9 = (bf16[3,16,32,256]{3,2,1,0:T(8,128)(2,1)}, bf16[3,16,32,256]{3,2,1,0:T(8,128)(2,1)}, u32[]{:S(2)}, u32[]{:S(2)}) collective-permute-start(bf16[3,16,32,256]{3,2,1,0:T(8,128)(2,1)} %get-tuple-element.23), channel_id=1, source_target_pairs={{0,6},{2,0},{4,2},{6,4},{1,7},{3,1},{5,3},{7,5},{8,14},{10,8},{12,... | collective-permute-start | bytes 2359304 | tf_op jit(solution)/shard_map/ppermute | solution.py:145
  25.0 49.7 %all-to-all-start.1 = ((bf16[16,3,2,64,256]{4,3,2,1,0:T(8,128)(2,1)}), bf16[16,3,2,64,256]{4,3,2,1,0:T(8,128)(2,1)}, u32[]{:S(2)}, u32[]{:S(2)}) async-start(bf16[16,3,2,64,256]{4,3,2,1,0:T(8,128)(2,1)} %shard_map.47), calls=%async_computation.1 | async-start | bytes 6291456 | tf_op jit(solution)/shard_map/all_to_all | solution.py:156
  33.4 18.1 %collective-permute-start.6 = (bf16[3,16,32,256]{3,2,1,0:T(8,128)(2,1)}, bf16[3,16,32,256]{3,2,1,0:T(8,128)(2,1)S(1)}, u32[]{:S(2)}, u32[]{:S(2)}) collective-permute-start(bf16[3,16,32,256]{3,2,1,0:T(8,128)(2,1)} %collective-permute-done.5.refs_6_), channel_id=1, source_target_pairs={{0,1},{1,0},{2,3},{3,2},{4,5},{5,4},{6,7},{7,6},{8,9},{9,8},{10,11... | collective-permute-start | bytes 2359304 | tf_op jit(solution)/shard_map/ppermute | solution.py:163
  49.8 2.5 %collective-permute-start.8 = (bf16[3,16,32,256]{3,2,1,0:T(8,128)(2,1)}, bf16[3,16,32,256]{3,2,1,0:T(8,128)(2,1)S(1)}, u32[]{:S(2)}, u32[]{:S(2)}) collective-permute-start(bf16[3,16,32,256]{3,2,1,0:T(8,128)(2,1)} %collective-permute-done.7.refs_8_), channel_id=1, source_target_pairs={{0,1},{1,0},{2,3},{3,2},{4,5},{5,4},{6,7},{7,6},{8,9},{9,8},{10,11... | collective-permute-start | bytes 2359304 | tf_op jit(solution)/shard_map/ppermute | solution.py:163
  50.4 3.2 %collective-permute-start.10 = (bf16[3,16,32,256]{3,2,1,0:T(8,128)(2,1)}, bf16[3,16,32,256]{3,2,1,0:T(8,128)(2,1)}, u32[]{:S(2)}, u32[]{:S(2)}) collective-permute-start(bf16[3,16,32,256]{3,2,1,0:T(8,128)(2,1)} %collective-permute-done.9.refs_10_), channel_id=1, source_target_pairs={{0,1},{1,0},{2,3},{3,2},{4,5},{5,4},{6,7},{7,6},{8,9},{9,8},{10,11... | collective-permute-start | bytes 2359304 | tf_op jit(solution)/shard_map/ppermute | solution.py:163
  51.5 2.1 %copy-start.2 = (bf16[3,16,32,256]{3,2,1,0:T(8,128)(2,1)}, bf16[3,16,32,256]{3,2,1,0:T(8,128)(2,1)S(1)}, u32[]{:S(2)}) copy-start(bf16[3,16,32,256]{3,2,1,0:T(8,128)(2,1)S(1)} %collective-permute-done.6.refs_7_) | copy-start | bytes 2359300
  52.3 1.3 copy-start.3
  128.5 6.1 %collective-permute-start.11 = (f32[16,4,64,128]{3,2,1,0:T(8,128)}, f32[16,4,64,128]{3,2,1,0:T(8,128)S(1)}, u32[]{:S(2)}, u32[]{:S(2)}) collective-permute-start(f32[16,4,64,128]{3,2,1,0:T(8,128)} %shard_map.49), channel_id=1, source_target_pairs={{0,1},{1,0},{2,3},{3,2},{4,5},{5,4},{6,7},{7,6},{8,9},{9,8},{10,11... | collective-permute-start | bytes 6291464 | tf_op jit(solution)/shard_map/ppermute | solution.py:171

commit v3 on v2

v3 whole, which is shorter than its diff:
```python
import jax
import jax.numpy as jnp
from jax import lax
from jax.experimental import pallas as pl
from jax.experimental.pallas import tpu as pltpu
from jax.sharding import Mesh
from jax.sharding import PartitionSpec as P

NX, NY, NZ, NC = 4, 4, 4, 2
NXY = NX * NY
BF, F32 = jnp.bfloat16, jnp.float32
LIMIT = 30 * 1024 * 1024
PAIR_FLOPS = 22_000_000_000


def spread_kernel(z_ref, tensor_ref, mu_ref, *outs):
    regrouped, blocks = outs[0], outs[1:]
    rows, pair = 16 * tensor_ref.shape[2], tensor_ref.shape[3]
    regrouped[:, 0] = jnp.swapaxes(tensor_ref[0], 0, 1).reshape(
        NXY, 2, tensor_ref.shape[1], pair
    )
    for s in range(NZ):
        z = lax.rem(z_ref[0] + s, NZ)
        blocks[s][0, :rows] = tensor_ref[0, pl.ds(z * 16, 16)].reshape(rows, pair)
        blocks[s][0, rows:] = mu_ref[0]


def spread(z, tensor, mu_rows):
    blocks, aux, width, pair = tensor.shape
    piece = (16 * width + 16, pair)
    return pl.pallas_call(
        spread_kernel,
        grid_spec=pltpu.PrefetchScalarGridSpec(
            num_scalar_prefetch=1,
            grid=(blocks,),
            in_specs=[
                pl.BlockSpec((1, aux, width, pair), lambda m, z: (m, 0, 0, 0)),
                pl.BlockSpec((1, 16, pair), lambda m, z: (m, 0, 0)),
            ],
            out_specs=[pl.BlockSpec((NXY, 1, 2, aux, pair), lambda m, z: (0, m, 0, 0, 0))]
            + [pl.BlockSpec((1, *piece), lambda m, z: (m, 0, 0))] * NZ,
        ),
        out_shape=[pltpu.HBM((NXY, blocks, 2, aux, pair), BF)]
        + [jax.ShapeDtypeStruct((blocks, *piece), BF)] * NZ,
        compiler_params=pltpu.CompilerParams(vmem_limit_bytes=LIMIT),
        cost_estimate=pl.CostEstimate(flops=1000, bytes_accessed=1000, transcendentals=0),
    )(z, tensor, mu_rows)


def gathered(ref, mu, t, per, width):
    return jnp.concatenate(
        [ref[pl.ds(pl.multiple_of(mu[t, k] * width, width), width), :] for k in range(per)],
        axis=0,
    )


def occupied(piece, mu, m, at, occ_ref, stage):
    per, half, width = mu.shape[1], occ_ref.shape[1], 32
    occ = gathered(occ_ref, mu, at[0], per, width)
    got = jnp.dot(piece[m, : 16 * width], occ, preferred_element_type=F32).astype(BF)
    stage[:, at[1] : at[1] + width, :] = got.reshape(16, width, half)


def early_kernel(mu_own, mu_other, own, other, occ_ref, out_ref, stage):
    stage[:, :64, :] = jnp.zeros((16, 64, stage.shape[2]), BF)
    for n in range(6):
        piece, mu = ((own, mu_own), (other, mu_other))[n // 3]
        occupied(piece, mu, n % 3, (n % 3, 64 + n * 32), occ_ref, stage)
    for p in range(16):
        for g in range(2):
            out_ref[p, :, g * 128 : (g + 1) * 128] = stage[p, g * 128 : (g + 1) * 128].T


def make_early(mu_own, mu_other, own, other, occ):
    half = occ.shape[1]
    vmem = pl.BlockSpec(memory_space=pltpu.VMEM)
    smem = pl.BlockSpec(memory_space=pltpu.SMEM)
    return pl.pallas_call(
        early_kernel,
        in_specs=[smem] * 2 + [vmem] * 3,
        out_specs=vmem,
        out_shape=jax.ShapeDtypeStruct((16, half, 256), BF),
        scratch_shapes=[pltpu.VMEM((16, 256, half), BF)],
        compiler_params=pltpu.CompilerParams(vmem_limit_bytes=LIMIT),
        cost_estimate=pl.CostEstimate(flops=1000, bytes_accessed=1000, transcendentals=0),
    )(mu_own, mu_other, own, other, occ)


def pair_kernel(z_ref, mu_own, mu_other, *refs):
    pieces, refs = refs[:6], refs[6:]
    occ_ref, virt_ref, early_ref, out_ref, turned, stage, result, out_sems = refs
    per, width, pair = mu_own.shape[1], 32, 256
    for n in range(18):
        piece, m = divmod(n, 3)
        mu = mu_other if piece % 2 else mu_own
        at = ((piece // 2 + 1) * 3 + m, n % 4 * width)
        occupied(pieces[piece], mu, m, at, occ_ref, stage)
        if n % 4 == 3:
            for p in range(16):
                turned[p, :, (n - 3) * width : (n + 1) * width] = stage[p].T
    turned[:, :, 512:] = early_ref[...]
    for p in range(16):
        turned[p, :, 512:576] = stage[p, :64].T
    stores = []
    for z in range(NZ):
        s = lax.rem(z_ref[0] - z + NZ, NZ)
        for m in range(3):
            lam = (z * 3 + m) * width
            left = turned[:, lam : lam + width, :].reshape(16 * width, -1)
            virt = gathered(virt_ref, mu_own, s * 3 + m, per, width)
            got = lax.dot_general(
                left, virt, (((1,), (1,)), ((), ())), preferred_element_type=F32
            ).astype(BF)
            got = jnp.swapaxes(got.reshape(16, width, pair), 0, 1)
            result[z, :, m, :, :] = got.reshape(NXY, 32, pair)
        stores.append(
            pltpu.make_async_copy(result.at[z], out_ref.at[:, z], out_sems.at[z])
        )
        stores[z].start()
    for store in stores:
        store.wait()


def make_paired(z, mu_own, mu_other, pieces, occ, virt, early):
    orbitals, half = occ.shape
    smem = pl.BlockSpec(memory_space=pltpu.SMEM)
    return pl.pallas_call(
        pair_kernel,
        in_specs=[smem] * 3 + [pl.BlockSpec(memory_space=pltpu.VMEM)] * 9,
        out_specs=pl.BlockSpec(memory_space=pltpu.HBM),
        out_shape=pltpu.HBM((NXY, NZ, 3, 32, 256), BF),
        scratch_shapes=[
            pltpu.VMEM((16, half, orbitals), BF),
            pltpu.VMEM((16, 128, half), BF),
            pltpu.VMEM((NZ, NXY, 3, 32, 256), BF),
            pltpu.SemaphoreType.DMA((NZ,)),
        ],
        compiler_params=pltpu.CompilerParams(vmem_limit_bytes=LIMIT),
        cost_estimate=pl.CostEstimate(
            flops=PAIR_FLOPS, bytes_accessed=12_000_000, transcendentals=0
        ),
    )(z, mu_own, mu_other, *pieces, occ, virt, early)


def listed_kernel(mu_ref, *refs):
    per = mu_ref.shape[1]
    refs[-1][:3] = mu_ref[...]
    for s in range(1, NZ):
        refs[-1][s * 3 : s * 3 + 3] = refs[s - 1][:, 0, :per].astype(F32).astype(jnp.int32)


def listed(mu_block, pieces):
    blocks, per = mu_block.shape
    tile = pl.BlockSpec((blocks, 16, 256), lambda i: (0, 32, 0))
    return pl.pallas_call(
        listed_kernel,
        grid=(1,),
        in_specs=[pl.BlockSpec((blocks, per), lambda i: (0, 0))] + [tile] * 3,
        out_specs=pl.BlockSpec((NZ * blocks, per), lambda i: (0, 0)),
        out_shape=jax.ShapeDtypeStruct((NZ * blocks, per), jnp.int32),
        compiler_params=pltpu.CompilerParams(vmem_limit_bytes=LIMIT),
    )(mu_block, *pieces)


def chi_kernel(core, a_ref, b_ref, out_ref):
    pair, parts = a_ref.shape[-1], [(m, r) for m in range(3) for r in range(2)]
    a = jnp.concatenate(
        [a_ref[:, m, r * 16 : (r + 1) * 16, :].reshape(-1, pair) for m, r in parts], axis=1
    )
    b = jnp.concatenate([b_ref[:, 0, :, m, r].reshape(-1, pair) for m, r in parts], axis=1)
    got = lax.dot_general(a, b, (((1,), (1,)), ((), ())), preferred_element_type=F32)
    for z in range(NZ):
        out_ref[:, z] = got[:, z * 128 : (z + 1) * 128].reshape(-1, 64, 128)


def chi_half(core, a, b):
    return pl.pallas_call(
        chi_kernel,
        grid_spec=pltpu.PrefetchScalarGridSpec(
            num_scalar_prefetch=1,
            grid=(2,),
            in_specs=[
                pl.BlockSpec((32, 3, 32, 256), lambda i, core: (i, 0, 0, 0)),
                pl.BlockSpec(
                    (4, 1, 2, 3, 2, 64, 256), lambda i, core: (0, core[0], 0, 0, 0, 0, 0)
                ),
            ],
            out_specs=pl.BlockSpec((8, NZ, 64, 128), lambda i, core: (i, 0, 0, 0)),
        ),
        out_shape=jax.ShapeDtypeStruct((NXY, NZ, 64, 128), F32),
        compiler_params=pltpu.CompilerParams(vmem_limit_bytes=LIMIT),
        cost_estimate=pl.CostEstimate(
            flops=1_700_000_000, bytes_accessed=7_000_000, transcendentals=0
        ),
    )(core, a, b)


def shards(tensor, mu_block, green_occ, green_virt):
    z, core = lax.axis_index("z"), lax.axis_index("core")
    orbitals = green_occ.shape[0]
    other = [(0, 1), (1, 0)]
    around = [[(i, (i + s) % NZ) for i in range(NZ)] for s in range(NZ)]

    mu_rows = jnp.pad(mu_block[:, None, :], ((0, 0), (0, 15), (0, 256 - mu_block.shape[1])))
    regrouped, *blocks = spread(z.reshape(1), tensor, mu_rows.astype(BF))
    arrived = [lax.ppermute(blocks[s], "z", around[s]) if s else blocks[0] for s in range(NZ)]
    q_side = lax.all_to_all(regrouped, ("x", "y"), split_axis=0, concat_axis=0, tiled=True)

    occ = lax.dynamic_index_in_dim(
        green_occ.reshape(orbitals, NZ, NC, -1), core, 2, keepdims=False
    ).reshape(orbitals, -1)
    order = jnp.stack(
        [((z - s) % NZ) * NC + c for s in (1, 2, 3, 0) for c in (core, 1 - core)]
    )
    virt = green_virt.reshape(NZ * NC, -1, orbitals)[order].reshape(orbitals, orbitals).T

    early = make_early(
        mu_block,
        lax.ppermute(mu_block, "core", other),
        blocks[0],
        lax.ppermute(blocks[0], "core", other),
        occ,
    )
    early, virt, *tail = lax.optimization_barrier((early, virt, *arrived[2:]))
    arrived = [arrived[1], *tail]
    mu_own = listed(mu_block, arrived)
    pieces = [q for p in arrived for q in (p, lax.ppermute(p, "core", other))]
    paired = make_paired(
        z.reshape(1), mu_own, lax.ppermute(mu_own, "core", other), pieces, occ, virt, early
    )
    p_side = lax.all_to_all(
        paired.reshape(NXY * NZ, 3, 32, 256), ("x", "y", "z"), 0, 0, tiled=True
    )
    q_side = q_side.reshape(4, 2, 2, 3, 2, 64, 256)
    given = chi_half((1 - core).reshape(1), p_side, q_side)
    kept = chi_half(core.reshape(1), p_side, q_side)
    chi = (kept + lax.ppermute(given, "core", other)).astype(BF)
    shares = lax.all_to_all(
        chi.reshape(NXY * NZ, 64, 128), ("x", "y", "z"), 0, 0, tiled=True
    )
    return shares.astype(F32).sum(0)


def solution(mesh):
    mesh = Mesh(mesh.devices.reshape(NX, NY, NZ, NC), ("x", "y", "z", "core"))
    return jax.shard_map(
        shards,
        mesh=mesh,
        in_specs=(P(("z", "core"), ("x", "y"), None, None), P(("z", "core"), None), P(), P()),
        out_specs=P(("x", "y"), ("z", "core")),
        check_vma=False,
    )
```

time: 162 us -> 150 us (0.926)
  Pallas kernels: 28.8 us -> 22.5 us
  waiting for transfers between devices: 31.2 us -> 25.3 us
  blocking collectives: 72.2 us -> 77.8 us
  starting transfers between devices: 17.5 us -> 14.3 us
    all_to_all x1, waiting for transfers between devices: 9.24 us -> 1.81 us  [shards(): lax.all_to_all(regrouped, ('x', 'y'), split_axis=0, concat_axis=0, tiled=...]
    all_to_all x1, blocking collectives: 47.7 us -> 54 us  [shards(): lax.all_to_all(paired.reshape(NXY * NZ, 3, 32, 256), ('x', 'y', 'z'), 0,...]
    pallas_call x2, Pallas kernels: 12.1 us -> 6.93 us  [chi_half(): pl.pallas_call(chi_kernel, grid_spec=pltpu.PrefetchScalarGridSpec(num_sca...]
    squeeze x1 -> x0, local copies, waits for them, and re-layouts: 3.63 us -> none  [shards(): lax.dynamic_index_in_dim(by_z, (z + s) % NZ, 1, keepdims=False)]
    ppermute x10 -> x8, starting transfers between devices: 10.4 us -> 7.09 us  [the longest x3 5.99 us: shards(): lax.ppermute(blocks[s], 'z', around[s])]
    ppermute x10 -> x8, waiting for transfers between devices: 20.6 us -> 22.8 us  [the longest x3 19.8 us: shards(): lax.ppermute(blocks[s], 'z', around[s])]
    unnamed x15 -> x7, local copies, waits for them, and re-layouts: 1.6 us -> 3.46 us
    pallas_call x2 -> x4, Pallas kernels: 16.7 us -> 15.6 us  [the longest x1 8.56 us: make_paired(): pl.pallas_call(pair_kernel, in_specs=[smem] * 3 + [pl.BlockSpec(memory_sp...]
  transfers between devices with their start and end apart: 13 -> 11, of which waited for: 8 -> 7; matrix products, arithmetic and copies ran while one was open for 5% -> 4% of each run, Pallas kernels for 14% -> 11%
where the time goes in v3:
time: 150 us; the launch traced here: 149 us
  blocking collectives  77.8 us (52%)
  waiting for transfers between devices  25.3 us (17%)
  Pallas kernels  22.5 us (15%)
  starting transfers between devices  14.3 us (10%)
  local copies, waits for them, and re-layouts  7.13 us (5%)
  other arithmetic  2.06 us (1%)
    all_to_all x1, blocking collectives, shards(): lax.all_to_all(paired.reshape(NXY * NZ, 3, 32, 256), ('x', 'y', 'z'), 0,...  54 us
    all_to_all x1, blocking collectives, shards(): lax.all_to_all(chi.reshape(NXY * NZ, 64, 128), ('x', 'y', 'z'), 0, 0, til...  23.8 us
    ppermute x3, waiting for transfers between devices, shards(): lax.ppermute(blocks[s], 'z', around[s])  19.8 us
    pallas_call x1, Pallas kernels, make_paired(): pl.pallas_call(pair_kernel, in_specs=[smem] * 3 + [pl.BlockSpec(memory_sp...  8.56 us
    all_to_all x1, starting transfers between devices, shards(): lax.all_to_all(regrouped, ('x', 'y'), split_axis=0, concat_axis=0, tiled=...  7.08 us
    pallas_call x2, Pallas kernels, chi_half(): pl.pallas_call(chi_kernel, grid_spec=pltpu.PrefetchScalarGridSpec(num_sca...  6.93 us
    ppermute x3, starting transfers between devices, shards(): lax.ppermute(blocks[s], 'z', around[s])  5.99 us
    unnamed x7, local copies, waits for them, and re-layouts  3.46 us
  transfers between devices with their start and end apart: 11, of which 7 were waited for; matrix products, arithmetic and copies ran while one was open for 4% of the time, Pallas kernels for 11%

profile of v3, /device:TPU:0, one launch (start us, length us, event | category | flops | bytes accessed | tf_op | source)
XLA Modules:
  0.0 149.2 jit_solution(17138584629839610624)
XLA Ops:
  0.0 0.0 copy-start
  0.0 0.0 copy-start.2
  0.0 0.8 convert_bitcast_fusion
  0.8 0.0 copy-start.1
  0.8 1.9 %copy-done.1 = bf16[3,64,32,256]{3,2,1,0:T(8,128)(2,1)S(1)} copy-done((bf16[3,64,32,256]{3,2,1,0:T(8,128)(2,1)S(1)}, bf16[3,64,32,256]{3,2,1,0:T(8,128)(2,1)}, u32[]{:S(2)}) %copy-start.1) | copy-done | bytes 3145752
  2.7 3.4 %shard_map.46 = (bf16[16,3,2,64,256]{4,3,2,1,0:T(8,128)(2,1)}, bf16[3,528,256]{2,1,0:T(8,128)(2,1)}, bf16[3,528,256]{2,1,0:T(8,128)(2,1)}, bf16[3,528,256]{2,1,0:T(8,128)(2,1)}, bf16[3,528,256]{2,1,0:T(8,128)(2,1)}) custom-call(s32[1]{0:T(128)} %bitcast.1.z_ref, bf16[3,64,32,256]{3,2,1,0:T(8,128)(2,1)S(1)} %copy-done.1, bf16[3,16,256]{2,1,0:T(8,128)(2,1)S(1)} %pad.5.mu_ref), custom_call_target="tpu_custom_call" | custom-call | flops 1000 | bytes 1000 | tf_op jit(solution)/shard_map/pallas_call | solution.py:31
  6.1 0.0 collective-permute-start.2
  6.1 4.0 %collective-permute-start.3 = (bf16[3,528,256]{2,1,0:T(8,128)(2,1)}, bf16[3,528,256]{2,1,0:T(8,128)(2,1)}, u32[]{:S(2)}, u32[]{:S(2)}) collective-permute-start(bf16[3,528,256]{2,1,0:T(8,128)(2,1)} %get-tuple-element.16), channel_id=1, source_target_pairs={{0,4},{2,6},{4,0},{6,2},{1,5},{3,7},{5,1},{7,3},{8,12},{10,14},{12... | collective-permute-start | bytes 2433032 | tf_op jit(solution)/shard_map/ppermute | solution.py:206
  10.0 0.7 collective-permute-start.4
  10.8 1.3 collective-permute-start
  12.1 0.0 copy-done.2
  12.1 0.0 collective-permute-start.1
  12.1 7.1 %all-to-all-start.1 = ((bf16[16,3,2,64,256]{4,3,2,1,0:T(8,128)(2,1)}), bf16[16,3,2,64,256]{4,3,2,1,0:T(8,128)(2,1)}, u32[]{:S(2)}, u32[]{:S(2)}) async-start(bf16[16,3,2,64,256]{4,3,2,1,0:T(8,128)(2,1)} %get-tuple-element.22), calls=%async_computation.1 | async-start | bytes 6291456 | tf_op jit(solution)/shard_map/all_to_all | solution.py:207
  19.2 0.1 stack.35
  19.4 0.0 copy-done
  19.4 0.6 gather_fusion
  20.0 0.6 copy.10
  20.6 1.6 %copy.8 = bf16[768,768]{0,1:T(8,128)(2,1)S(1)} copy(bf16[768,768]{1,0:T(8,128)(2,1)} %param.6) | data formatting | bytes 2359296 | tf_op args[2]
  22.2 0.9 constant_dynamic-slice_fusion
  23.1 1.4 copy.9.occ_ref.refs_6_
  24.5 0.0 collective-permute-done.1.mu_other
  24.5 0.0 collective-permute-done.2.other
  24.5 2.9 %shard_map.47.refs_8_ = bf16[16,384,256]{2,1,0:T(8,128)(2,1)S(1)} custom-call(s32[3,8]{1,0:T(4,128)S(1)} %copy-done.2, s32[3,8]{1,0:T(4,128)S(1)} %collective-permute-done.1.mu_other, bf16[3,528,256]{2,1,0:T(8,128)(2,1)} %get-tuple-element.15.own, bf16[3,528,256]{2,1,0:T(8,128)(2,1)} %collective-permute-done.2.other, bf16[768,384]{1,0:T(8,128)(2,1)S(1)} %copy.9.occ_ref.refs_6_), custom_call_target="tpu_custom_call" | custom-call | flops 1000 | bytes 1000 | tf_op jit(solution)/shard_map/pallas_call | solution.py:78
  27.4 1.9 %collective-permute-done.3.refs_1_.refs_2_ = bf16[3,528,256]{2,1,0:T(8,128)(2,1)} collective-permute-done((bf16[3,528,256]{2,1,0:T(8,128)(2,1)}, bf16[3,528,256]{2,1,0:T(8,128)(2,1)}, u32[]{:S(2)}, u32[]{:S(2)}) %collective-permute-start.3) | collective-permute-done | bytes 811040 | tf_op jit(solution)/shard_map/ppermute | solution.py:206
  29.3 17.9 %collective-permute-done.4.refs_2_.refs_4_ = bf16[3,528,256]{2,1,0:T(8,128)(2,1)} collective-permute-done((bf16[3,528,256]{2,1,0:T(8,128)(2,1)}, bf16[3,528,256]{2,1,0:T(8,128)(2,1)}, u32[]{:S(2)}, u32[]{:S(2)}) %collective-permute-start.4) | collective-permute-done | bytes 811040 | tf_op jit(solution)/shard_map/ppermute | solution.py:206
  47.3 0.0 collective-permute-start.7
  47.3 0.0 collective-permute-done.refs_0_
  47.3 0.5 collective-permute-start.6
  47.8 0.0 collective-permute-start.8
  47.8 0.8 shard_map.48.mu_own
  48.6 0.6 collective-permute-start.5
  49.1 1.6 %collective-permute-done.5.mu_other = s32[12,8]{1,0:T(8,128)S(1)} collective-permute-done((s32[12,8]{1,0:T(8,128)S(1)}, s32[12,8]{1,0:T(8,128)S(1)}, u32[]{:S(2)}, u32[]{:S(2)}) %collective-permute-start.5) | collective-permute-done | bytes 416 | tf_op jit(solution)/shard_map/ppermute | solution.py:229
  50.8 0.2 collective-permute-done.6.refs_1_
  50.9 0.0 collective-permute-done.7.refs_3_
  50.9 1.2 collective-permute-done.8.refs_5_
  52.1 8.6 %shard_map.49 = bf16[16,4,3,32,256]{4,3,2,1,0:T(8,128)(2,1)} custom-call(s32[1]{0:T(128)} %bitcast.1.z_ref, s32[12,8]{1,0:T(8,128)S(1)} %shard_map.48.mu_own, s32[12,8]{1,0:T(8,128)S(1)} %collective-permute-done.5.mu_other, bf16[3,528,256]{2,1,0:T(8,128)(2,1)} %collective-permute-done.refs_0_, bf16[3,528,256]{2,1,0:T(8,128)(2,1)S(1)} %collective-permute-done.6.refs_1_, ...), custom_call_target="tpu_custom_call" | custom-call | flops 22000001024 | bytes 12000000 | tf_op jit(solution)/shard_map/pallas_call | solution.py:127
  60.7 1.8 %all-to-all-done.1 = bf16[16,3,2,64,256]{4,3,2,1,0:T(8,128)(2,1)} async-done(((bf16[16,3,2,64,256]{4,3,2,1,0:T(8,128)(2,1)}), bf16[16,3,2,64,256]{4,3,2,1,0:T(8,128)(2,1)}, u32[]{:S(2)}, u32[]{:S(2)}) %all-to-all-start.1) | async-done | bytes 3145760 | tf_op jit(solution)/shard_map/all_to_all | solution.py:207
  62.5 54.0 %all_to_all.15.a_ref = bf16[64,3,32,256]{3,2,1,0:T(8,128)(2,1)S(1)} all-to-all(bf16[64,3,32,256]{3,2,1,0:T(8,128)(2,1)} %bitcast.27), channel_id=1, replica_groups=mesh['x'=4,'y'=4,'z'=4,'core'=2] {'x','y','z'}, dimensions={0} | all-to-all | bytes 6291456 | tf_op jit(solution)/shard_map/all_to_all | solution.py:231
  116.5 3.5 %shard_map.51 = f32[16,4,64,128]{3,2,1,0:T(8,128)S(1)} custom-call(s32[1]{0:T(128)} %bitcast.19.core, bf16[64,3,32,256]{3,2,1,0:T(8,128)(2,1)S(1)} %all_to_all.15.a_ref, bf16[4,2,2,3,2,64,256]{6,5,4,3,2,1,0:T(8,128)(2,1)} %bitcast.18.b_ref), custom_call_target="tpu_custom_call" | custom-call | flops 1700000000 | bytes 7000000 | tf_op jit(solution)/shard_map/pallas_call | solution.py:177
  119.9 0.1 collective-permute-start.9
  120.0 3.5 %shard_map.50 = f32[16,4,64,128]{3,2,1,0:T(8,128)S(1)} custom-call(s32[1]{0:T(128)} %bitcast.core, bf16[64,3,32,256]{3,2,1,0:T(8,128)(2,1)S(1)} %all_to_all.15.a_ref, bf16[4,2,2,3,2,64,256]{6,5,4,3,2,1,0:T(8,128)(2,1)} %bitcast.18.b_ref), custom_call_target="tpu_custom_call" | custom-call | flops 1700000000 | bytes 7000000 | tf_op jit(solution)/shard_map/pallas_call | solution.py:177
  123.5 0.7 collective-permute-done.9
  124.2 0.5 add_convert_fusion
  124.6 23.8 %all_to_all.16 = bf16[64,64,128]{2,1,0:T(8,128)(2,1)S(1)} all-to-all(bf16[64,64,128]{2,1,0:T(8,128)(2,1)S(1)} %bitcast.26), channel_id=1, replica_groups=mesh['x'=4,'y'=4,'z'=4,'core'=2] {'x','y','z'}, dimensions={0} | all-to-all | bytes 2097152 | tf_op jit(solution)/shard_map/all_to_all | solution.py:238
  148.4 0.8 convert_reduce_fusion
  (4 shorter events, 0.0 us)
Async XLA Ops:
  0.0 19.4 %copy-start = (bf16[768,768]{1,0:T(8,128)(2,1)S(1)}, bf16[768,768]{1,0:T(8,128)(2,1)}, u32[]{:S(2)}) copy-start(bf16[768,768]{1,0:T(8,128)(2,1)} %param.7) | copy-start | bytes 3538948
  0.0 12.1 %copy-start.2 = (s32[3,8]{1,0:T(4,128)S(1)}, s32[3,8]{1,0:T(4,128)}, u32[]{:S(2)}) copy-start(s32[3,8]{1,0:T(4,128)} %mu_ref.1) | copy-start | bytes 292
  0.8 1.9 %copy-start.1 = (bf16[3,64,32,256]{3,2,1,0:T(8,128)(2,1)S(1)}, bf16[3,64,32,256]{3,2,1,0:T(8,128)(2,1)}, u32[]{:S(2)}) copy-start(bf16[3,64,32,256]{3,2,1,0:T(8,128)(2,1)} %tensor_ref.1) | copy-start | bytes 9437188
  6.1 18.4 %collective-permute-start.2 = (bf16[3,528,256]{2,1,0:T(8,128)(2,1)}, bf16[3,528,256]{2,1,0:T(8,128)(2,1)}, u32[]{:S(2)}, u32[]{:S(2)}) collective-permute-start(bf16[3,528,256]{2,1,0:T(8,128)(2,1)} %get-tuple-element.15.own), channel_id=1, source_target_pairs={{0,1},{1,0},{2,3},{3,2},{4,5},{5,4},{6,7},{7,6},{8,9},{9,8},{10,11... | collective-permute-start | bytes 2433032 | tf_op jit(solution)/shard_map/ppermute | solution.py:221
  6.1 23.2 %collective-permute-start.3 = (bf16[3,528,256]{2,1,0:T(8,128)(2,1)}, bf16[3,528,256]{2,1,0:T(8,128)(2,1)}, u32[]{:S(2)}, u32[]{:S(2)}) collective-permute-start(bf16[3,528,256]{2,1,0:T(8,128)(2,1)} %get-tuple-element.16), channel_id=1, source_target_pairs={{0,4},{2,6},{4,0},{6,2},{1,5},{3,7},{5,1},{7,3},{8,12},{10,14},{12... | collective-permute-start | bytes 2433032 | tf_op jit(solution)/shard_map/ppermute | solution.py:206
  10.0 37.2 %collective-permute-start.4 = (bf16[3,528,256]{2,1,0:T(8,128)(2,1)}, bf16[3,528,256]{2,1,0:T(8,128)(2,1)}, u32[]{:S(2)}, u32[]{:S(2)}) collective-permute-start(bf16[3,528,256]{2,1,0:T(8,128)(2,1)} %get-tuple-element.17), channel_id=1, source_target_pairs={{0,6},{2,0},{4,2},{6,4},{1,7},{3,1},{5,3},{7,5},{8,14},{10,8},{12,... | collective-permute-start | bytes 2433032 | tf_op jit(solution)/shard_map/ppermute | solution.py:206
  10.8 36.5 %collective-permute-start = (bf16[3,528,256]{2,1,0:T(8,128)(2,1)}, bf16[3,528,256]{2,1,0:T(8,128)(2,1)}, u32[]{:S(2)}, u32[]{:S(2)}) collective-permute-start(bf16[3,528,256]{2,1,0:T(8,128)(2,1)} %get-tuple-element.14), channel_id=1, source_target_pairs={{0,2},{2,4},{4,6},{6,0},{1,3},{3,5},{5,7},{7,1},{8,10},{10,12},{12... | collective-permute-start | bytes 2433032 | tf_op jit(solution)/shard_map/ppermute | solution.py:206
  12.1 12.4 %collective-permute-start.1 = (s32[3,8]{1,0:T(4,128)S(1)}, s32[3,8]{1,0:T(4,128)S(1)}, u32[]{:S(2)}, u32[]{:S(2)}) collective-permute-start(s32[3,8]{1,0:T(4,128)S(1)} %copy-done.2), channel_id=1, source_target_pairs={{0,1},{1,0},{2,3},{3,2},{4,5},{5,4},{6,7},{7,6},{8,9},{9,8},{10,11... | collective-permute-start | bytes 296 | tf_op jit(solution)/shard_map/ppermute | solution.py:219
  12.1 50.4 %all-to-all-start.1 = ((bf16[16,3,2,64,256]{4,3,2,1,0:T(8,128)(2,1)}), bf16[16,3,2,64,256]{4,3,2,1,0:T(8,128)(2,1)}, u32[]{:S(2)}, u32[]{:S(2)}) async-start(bf16[16,3,2,64,256]{4,3,2,1,0:T(8,128)(2,1)} %get-tuple-element.22), calls=%async_computation.1 | async-start | bytes 6291456 | tf_op jit(solution)/shard_map/all_to_all | solution.py:207
  47.3 3.7 %collective-permute-start.7 = (bf16[3,528,256]{2,1,0:T(8,128)(2,1)}, bf16[3,528,256]{2,1,0:T(8,128)(2,1)S(1)}, u32[]{:S(2)}, u32[]{:S(2)}) collective-permute-start(bf16[3,528,256]{2,1,0:T(8,128)(2,1)} %collective-permute-done.3.refs_1_.refs_2_), channel_id=1, source_target_pairs={{0,1},{1,0},{2,3},{3,2},{4,5},{5,4},{6,7},{7,6},{8,9},{9,8},{10,11... | collective-permute-start | bytes 2433032 | tf_op jit(solution)/shard_map/ppermute | solution.py:227
  47.3 3.7 %collective-permute-start.6 = (bf16[3,528,256]{2,1,0:T(8,128)(2,1)}, bf16[3,528,256]{2,1,0:T(8,128)(2,1)S(1)}, u32[]{:S(2)}, u32[]{:S(2)}) collective-permute-start(bf16[3,528,256]{2,1,0:T(8,128)(2,1)} %collective-permute-done.refs_0_), channel_id=1, source_target_pairs={{0,1},{1,0},{2,3},{3,2},{4,5},{5,4},{6,7},{7,6},{8,9},{9,8},{10,11... | collective-permute-start | bytes 2433032 | tf_op jit(solution)/shard_map/ppermute | solution.py:227
  47.8 4.3 %collective-permute-start.8 = (bf16[3,528,256]{2,1,0:T(8,128)(2,1)}, bf16[3,528,256]{2,1,0:T(8,128)(2,1)S(1)}, u32[]{:S(2)}, u32[]{:S(2)}) collective-permute-start(bf16[3,528,256]{2,1,0:T(8,128)(2,1)} %collective-permute-done.4.refs_2_.refs_4_), channel_id=1, source_target_pairs={{0,1},{1,0},{2,3},{3,2},{4,5},{5,4},{6,7},{7,6},{8,9},{9,8},{10,11... | collective-permute-start | bytes 2433032 | tf_op jit(solution)/shard_map/ppermute | solution.py:227
  48.6 2.2 %collective-permute-start.5 = (s32[12,8]{1,0:T(8,128)S(1)}, s32[12,8]{1,0:T(8,128)S(1)}, u32[]{:S(2)}, u32[]{:S(2)}) collective-permute-start(s32[12,8]{1,0:T(8,128)S(1)} %shard_map.48.mu_own), channel_id=1, source_target_pairs={{0,1},{1,0},{2,3},{3,2},{4,5},{5,4},{6,7},{7,6},{8,9},{9,8},{10,11... | collective-permute-start | bytes 1160 | tf_op jit(solution)/shard_map/ppermute | solution.py:229
  119.9 4.2 %collective-permute-start.9 = (f32[16,4,64,128]{3,2,1,0:T(8,128)S(1)}, f32[16,4,64,128]{3,2,1,0:T(8,128)S(1)}, u32[]{:S(2)}, u32[]{:S(2)}) collective-permute-start(f32[16,4,64,128]{3,2,1,0:T(8,128)S(1)} %shard_map.51), channel_id=1, source_target_pairs={{0,1},{1,0},{2,3},{3,2},{4,5},{5,4},{6,7},{7,6},{8,9},{9,8},{10,11... | collective-permute-start | bytes 6291464 | tf_op jit(solution)/shard_map/ppermute | solution.py:237

commit v4 on v3

--- a/solution.py
+++ b/solution.py
@@ -10,41 +10,73 @@
 NXY = NX * NY
 BF, F32 = jnp.bfloat16, jnp.float32
 LIMIT = 30 * 1024 * 1024
-PAIR_FLOPS = 22_000_000_000
-
-
-def spread_kernel(z_ref, tensor_ref, mu_ref, *outs):
-    regrouped, blocks = outs[0], outs[1:]
-    rows, pair = 16 * tensor_ref.shape[2], tensor_ref.shape[3]
-    regrouped[:, 0] = jnp.swapaxes(tensor_ref[0], 0, 1).reshape(
-        NXY, 2, tensor_ref.shape[1], pair
-    )
+PAIR_FLOPS = 15_000_000_000
+
+
+def spread_kernel(z_ref, mu_ref, tensor_ref, *refs):
+    regrouped, blocks = refs[0], refs[1 : 1 + NZ]
+    held, turned, listed, in_sems, out_sems, cut_sems, mu_sems = refs[1 + NZ :]
+    count, aux, width, pair = tensor_ref.shape
+    loads = [
+        pltpu.make_async_copy(tensor_ref.at[m], held.at[m], in_sems.at[m])
+        for m in range(count)
+    ]
+    for load in loads:
+        load.start()
+    lane = lax.broadcasted_iota(jnp.int32, (width, pair), 1)
+    for m in range(count):
+        tile = jnp.zeros((width, pair), jnp.int32)
+        for k in range(mu_ref.shape[1]):
+            tile = jnp.where(lane == k, mu_ref[m, k], tile)
+        listed[m, 0] = tile.astype(F32).astype(BF)
+    copies = []
     for s in range(NZ):
-        z = lax.rem(z_ref[0] + s, NZ)
-        blocks[s][0, :rows] = tensor_ref[0, pl.ds(z * 16, 16)].reshape(rows, pair)
-        blocks[s][0, rows:] = mu_ref[0]
-
-
-def spread(z, tensor, mu_rows):
+        to = blocks[s].at[:, pl.ds(16, 1)]
+        copies.append(pltpu.make_async_copy(listed, to, mu_sems.at[s]))
+        copies[-1].start()
+    for m in range(count):
+        loads[m].wait()
+        for s in range(NZ):
+            z = lax.rem(z_ref[0] + s, NZ)
+            copies.append(
+                pltpu.make_async_copy(
+                    held.at[m, pl.ds(z * 16, 16)],
+                    blocks[s].at[m, pl.ds(0, 16)],
+                    cut_sems.at[m * NZ + s],
+                )
+            )
+            copies[-1].start()
+        turned[m] = jnp.swapaxes(held[m], 0, 1).reshape(NXY, 2, aux, pair)
+        copies.append(
+            pltpu.make_async_copy(turned.at[m], regrouped.at[:, m], out_sems.at[m])
+        )
+        copies[-1].start()
+    for copy in copies:
+        copy.wait()
+
+
+def spread(z, mu, tensor):
     blocks, aux, width, pair = tensor.shape
-    piece = (16 * width + 16, pair)
+    smem = pl.BlockSpec(memory_space=pltpu.SMEM)
+    anywhere = pl.BlockSpec(memory_space=pl.ANY)
     return pl.pallas_call(
         spread_kernel,
-        grid_spec=pltpu.PrefetchScalarGridSpec(
-            num_scalar_prefetch=1,
-            grid=(blocks,),
-            in_specs=[
-                pl.BlockSpec((1, aux, width, pair), lambda m, z: (m, 0, 0, 0)),
-                pl.BlockSpec((1, 16, pair), lambda m, z: (m, 0, 0)),
-            ],
-            out_specs=[pl.BlockSpec((NXY, 1, 2, aux, pair), lambda m, z: (0, m, 0, 0, 0))]
-            + [pl.BlockSpec((1, *piece), lambda m, z: (m, 0, 0))] * NZ,
-        ),
+        in_specs=[smem, smem, anywhere],
+        out_specs=[anywhere] * (1 + NZ),
         out_shape=[pltpu.HBM((NXY, blocks, 2, aux, pair), BF)]
-        + [jax.ShapeDtypeStruct((blocks, *piece), BF)] * NZ,
-        compiler_params=pltpu.CompilerParams(vmem_limit_bytes=LIMIT),
+        + [jax.ShapeDtypeStruct((blocks, 17, width, pair), BF)] * NZ,
+        scratch_shapes=[
+            pltpu.VMEM(tensor.shape, BF),
+            pltpu.VMEM((blocks, NXY, 2, aux, pair), BF),
+            pltpu.VMEM((blocks, 1, width, pair), BF),
+            pltpu.SemaphoreType.DMA((blocks,)),
+            pltpu.SemaphoreType.DMA((blocks,)),
+            pltpu.SemaphoreType.DMA((blocks * NZ,)),
+            pltpu.SemaphoreType.DMA((NZ,)),
+        ],
+        compiler_params=pltpu.CompilerParams(vmem_limit_bytes=60 * 1024 * 1024),
         cost_estimate=pl.CostEstimate(flops=1000, bytes_accessed=1000, transcendentals=0),
-    )(z, tensor, mu_rows)
+    )(z, mu, tensor)
 
 
 def gathered(ref, mu, t, per, width):
@@ -57,7 +89,9 @@
 def occupied(piece, mu, m, at, occ_ref, stage):
     per, half, width = mu.shape[1], occ_ref.shape[1], 32
     occ = gathered(occ_ref, mu, at[0], per, width)
-    got = jnp.dot(piece[m, : 16 * width], occ, preferred_element_type=F32).astype(BF)
+    got = jnp.dot(
+        piece[m, :16].reshape(16 * width, -1), occ, preferred_element_type=F32
+    ).astype(BF)
     stage[:, at[1] : at[1] + width, :] = got.reshape(16, width, half)
 
 
@@ -146,12 +180,12 @@
     per = mu_ref.shape[1]
     refs[-1][:3] = mu_ref[...]
     for s in range(1, NZ):
-        refs[-1][s * 3 : s * 3 + 3] = refs[s - 1][:, 0, :per].astype(F32).astype(jnp.int32)
+        refs[-1][s * 3 : s * 3 + 3] = refs[s - 1][:, 0, 0, :per].astype(F32).astype(jnp.int32)
 
 
 def listed(mu_block, pieces):
     blocks, per = mu_block.shape
-    tile = pl.BlockSpec((blocks, 16, 256), lambda i: (0, 32, 0))
+    tile = pl.BlockSpec((blocks, 1, 32, 256), lambda i: (0, 16, 0, 0))
     return pl.pallas_call(
         listed_kernel,
         grid=(1,),
@@ -201,8 +235,7 @@
     other = [(0, 1), (1, 0)]
     around = [[(i, (i + s) % NZ) for i in range(NZ)] for s in range(NZ)]
 
-    mu_rows = jnp.pad(mu_block[:, None, :], ((0, 0), (0, 15), (0, 256 - mu_block.shape[1])))
-    regrouped, *blocks = spread(z.reshape(1), tensor, mu_rows.astype(BF))
+    regrouped, *blocks = spread(z.reshape(1), mu_block, tensor)
     arrived = [lax.ppermute(blocks[s], "z", around[s]) if s else blocks[0] for s in range(NZ)]
     q_side = lax.all_to_all(regrouped, ("x", "y"), split_axis=0, concat_axis=0, tiled=True)
 
@@ -221,8 +254,8 @@
         lax.ppermute(blocks[0], "core", other),
         occ,
     )
-    early, virt, *tail = lax.optimization_barrier((early, virt, *arrived[2:]))
-    arrived = [arrived[1], *tail]
+    early, virt, last = lax.optimization_barrier((early, virt, arrived[2]))
+    arrived = [arrived[1], last, arrived[3]]
     mu_own = listed(mu_block, arrived)
     pieces = [q for p in arrived for q in (p, lax.ppermute(p, "core", other))]
     paired = make_paired(

time: 150 us -> 145 us (0.967)
  blocking collectives: 77.8 us -> 72.6 us
    all_to_all x1, blocking collectives: 54 us -> 49 us  [shards(): lax.all_to_all(paired.reshape(NXY * NZ, 3, 32, 256), ('x', 'y', 'z'), 0,...]
    pallas_call x1, Pallas kernels: 3.37 us -> 4.92 us  [spread(): pl.pallas_call(spread_kernel, in_specs=[smem, smem, anywhere], out_specs=...]
where the time goes in v4:
time: 145 us; the launch traced here: 144 us
  blocking collectives  72.6 us (50%)
  waiting for transfers between devices  24.1 us (17%)
  Pallas kernels  23.9 us (16%)
  starting transfers between devices  15.6 us (11%)
  local copies, waits for them, and re-layouts  6.38 us (4%)
    all_to_all x1, blocking collectives, shards(): lax.all_to_all(paired.reshape(NXY * NZ, 3, 32, 256), ('x', 'y', 'z'), 0,...  49 us
    all_to_all x1, blocking collectives, shards(): lax.all_to_all(chi.reshape(NXY * NZ, 64, 128), ('x', 'y', 'z'), 0, 0, til...  23.5 us
    ppermute x3, waiting for transfers between devices, shards(): lax.ppermute(blocks[s], 'z', around[s])  18.4 us
    pallas_call x1, Pallas kernels, make_paired(): pl.pallas_call(pair_kernel, in_specs=[smem] * 3 + [pl.BlockSpec(memory_sp...  8.57 us
    ppermute x3, starting transfers between devices, shards(): lax.ppermute(blocks[s], 'z', around[s])  7.28 us
    all_to_all x1, starting transfers between devices, shards(): lax.all_to_all(regrouped, ('x', 'y'), split_axis=0, concat_axis=0, tiled=...  7.21 us
    pallas_call x2, Pallas kernels, chi_half(): pl.pallas_call(chi_kernel, grid_spec=pltpu.PrefetchScalarGridSpec(num_sca...  6.93 us
    pallas_call x1, Pallas kernels, spread(): pl.pallas_call(spread_kernel, in_specs=[smem, smem, anywhere], out_specs=...  4.92 us
  transfers between devices with their start and end apart: 11, of which 7 were waited for; matrix products, arithmetic and copies ran while one was open for 4% of the time, Pallas kernels for 11%

profile of v4, /device:TPU:0, one launch (start us, length us, event | category | flops | bytes accessed | tf_op | source)
XLA Modules:
  0.0 144.0 jit_solution(2015162622132788145)
XLA Ops:
  0.0 0.0 copy-start
  0.0 4.9 %shard_map.46 = (bf16[16,3,2,64,256]{4,3,2,1,0:T(8,128)(2,1)}, bf16[3,17,32,256]{3,2,1,0:T(8,128)(2,1)}, bf16[3,17,32,256]{3,2,1,0:T(8,128)(2,1)}, bf16[3,17,32,...) custom-call(s32[1]{0:T(128)} %bitcast.1.z_ref, s32[3,8]{1,0:T(4,128)} %mu_ref.3, bf16[3,64,32,256]{3,2,1,0:T(8,128)(2,1)} %tensor_ref.1), custom_call_target="tpu_custom_call" | custom-call | flops 1000 | bytes 1000 | tf_op jit(solution)/shard_map/pallas_call | solution.py:62
  4.9 0.1 collective-permute-start.2
  5.0 4.0 %collective-permute-start.3 = (bf16[3,17,32,256]{3,2,1,0:T(8,128)(2,1)}, bf16[3,17,32,256]{3,2,1,0:T(8,128)(2,1)}, u32[]{:S(2)}, u32[]{:S(2)}) collective-permute-start(bf16[3,17,32,256]{3,2,1,0:T(8,128)(2,1)} %get-tuple-element.15), channel_id=1, source_target_pairs={{0,4},{2,6},{4,0},{6,2},{1,5},{3,7},{5,1},{7,3},{8,12},{10,14},{12... | collective-permute-start | bytes 2506760 | tf_op jit(solution)/shard_map/ppermute | solution.py:239
  9.1 1.0 collective-permute-start
  10.1 2.2 %collective-permute-start.4 = (bf16[3,17,32,256]{3,2,1,0:T(8,128)(2,1)}, bf16[3,17,32,256]{3,2,1,0:T(8,128)(2,1)}, u32[]{:S(2)}, u32[]{:S(2)}) collective-permute-start(bf16[3,17,32,256]{3,2,1,0:T(8,128)(2,1)} %get-tuple-element.17), channel_id=1, source_target_pairs={{0,6},{2,0},{4,2},{6,4},{1,7},{3,1},{5,3},{7,5},{8,14},{10,8},{12,... | collective-permute-start | bytes 2506760 | tf_op jit(solution)/shard_map/ppermute | solution.py:239
  12.3 0.0 copy-start.2
  12.3 7.2 %all-to-all-start.1 = ((bf16[16,3,2,64,256]{4,3,2,1,0:T(8,128)(2,1)}), bf16[16,3,2,64,256]{4,3,2,1,0:T(8,128)(2,1)}, u32[]{:S(2)}, u32[]{:S(2)}) async-start(bf16[16,3,2,64,256]{4,3,2,1,0:T(8,128)(2,1)} %get-tuple-element.20), calls=%async_computation.1 | async-start | bytes 6291456 | tf_op jit(solution)/shard_map/all_to_all | solution.py:240
  19.5 0.0 copy-done.2
  19.5 0.1 collective-permute-start.1
  19.7 0.1 stack.35
  19.8 0.0 copy-done
  19.8 0.6 gather_fusion
  20.5 0.6 copy.8
  21.1 1.6 %copy.6 = bf16[768,768]{0,1:T(8,128)(2,1)S(1)} copy(bf16[768,768]{1,0:T(8,128)(2,1)} %param.6) | data formatting | bytes 2359296 | tf_op args[2]
  22.7 0.9 constant_dynamic-slice_fusion
  23.6 1.4 copy.7.occ_ref.refs_6_
  25.0 0.0 collective-permute-done.1.mu_other
  25.0 0.0 collective-permute-done.2.other
  25.0 0.0 copy-start.1
  25.0 1.1 copy-done.1
  26.2 2.6 %shard_map.47.refs_8_ = bf16[16,384,256]{2,1,0:T(8,128)(2,1)S(1)} custom-call(s32[3,8]{1,0:T(4,128)S(1)} %copy-done.2, s32[3,8]{1,0:T(4,128)S(1)} %collective-permute-done.1.mu_other, bf16[3,17,32,256]{3,2,1,0:T(8,128)(2,1)S(1)} %copy-done.1, bf16[3,17,32,256]{3,2,1,0:T(8,128)(2,1)} %collective-permute-done.2.other, bf16[768,384]{1,0:T(8,128)(2,1)S(1)} %copy.7.occ_ref.refs_6_), custom_call_target="tpu_custom_call" | custom-call | flops 1000 | bytes 1000 | tf_op jit(solution)/shard_map/pallas_call | solution.py:112
  28.8 0.1 collective-permute-done.3.refs_1_.refs_2_
  28.9 17.6 %collective-permute-done.refs_0_ = bf16[3,17,32,256]{3,2,1,0:T(8,128)(2,1)} collective-permute-done((bf16[3,17,32,256]{3,2,1,0:T(8,128)(2,1)}, bf16[3,17,32,256]{3,2,1,0:T(8,128)(2,1)}, u32[]{:S(2)}, u32[]{:S(2)}) %collective-permute-start) | collective-permute-done | bytes 835616 | tf_op jit(solution)/shard_map/ppermute | solution.py:239
  46.5 0.0 collective-permute-start.6
  46.5 0.8 collective-permute-done.4.refs_2_.refs_4_
  47.3 0.0 collective-permute-start.8
  47.3 0.5 collective-permute-start.7
  47.8 0.9 shard_map.48.mu_own
  48.6 0.3 collective-permute-start.5
  48.9 2.3 %collective-permute-done.5.mu_other = s32[12,8]{1,0:T(8,128)S(1)} collective-permute-done((s32[12,8]{1,0:T(8,128)S(1)}, s32[12,8]{1,0:T(8,128)S(1)}, u32[]{:S(2)}, u32[]{:S(2)}) %collective-permute-start.5) | collective-permute-done | bytes 416 | tf_op jit(solution)/shard_map/ppermute | solution.py:262
  51.2 0.0 collective-permute-done.6.refs_1_
  51.2 0.0 collective-permute-done.8.refs_5_
  51.2 0.2 collective-permute-done.7.refs_3_
  51.4 8.6 %shard_map.49 = bf16[16,4,3,32,256]{4,3,2,1,0:T(8,128)(2,1)} custom-call(s32[1]{0:T(128)} %bitcast.1.z_ref, s32[12,8]{1,0:T(8,128)S(1)} %shard_map.48.mu_own, s32[12,8]{1,0:T(8,128)S(1)} %collective-permute-done.5.mu_other, bf16[3,17,32,256]{3,2,1,0:T(8,128)(2,1)} %collective-permute-done.refs_0_, ...), custom_call_target="tpu_custom_call" | custom-call | flops 15000000512 | bytes 12000000 | tf_op jit(solution)/shard_map/pallas_call | solution.py:161
  60.0 2.5 %all-to-all-done.1 = bf16[16,3,2,64,256]{4,3,2,1,0:T(8,128)(2,1)} async-done(((bf16[16,3,2,64,256]{4,3,2,1,0:T(8,128)(2,1)}), bf16[16,3,2,64,256]{4,3,2,1,0:T(8,128)(2,1)}, u32[]{:S(2)}, u32[]{:S(2)}) %all-to-all-start.1) | async-done | bytes 3145760 | tf_op jit(solution)/shard_map/all_to_all | solution.py:240
  62.5 49.0 %all_to_all.15.a_ref = bf16[64,3,32,256]{3,2,1,0:T(8,128)(2,1)S(1)} all-to-all(bf16[64,3,32,256]{3,2,1,0:T(8,128)(2,1)} %bitcast.25), channel_id=1, replica_groups=mesh['x'=4,'y'=4,'z'=4,'core'=2] {'x','y','z'}, dimensions={0} | all-to-all | bytes 6291456 | tf_op jit(solution)/shard_map/all_to_all | solution.py:264
  111.5 3.4 %shard_map.51 = f32[16,4,64,128]{3,2,1,0:T(8,128)S(1)} custom-call(s32[1]{0:T(128)} %bitcast.18.core, bf16[64,3,32,256]{3,2,1,0:T(8,128)(2,1)S(1)} %all_to_all.15.a_ref, bf16[4,2,2,3,2,64,256]{6,5,4,3,2,1,0:T(8,128)(2,1)} %bitcast.17.b_ref), custom_call_target="tpu_custom_call" | custom-call | flops 1700000000 | bytes 7000000 | tf_op jit(solution)/shard_map/pallas_call | solution.py:211
  115.0 0.1 collective-permute-start.9
  115.1 3.5 %shard_map.50 = f32[16,4,64,128]{3,2,1,0:T(8,128)S(1)} custom-call(s32[1]{0:T(128)} %bitcast.core, bf16[64,3,32,256]{3,2,1,0:T(8,128)(2,1)S(1)} %all_to_all.15.a_ref, bf16[4,2,2,3,2,64,256]{6,5,4,3,2,1,0:T(8,128)(2,1)} %bitcast.17.b_ref), custom_call_target="tpu_custom_call" | custom-call | flops 1700000000 | bytes 7000000 | tf_op jit(solution)/shard_map/pallas_call | solution.py:211
  118.6 0.7 collective-permute-done.9
  119.2 0.5 add_convert_fusion
  119.7 23.5 %all_to_all.16 = bf16[64,64,128]{2,1,0:T(8,128)(2,1)S(1)} all-to-all(bf16[64,64,128]{2,1,0:T(8,128)(2,1)S(1)} %bitcast.24), channel_id=1, replica_groups=mesh['x'=4,'y'=4,'z'=4,'core'=2] {'x','y','z'}, dimensions={0} | all-to-all | bytes 2097152 | tf_op jit(solution)/shard_map/all_to_all | solution.py:271
  143.3 0.8 convert_reduce_fusion
  (2 shorter events, 0.0 us)
Async XLA Ops:
  0.0 19.8 %copy-start = (bf16[768,768]{1,0:T(8,128)(2,1)S(1)}, bf16[768,768]{1,0:T(8,128)(2,1)}, u32[]{:S(2)}) copy-start(bf16[768,768]{1,0:T(8,128)(2,1)} %param.7) | copy-start | bytes 3538948
  4.9 20.1 %collective-permute-start.2 = (bf16[3,17,32,256]{3,2,1,0:T(8,128)(2,1)}, bf16[3,17,32,256]{3,2,1,0:T(8,128)(2,1)}, u32[]{:S(2)}, u32[]{:S(2)}) collective-permute-start(bf16[3,17,32,256]{3,2,1,0:T(8,128)(2,1)} %get-tuple-element.14.own), channel_id=1, source_target_pairs={{0,1},{1,0},{2,3},{3,2},{4,5},{5,4},{6,7},{7,6},{8,9},{9,8},{10,11... | collective-permute-start | bytes 2506760 | tf_op jit(solution)/shard_map/ppermute | solution.py:254
  5.0 23.8 %collective-permute-start.3 = (bf16[3,17,32,256]{3,2,1,0:T(8,128)(2,1)}, bf16[3,17,32,256]{3,2,1,0:T(8,128)(2,1)}, u32[]{:S(2)}, u32[]{:S(2)}) collective-permute-start(bf16[3,17,32,256]{3,2,1,0:T(8,128)(2,1)} %get-tuple-element.15), channel_id=1, source_target_pairs={{0,4},{2,6},{4,0},{6,2},{1,5},{3,7},{5,1},{7,3},{8,12},{10,14},{12... | collective-permute-start | bytes 2506760 | tf_op jit(solution)/shard_map/ppermute | solution.py:239
  9.1 37.4 %collective-permute-start = (bf16[3,17,32,256]{3,2,1,0:T(8,128)(2,1)}, bf16[3,17,32,256]{3,2,1,0:T(8,128)(2,1)}, u32[]{:S(2)}, u32[]{:S(2)}) collective-permute-start(bf16[3,17,32,256]{3,2,1,0:T(8,128)(2,1)} %get-tuple-element.13), channel_id=1, source_target_pairs={{0,2},{2,4},{4,6},{6,0},{1,3},{3,5},{5,7},{7,1},{8,10},{10,12},{12... | collective-permute-start | bytes 2506760 | tf_op jit(solution)/shard_map/ppermute | solution.py:239
  10.1 37.2 %collective-permute-start.4 = (bf16[3,17,32,256]{3,2,1,0:T(8,128)(2,1)}, bf16[3,17,32,256]{3,2,1,0:T(8,128)(2,1)}, u32[]{:S(2)}, u32[]{:S(2)}) collective-permute-start(bf16[3,17,32,256]{3,2,1,0:T(8,128)(2,1)} %get-tuple-element.17), channel_id=1, source_target_pairs={{0,6},{2,0},{4,2},{6,4},{1,7},{3,1},{5,3},{7,5},{8,14},{10,8},{12,... | collective-permute-start | bytes 2506760 | tf_op jit(solution)/shard_map/ppermute | solution.py:239
  12.3 7.2 %copy-start.2 = (s32[3,8]{1,0:T(4,128)S(1)}, s32[3,8]{1,0:T(4,128)}, u32[]{:S(2)}) copy-start(s32[3,8]{1,0:T(4,128)} %mu_ref.3) | copy-start | bytes 292
  12.3 50.2 %all-to-all-start.1 = ((bf16[16,3,2,64,256]{4,3,2,1,0:T(8,128)(2,1)}), bf16[16,3,2,64,256]{4,3,2,1,0:T(8,128)(2,1)}, u32[]{:S(2)}, u32[]{:S(2)}) async-start(bf16[16,3,2,64,256]{4,3,2,1,0:T(8,128)(2,1)} %get-tuple-element.20), calls=%async_computation.1 | async-start | bytes 6291456 | tf_op jit(solution)/shard_map/all_to_all | solution.py:240
  19.5 5.4 %collective-permute-start.1 = (s32[3,8]{1,0:T(4,128)S(1)}, s32[3,8]{1,0:T(4,128)S(1)}, u32[]{:S(2)}, u32[]{:S(2)}) collective-permute-start(s32[3,8]{1,0:T(4,128)S(1)} %copy-done.2), channel_id=1, source_target_pairs={{0,1},{1,0},{2,3},{3,2},{4,5},{5,4},{6,7},{7,6},{8,9},{9,8},{10,11... | collective-permute-start | bytes 296 | tf_op jit(solution)/shard_map/ppermute | solution.py:252
  25.0 1.2 copy-start.1
  46.5 4.8 %collective-permute-start.6 = (bf16[3,17,32,256]{3,2,1,0:T(8,128)(2,1)}, bf16[3,17,32,256]{3,2,1,0:T(8,128)(2,1)S(1)}, u32[]{:S(2)}, u32[]{:S(2)}) collective-permute-start(bf16[3,17,32,256]{3,2,1,0:T(8,128)(2,1)} %collective-permute-done.refs_0_), channel_id=1, source_target_pairs={{0,1},{1,0},{2,3},{3,2},{4,5},{5,4},{6,7},{7,6},{8,9},{9,8},{10,11... | collective-permute-start | bytes 2506760 | tf_op jit(solution)/shard_map/ppermute | solution.py:260
  47.3 4.0 %collective-permute-start.8 = (bf16[3,17,32,256]{3,2,1,0:T(8,128)(2,1)}, bf16[3,17,32,256]{3,2,1,0:T(8,128)(2,1)S(1)}, u32[]{:S(2)}, u32[]{:S(2)}) collective-permute-start(bf16[3,17,32,256]{3,2,1,0:T(8,128)(2,1)} %collective-permute-done.4.refs_2_.refs_4_), channel_id=1, source_target_pairs={{0,1},{1,0},{2,3},{3,2},{4,5},{5,4},{6,7},{7,6},{8,9},{9,8},{10,11... | collective-permute-start | bytes 2506760 | tf_op jit(solution)/shard_map/ppermute | solution.py:260
  47.3 4.2 %collective-permute-start.7 = (bf16[3,17,32,256]{3,2,1,0:T(8,128)(2,1)}, bf16[3,17,32,256]{3,2,1,0:T(8,128)(2,1)S(1)}, u32[]{:S(2)}, u32[]{:S(2)}) collective-permute-start(bf16[3,17,32,256]{3,2,1,0:T(8,128)(2,1)} %collective-permute-done.3.refs_1_.refs_2_), channel_id=1, source_target_pairs={{0,1},{1,0},{2,3},{3,2},{4,5},{5,4},{6,7},{7,6},{8,9},{9,8},{10,11... | collective-permute-start | bytes 2506760 | tf_op jit(solution)/shard_map/ppermute | solution.py:260
  48.6 2.6 %collective-permute-start.5 = (s32[12,8]{1,0:T(8,128)S(1)}, s32[12,8]{1,0:T(8,128)S(1)}, u32[]{:S(2)}, u32[]{:S(2)}) collective-permute-start(s32[12,8]{1,0:T(8,128)S(1)} %shard_map.48.mu_own), channel_id=1, source_target_pairs={{0,1},{1,0},{2,3},{3,2},{4,5},{5,4},{6,7},{7,6},{8,9},{9,8},{10,11... | collective-permute-start | bytes 1160 | tf_op jit(solution)/shard_map/ppermute | solution.py:262
  115.0 4.2 %collective-permute-start.9 = (f32[16,4,64,128]{3,2,1,0:T(8,128)S(1)}, f32[16,4,64,128]{3,2,1,0:T(8,128)S(1)}, u32[]{:S(2)}, u32[]{:S(2)}) collective-permute-start(f32[16,4,64,128]{3,2,1,0:T(8,128)S(1)} %shard_map.51), channel_id=1, source_target_pairs={{0,1},{1,0},{2,3},{3,2},{4,5},{5,4},{6,7},{7,6},{8,9},{9,8},{10,11... | collective-permute-start | bytes 6291464 | tf_op jit(solution)/shard_map/ppermute | solution.py:270

commit v5 on v4

--- a/solution.py
+++ b/solution.py
@@ -1,3 +1,5 @@
+import functools
+
 import jax
 import jax.numpy as jnp
 from jax import lax
@@ -13,70 +15,88 @@
 PAIR_FLOPS = 15_000_000_000
 
 
-def spread_kernel(z_ref, mu_ref, tensor_ref, *refs):
+def spread_kernel(mu_ref, tensor_ref, *refs):
     regrouped, blocks = refs[0], refs[1 : 1 + NZ]
-    held, turned, listed, in_sems, out_sems, cut_sems, mu_sems = refs[1 + NZ :]
+    held, turned, listed, mu, in_sems, out_sems, cut_sems, mu_sems = refs[1 + NZ :]
+    z_own = lax.axis_index("z")
     count, aux, width, pair = tensor_ref.shape
+    part = aux // 2
     loads = [
-        pltpu.make_async_copy(tensor_ref.at[m], held.at[m], in_sems.at[m])
+        pltpu.make_async_copy(
+            tensor_ref.at[m, pl.ds(h * part, part)],
+            held.at[m, pl.ds(h * part, part)],
+            in_sems.at[2 * m + h],
+        )
         for m in range(count)
+        for h in range(2)
     ]
     for load in loads:
         load.start()
+    fetch = pltpu.make_async_copy(mu_ref, mu, mu_sems.at[NZ])
+    fetch.start()
+    copies = []
+    for m in range(count):
+        loads[2 * m].wait()
+        for h in range(2):
+            if h == 1:
+                loads[2 * m + 1].wait()
+                for s in range(NZ):
+                    z = lax.rem(z_own + s, NZ)
+                    copies.append(
+                        pltpu.make_async_copy(
+                            held.at[m, pl.ds(z * 16, 16)],
+                            blocks[s].at[m, pl.ds(0, 16)],
+                            cut_sems.at[m * NZ + s],
+                        )
+                    )
+                    copies[-1].start()
+            rows = held[m, h * part : (h + 1) * part]
+            turned[m, h] = jnp.swapaxes(rows, 0, 1).reshape(NXY, 2, part, pair)
+            copies.append(
+                pltpu.make_async_copy(
+                    turned.at[m, h],
+                    regrouped.at[:, m, :, pl.ds(h * part, part)],
+                    out_sems.at[2 * m + h],
+                )
+            )
+            copies[-1].start()
+    fetch.wait()
     lane = lax.broadcasted_iota(jnp.int32, (width, pair), 1)
     for m in range(count):
         tile = jnp.zeros((width, pair), jnp.int32)
-        for k in range(mu_ref.shape[1]):
-            tile = jnp.where(lane == k, mu_ref[m, k], tile)
+        for k in range(mu.shape[1]):
+            tile = jnp.where(lane == k, mu[m, k], tile)
         listed[m, 0] = tile.astype(F32).astype(BF)
-    copies = []
     for s in range(NZ):
         to = blocks[s].at[:, pl.ds(16, 1)]
         copies.append(pltpu.make_async_copy(listed, to, mu_sems.at[s]))
         copies[-1].start()
-    for m in range(count):
-        loads[m].wait()
-        for s in range(NZ):
-            z = lax.rem(z_ref[0] + s, NZ)
-            copies.append(
-                pltpu.make_async_copy(
-                    held.at[m, pl.ds(z * 16, 16)],
-                    blocks[s].at[m, pl.ds(0, 16)],
-                    cut_sems.at[m * NZ + s],
-                )
-            )
-            copies[-1].start()
-        turned[m] = jnp.swapaxes(held[m], 0, 1).reshape(NXY, 2, aux, pair)
-        copies.append(
-            pltpu.make_async_copy(turned.at[m], regrouped.at[:, m], out_sems.at[m])
-        )
-        copies[-1].start()
     for copy in copies:
         copy.wait()
 
 
-def spread(z, mu, tensor):
+def spread(mu, tensor):
     blocks, aux, width, pair = tensor.shape
-    smem = pl.BlockSpec(memory_space=pltpu.SMEM)
     anywhere = pl.BlockSpec(memory_space=pl.ANY)
     return pl.pallas_call(
         spread_kernel,
-        in_specs=[smem, smem, anywhere],
+        in_specs=[anywhere] * 2,
         out_specs=[anywhere] * (1 + NZ),
         out_shape=[pltpu.HBM((NXY, blocks, 2, aux, pair), BF)]
         + [jax.ShapeDtypeStruct((blocks, 17, width, pair), BF)] * NZ,
         scratch_shapes=[
             pltpu.VMEM(tensor.shape, BF),
-            pltpu.VMEM((blocks, NXY, 2, aux, pair), BF),
+            pltpu.VMEM((blocks, 2, NXY, 2, aux // 2, pair), BF),
             pltpu.VMEM((blocks, 1, width, pair), BF),
-            pltpu.SemaphoreType.DMA((blocks,)),
-            pltpu.SemaphoreType.DMA((blocks,)),
+            pltpu.SMEM(mu.shape, mu.dtype),
+            pltpu.SemaphoreType.DMA((2 * blocks,)),
+            pltpu.SemaphoreType.DMA((2 * blocks,)),
             pltpu.SemaphoreType.DMA((blocks * NZ,)),
-            pltpu.SemaphoreType.DMA((NZ,)),
+            pltpu.SemaphoreType.DMA((NZ + 1,)),
         ],
         compiler_params=pltpu.CompilerParams(vmem_limit_bytes=60 * 1024 * 1024),
         cost_estimate=pl.CostEstimate(flops=1000, bytes_accessed=1000, transcendentals=0),
-    )(z, mu, tensor)
+    )(mu, tensor)
 
 
 def gathered(ref, mu, t, per, width):
@@ -120,10 +140,11 @@
     )(mu_own, mu_other, own, other, occ)
 
 
-def pair_kernel(z_ref, mu_own, mu_other, *refs):
+def pair_kernel(mu_own, mu_other, *refs):
     pieces, refs = refs[:6], refs[6:]
     occ_ref, virt_ref, early_ref, out_ref, turned, stage, result, out_sems = refs
     per, width, pair = mu_own.shape[1], 32, 256
+    z_own = lax.axis_index("z")
     for n in range(18):
         piece, m = divmod(n, 3)
         mu = mu_other if piece % 2 else mu_own
@@ -137,7 +158,7 @@
         turned[p, :, 512:576] = stage[p, :64].T
     stores = []
     for z in range(NZ):
-        s = lax.rem(z_ref[0] - z + NZ, NZ)
+        s = lax.rem(z_own - z + NZ, NZ)
         for m in range(3):
             lam = (z * 3 + m) * width
             left = turned[:, lam : lam + width, :].reshape(16 * width, -1)
@@ -155,12 +176,12 @@
         store.wait()
 
 
-def make_paired(z, mu_own, mu_other, pieces, occ, virt, early):
+def make_paired(mu_own, mu_other, pieces, occ, virt, early):
     orbitals, half = occ.shape
     smem = pl.BlockSpec(memory_space=pltpu.SMEM)
     return pl.pallas_call(
         pair_kernel,
-        in_specs=[smem] * 3 + [pl.BlockSpec(memory_space=pltpu.VMEM)] * 9,
+        in_specs=[smem] * 2 + [pl.BlockSpec(memory_space=pltpu.VMEM)] * 9,
         out_specs=pl.BlockSpec(memory_space=pltpu.HBM),
         out_shape=pltpu.HBM((NXY, NZ, 3, 32, 256), BF),
         scratch_shapes=[
@@ -173,7 +194,7 @@
         cost_estimate=pl.CostEstimate(
             flops=PAIR_FLOPS, bytes_accessed=12_000_000, transcendentals=0
         ),
-    )(z, mu_own, mu_other, *pieces, occ, virt, early)
+    )(mu_own, mu_other, *pieces, occ, virt, early)
 
 
 def listed_kernel(mu_ref, *refs):
@@ -196,37 +217,59 @@
     )(mu_block, *pieces)
 
 
-def chi_kernel(core, a_ref, b_ref, out_ref):
-    pair, parts = a_ref.shape[-1], [(m, r) for m in range(3) for r in range(2)]
-    a = jnp.concatenate(
-        [a_ref[:, m, r * 16 : (r + 1) * 16, :].reshape(-1, pair) for m, r in parts], axis=1
-    )
-    b = jnp.concatenate([b_ref[:, 0, :, m, r].reshape(-1, pair) for m, r in parts], axis=1)
-    got = lax.dot_general(a, b, (((1,), (1,)), ((), ())), preferred_element_type=F32)
-    for z in range(NZ):
-        out_ref[:, z] = got[:, z * 128 : (z + 1) * 128].reshape(-1, 64, 128)
-
-
-def chi_half(core, a, b):
-    return pl.pallas_call(
-        chi_kernel,
-        grid_spec=pltpu.PrefetchScalarGridSpec(
-            num_scalar_prefetch=1,
-            grid=(2,),
-            in_specs=[
-                pl.BlockSpec((32, 3, 32, 256), lambda i, core: (i, 0, 0, 0)),
-                pl.BlockSpec(
-                    (4, 1, 2, 3, 2, 64, 256), lambda i, core: (0, core[0], 0, 0, 0, 0, 0)
-                ),
-            ],
-            out_specs=pl.BlockSpec((8, NZ, 64, 128), lambda i, core: (i, 0, 0, 0)),
-        ),
+def chi_kernel(far, a_ref, b_ref, out_ref, held, total, sems):
+    pair = a_ref.shape[-1]
+    core = lax.rem(lax.axis_index("core") + far, NC)
+    loads = [
+        pltpu.make_async_copy(b_ref.at[:, core, :, m], held.at[m], sems.at[m])
+        for m in range(3)
+    ]
+    for load in loads:
+        load.start()
+    for m in range(3):
+        loads[m].wait()
+        b = jnp.concatenate([held[m, :, :, r].reshape(-1, pair) for r in range(2)], axis=1)
+        for i in range(2):
+            a = jnp.concatenate(
+                [
+                    a_ref[i * 32 : (i + 1) * 32, m, r * 16 : (r + 1) * 16, :].reshape(-1, pair)
+                    for r in range(2)
+                ],
+                axis=1,
+            )
+            got = lax.dot_general(a, b, (((1,), (1,)), ((), ())), preferred_element_type=F32)
+            if m == 0:
+                total[i] = got
+            elif m == 1:
+                total[i] += got
+            else:
+                got += total[i]
+                for z in range(NZ):
+                    out_ref[i * 8 : (i + 1) * 8, z] = got[:, z * 128 : (z + 1) * 128].reshape(
+                        -1, 64, 128
+                    )
+
+
+def chi_half(far, a, b):
+    vmem = pl.BlockSpec(memory_space=pltpu.VMEM)
+    return pl.pallas_call(
+        functools.partial(chi_kernel, far),
+        in_specs=[
+            vmem,
+            pl.BlockSpec(memory_space=pl.ANY),
+        ],
+        out_specs=vmem,
         out_shape=jax.ShapeDtypeStruct((NXY, NZ, 64, 128), F32),
+        scratch_shapes=[
+            pltpu.VMEM((3, 4, 2, 2, 64, 256), BF),
+            pltpu.VMEM((2, 512, 512), F32),
+            pltpu.SemaphoreType.DMA((3,)),
+        ],
         compiler_params=pltpu.CompilerParams(vmem_limit_bytes=LIMIT),
         cost_estimate=pl.CostEstimate(
             flops=1_700_000_000, bytes_accessed=7_000_000, transcendentals=0
         ),
-    )(core, a, b)
+    )(a, b)
 
 
 def shards(tensor, mu_block, green_occ, green_virt):
@@ -235,7 +278,7 @@
     other = [(0, 1), (1, 0)]
     around = [[(i, (i + s) % NZ) for i in range(NZ)] for s in range(NZ)]
 
-    regrouped, *blocks = spread(z.reshape(1), mu_block, tensor)
+    regrouped, *blocks = spread(mu_block, tensor)
     arrived = [lax.ppermute(blocks[s], "z", around[s]) if s else blocks[0] for s in range(NZ)]
     q_side = lax.all_to_all(regrouped, ("x", "y"), split_axis=0, concat_axis=0, tiled=True)
 
@@ -259,14 +302,14 @@
     mu_own = listed(mu_block, arrived)
     pieces = [q for p in arrived for q in (p, lax.ppermute(p, "core", other))]
     paired = make_paired(
-        z.reshape(1), mu_own, lax.ppermute(mu_own, "core", other), pieces, occ, virt, early
+        mu_own, lax.ppermute(mu_own, "core", other), pieces, occ, virt, early
     )
     p_side = lax.all_to_all(
         paired.reshape(NXY * NZ, 3, 32, 256), ("x", "y", "z"), 0, 0, tiled=True
     )
     q_side = q_side.reshape(4, 2, 2, 3, 2, 64, 256)
-    given = chi_half((1 - core).reshape(1), p_side, q_side)
-    kept = chi_half(core.reshape(1), p_side, q_side)
+    given = chi_half(1, p_side, q_side)
+    kept = chi_half(0, p_side, q_side)
     chi = (kept + lax.ppermute(given, "core", other)).astype(BF)
     shares = lax.all_to_all(
         chi.reshape(NXY * NZ, 64, 128), ("x", "y", "z"), 0, 0, tiled=True

time: 145 us -> 144 us (level)
  Pallas kernels: 23.9 us -> 22.4 us
    pallas_call x4, Pallas kernels: 20.4 us -> 18.9 us  [the longest x1 8.53 us: make_paired(): pl.pallas_call(pair_kernel, in_specs=[smem] * 2 + [pl.BlockSpec(memory_sp...]
where the time goes in v5:
time: 144 us; the launch traced here: 143 us
  blocking collectives  72.6 us (50%)
  waiting for transfers between devices  24.6 us (17%)
  Pallas kernels  22.4 us (16%)
  starting transfers between devices  15.6 us (11%)
  local copies, waits for them, and re-layouts  6.36 us (4%)
    all_to_all x1, blocking collectives, shards(): lax.all_to_all(paired.reshape(NXY * NZ, 3, 32, 256), ('x', 'y', 'z'), 0,...  49 us
    all_to_all x1, blocking collectives, shards(): lax.all_to_all(chi.reshape(NXY * NZ, 64, 128), ('x', 'y', 'z'), 0, 0, til...  23.6 us
    ppermute x3, waiting for transfers between devices, shards(): lax.ppermute(blocks[s], 'z', around[s])  18.4 us
    pallas_call x1, Pallas kernels, make_paired(): pl.pallas_call(pair_kernel, in_specs=[smem] * 2 + [pl.BlockSpec(memory_sp...  8.53 us
    ppermute x3, starting transfers between devices, shards(): lax.ppermute(blocks[s], 'z', around[s])  7.28 us
    all_to_all x1, starting transfers between devices, shards(): lax.all_to_all(regrouped, ('x', 'y'), split_axis=0, concat_axis=0, tiled=...  7.21 us
    pallas_call x2, Pallas kernels, chi_half(): pl.pallas_call(functools.partial(chi_kernel, far), in_specs=[vmem, pl.Blo...  6.13 us
    pallas_call x1, Pallas kernels, spread(): pl.pallas_call(spread_kernel, in_specs=[anywhere] * 2, out_specs=[anywher...  4.2 us
  transfers between devices with their start and end apart: 11, of which 7 were waited for; matrix products, arithmetic and copies ran while one was open for 4% of the time, Pallas kernels for 11%

profile of v5, /device:TPU:0, one launch (start us, length us, event | category | flops | bytes accessed | tf_op | source)
XLA Modules:
  0.0 142.9 jit_solution(6292259299696746884)
XLA Ops:
  0.0 0.0 copy-start
  0.0 4.2 %shard_map.46 = (bf16[16,3,2,64,256]{4,3,2,1,0:T(8,128)(2,1)}, bf16[3,17,32,256]{3,2,1,0:T(8,128)(2,1)}, bf16[3,17,32,256]{3,2,1,0:T(8,128)(2,1)}, bf16[3,17,32,...) custom-call(s32[3,8]{1,0:T(4,128)} %mu_ref.3, bf16[3,64,32,256]{3,2,1,0:T(8,128)(2,1)} %tensor_ref.1), custom_call_target="tpu_custom_call" | custom-call | flops 1000 | bytes 1000 | tf_op jit(solution)/shard_map/pallas_call | solution.py:81
  4.2 0.1 collective-permute-start.2
  4.3 4.0 %collective-permute-start.3 = (bf16[3,17,32,256]{3,2,1,0:T(8,128)(2,1)}, bf16[3,17,32,256]{3,2,1,0:T(8,128)(2,1)}, u32[]{:S(2)}, u32[]{:S(2)}) collective-permute-start(bf16[3,17,32,256]{3,2,1,0:T(8,128)(2,1)} %get-tuple-element.15), channel_id=1, source_target_pairs={{0,4},{2,6},{4,0},{6,2},{1,5},{3,7},{5,1},{7,3},{8,12},{10,14},{12... | collective-permute-start | bytes 2506760 | tf_op jit(solution)/shard_map/ppermute | solution.py:282
  8.3 1.0 collective-permute-start
  9.4 2.2 %collective-permute-start.4 = (bf16[3,17,32,256]{3,2,1,0:T(8,128)(2,1)}, bf16[3,17,32,256]{3,2,1,0:T(8,128)(2,1)}, u32[]{:S(2)}, u32[]{:S(2)}) collective-permute-start(bf16[3,17,32,256]{3,2,1,0:T(8,128)(2,1)} %get-tuple-element.17), channel_id=1, source_target_pairs={{0,6},{2,0},{4,2},{6,4},{1,7},{3,1},{5,3},{7,5},{8,14},{10,8},{12,... | collective-permute-start | bytes 2506760 | tf_op jit(solution)/shard_map/ppermute | solution.py:282
  11.6 0.0 copy-start.2
  11.6 7.2 %all-to-all-start.1 = ((bf16[16,3,2,64,256]{4,3,2,1,0:T(8,128)(2,1)}), bf16[16,3,2,64,256]{4,3,2,1,0:T(8,128)(2,1)}, u32[]{:S(2)}, u32[]{:S(2)}) async-start(bf16[16,3,2,64,256]{4,3,2,1,0:T(8,128)(2,1)} %get-tuple-element.20), calls=%async_computation.1 | async-start | bytes 6291456 | tf_op jit(solution)/shard_map/all_to_all | solution.py:283
  18.8 0.0 copy-done.2
  18.8 0.1 collective-permute-start.1
  19.0 0.1 stack.35
  19.1 0.0 copy-done
  19.1 0.6 gather_fusion
  19.7 0.6 copy.8
  20.4 1.6 %copy.6 = bf16[768,768]{0,1:T(8,128)(2,1)S(1)} copy(bf16[768,768]{1,0:T(8,128)(2,1)} %param.6) | data formatting | bytes 2359296 | tf_op args[2]
  22.0 0.9 constant_dynamic-slice_fusion
  22.9 1.4 copy.7.occ_ref.refs_6_
  24.2 0.0 collective-permute-done.1.mu_other
  24.3 0.0 collective-permute-done.2.other
  24.3 0.0 copy-start.1
  24.3 1.1 copy-done.1
  25.4 2.6 %shard_map.47.refs_8_ = bf16[16,384,256]{2,1,0:T(8,128)(2,1)S(1)} custom-call(s32[3,8]{1,0:T(4,128)S(1)} %copy-done.2, s32[3,8]{1,0:T(4,128)S(1)} %collective-permute-done.1.mu_other, bf16[3,17,32,256]{3,2,1,0:T(8,128)(2,1)S(1)} %copy-done.1, bf16[3,17,32,256]{3,2,1,0:T(8,128)(2,1)} %collective-permute-done.2.other, bf16[768,384]{1,0:T(8,128)(2,1)S(1)} %copy.7.occ_ref.refs_6_), custom_call_target="tpu_custom_call" | custom-call | flops 1000 | bytes 1000 | tf_op jit(solution)/shard_map/pallas_call | solution.py:132
  28.1 0.1 collective-permute-done.3.refs_1_.refs_2_
  28.2 17.6 %collective-permute-done.refs_0_ = bf16[3,17,32,256]{3,2,1,0:T(8,128)(2,1)} collective-permute-done((bf16[3,17,32,256]{3,2,1,0:T(8,128)(2,1)}, bf16[3,17,32,256]{3,2,1,0:T(8,128)(2,1)}, u32[]{:S(2)}, u32[]{:S(2)}) %collective-permute-start) | collective-permute-done | bytes 835616 | tf_op jit(solution)/shard_map/ppermute | solution.py:282
  45.7 0.0 collective-permute-start.6
  45.8 0.8 collective-permute-done.4.refs_2_.refs_4_
  46.5 0.0 collective-permute-start.8
  46.5 0.5 collective-permute-start.7
  47.0 0.9 shard_map.48.mu_own
  47.9 0.3 collective-permute-start.5
  48.2 2.3 %collective-permute-done.5.mu_other = s32[12,8]{1,0:T(8,128)S(1)} collective-permute-done((s32[12,8]{1,0:T(8,128)S(1)}, s32[12,8]{1,0:T(8,128)S(1)}, u32[]{:S(2)}, u32[]{:S(2)}) %collective-permute-start.5) | collective-permute-done | bytes 416 | tf_op jit(solution)/shard_map/ppermute | solution.py:305
  50.5 0.0 collective-permute-done.6.refs_1_
  50.5 0.0 collective-permute-done.8.refs_5_
  50.5 0.2 collective-permute-done.7.refs_3_
  50.7 8.5 %shard_map.49 = bf16[16,4,3,32,256]{4,3,2,1,0:T(8,128)(2,1)} custom-call(s32[12,8]{1,0:T(8,128)S(1)} %shard_map.48.mu_own, s32[12,8]{1,0:T(8,128)S(1)} %collective-permute-done.5.mu_other, bf16[3,17,32,256]{3,2,1,0:T(8,128)(2,1)} %collective-permute-done.refs_0_, bf16[3,17,32,256]{3,2,1,0:T(8,128)(2,1)S(1)} %collective-permute-done.6.refs_1_, ...), custom_call_target="tpu_custom_call" | custom-call | flops 15000000512 | bytes 12000000 | tf_op jit(solution)/shard_map/pallas_call | solution.py:182
  59.2 2.6 %all-to-all-done.1 = bf16[16,3,2,64,256]{4,3,2,1,0:T(8,128)(2,1)} async-done(((bf16[16,3,2,64,256]{4,3,2,1,0:T(8,128)(2,1)}), bf16[16,3,2,64,256]{4,3,2,1,0:T(8,128)(2,1)}, u32[]{:S(2)}, u32[]{:S(2)}) %all-to-all-start.1) | async-done | bytes 3145760 | tf_op jit(solution)/shard_map/all_to_all | solution.py:283
  61.8 49.0 %all_to_all.15.a_ref = bf16[64,3,32,256]{3,2,1,0:T(8,128)(2,1)S(1)} all-to-all(bf16[64,3,32,256]{3,2,1,0:T(8,128)(2,1)} %bitcast.22), channel_id=1, replica_groups=mesh['x'=4,'y'=4,'z'=4,'core'=2] {'x','y','z'}, dimensions={0} | all-to-all | bytes 6291456 | tf_op jit(solution)/shard_map/all_to_all | solution.py:307
  110.8 3.1 %shard_map.51 = f32[16,4,64,128]{3,2,1,0:T(8,128)S(1)} custom-call(bf16[64,3,32,256]{3,2,1,0:T(8,128)(2,1)S(1)} %all_to_all.15.a_ref, bf16[4,2,2,3,2,64,256]{6,5,4,3,2,1,0:T(8,128)(2,1)} %bitcast.15.b_ref), custom_call_target="tpu_custom_call" | custom-call | flops 1700000000 | bytes 7000000 | tf_op jit(solution)/shard_map/pallas_call | solution.py:255
  113.8 0.1 collective-permute-start.9
  113.9 3.1 %shard_map.50 = f32[16,4,64,128]{3,2,1,0:T(8,128)S(1)} custom-call(bf16[64,3,32,256]{3,2,1,0:T(8,128)(2,1)S(1)} %all_to_all.15.a_ref, bf16[4,2,2,3,2,64,256]{6,5,4,3,2,1,0:T(8,128)(2,1)} %bitcast.15.b_ref), custom_call_target="tpu_custom_call" | custom-call | flops 1700000000 | bytes 7000000 | tf_op jit(solution)/shard_map/pallas_call | solution.py:255
  117.0 1.1 collective-permute-done.9
  118.1 0.5 add_convert_fusion
  118.6 23.6 %all_to_all.16 = bf16[64,64,128]{2,1,0:T(8,128)(2,1)S(1)} all-to-all(bf16[64,64,128]{2,1,0:T(8,128)(2,1)S(1)} %bitcast.21), channel_id=1, replica_groups=mesh['x'=4,'y'=4,'z'=4,'core'=2] {'x','y','z'}, dimensions={0} | all-to-all | bytes 2097152 | tf_op jit(solution)/shard_map/all_to_all | solution.py:314
  142.2 0.8 convert_reduce_fusion
  (2 shorter events, 0.0 us)
Async XLA Ops:
  0.0 19.1 %copy-start = (bf16[768,768]{1,0:T(8,128)(2,1)S(1)}, bf16[768,768]{1,0:T(8,128)(2,1)}, u32[]{:S(2)}) copy-start(bf16[768,768]{1,0:T(8,128)(2,1)} %param.7) | copy-start | bytes 3538948
  4.2 20.0 %collective-permute-start.2 = (bf16[3,17,32,256]{3,2,1,0:T(8,128)(2,1)}, bf16[3,17,32,256]{3,2,1,0:T(8,128)(2,1)}, u32[]{:S(2)}, u32[]{:S(2)}) collective-permute-start(bf16[3,17,32,256]{3,2,1,0:T(8,128)(2,1)} %get-tuple-element.14.own), channel_id=1, source_target_pairs={{0,1},{1,0},{2,3},{3,2},{4,5},{5,4},{6,7},{7,6},{8,9},{9,8},{10,11... | collective-permute-start | bytes 2506760 | tf_op jit(solution)/shard_map/ppermute | solution.py:297
  4.3 23.8 %collective-permute-start.3 = (bf16[3,17,32,256]{3,2,1,0:T(8,128)(2,1)}, bf16[3,17,32,256]{3,2,1,0:T(8,128)(2,1)}, u32[]{:S(2)}, u32[]{:S(2)}) collective-permute-start(bf16[3,17,32,256]{3,2,1,0:T(8,128)(2,1)} %get-tuple-element.15), channel_id=1, source_target_pairs={{0,4},{2,6},{4,0},{6,2},{1,5},{3,7},{5,1},{7,3},{8,12},{10,14},{12... | collective-permute-start | bytes 2506760 | tf_op jit(solution)/shard_map/ppermute | solution.py:282
  8.3 37.4 %collective-permute-start = (bf16[3,17,32,256]{3,2,1,0:T(8,128)(2,1)}, bf16[3,17,32,256]{3,2,1,0:T(8,128)(2,1)}, u32[]{:S(2)}, u32[]{:S(2)}) collective-permute-start(bf16[3,17,32,256]{3,2,1,0:T(8,128)(2,1)} %get-tuple-element.13), channel_id=1, source_target_pairs={{0,2},{2,4},{4,6},{6,0},{1,3},{3,5},{5,7},{7,1},{8,10},{10,12},{12... | collective-permute-start | bytes 2506760 | tf_op jit(solution)/shard_map/ppermute | solution.py:282
  9.4 37.2 %collective-permute-start.4 = (bf16[3,17,32,256]{3,2,1,0:T(8,128)(2,1)}, bf16[3,17,32,256]{3,2,1,0:T(8,128)(2,1)}, u32[]{:S(2)}, u32[]{:S(2)}) collective-permute-start(bf16[3,17,32,256]{3,2,1,0:T(8,128)(2,1)} %get-tuple-element.17), channel_id=1, source_target_pairs={{0,6},{2,0},{4,2},{6,4},{1,7},{3,1},{5,3},{7,5},{8,14},{10,8},{12,... | collective-permute-start | bytes 2506760 | tf_op jit(solution)/shard_map/ppermute | solution.py:282
  11.6 7.2 %copy-start.2 = (s32[3,8]{1,0:T(4,128)S(1)}, s32[3,8]{1,0:T(4,128)}, u32[]{:S(2)}) copy-start(s32[3,8]{1,0:T(4,128)} %mu_ref.3) | copy-start | bytes 292
  11.6 50.2 %all-to-all-start.1 = ((bf16[16,3,2,64,256]{4,3,2,1,0:T(8,128)(2,1)}), bf16[16,3,2,64,256]{4,3,2,1,0:T(8,128)(2,1)}, u32[]{:S(2)}, u32[]{:S(2)}) async-start(bf16[16,3,2,64,256]{4,3,2,1,0:T(8,128)(2,1)} %get-tuple-element.20), calls=%async_computation.1 | async-start | bytes 6291456 | tf_op jit(solution)/shard_map/all_to_all | solution.py:283
  18.8 5.4 %collective-permute-start.1 = (s32[3,8]{1,0:T(4,128)S(1)}, s32[3,8]{1,0:T(4,128)S(1)}, u32[]{:S(2)}, u32[]{:S(2)}) collective-permute-start(s32[3,8]{1,0:T(4,128)S(1)} %copy-done.2), channel_id=1, source_target_pairs={{0,1},{1,0},{2,3},{3,2},{4,5},{5,4},{6,7},{7,6},{8,9},{9,8},{10,11... | collective-permute-start | bytes 296 | tf_op jit(solution)/shard_map/ppermute | solution.py:295
  24.3 1.2 copy-start.1
  45.7 4.8 %collective-permute-start.6 = (bf16[3,17,32,256]{3,2,1,0:T(8,128)(2,1)}, bf16[3,17,32,256]{3,2,1,0:T(8,128)(2,1)S(1)}, u32[]{:S(2)}, u32[]{:S(2)}) collective-permute-start(bf16[3,17,32,256]{3,2,1,0:T(8,128)(2,1)} %collective-permute-done.refs_0_), channel_id=1, source_target_pairs={{0,1},{1,0},{2,3},{3,2},{4,5},{5,4},{6,7},{7,6},{8,9},{9,8},{10,11... | collective-permute-start | bytes 2506760 | tf_op jit(solution)/shard_map/ppermute | solution.py:303
  46.5 4.0 %collective-permute-start.8 = (bf16[3,17,32,256]{3,2,1,0:T(8,128)(2,1)}, bf16[3,17,32,256]{3,2,1,0:T(8,128)(2,1)S(1)}, u32[]{:S(2)}, u32[]{:S(2)}) collective-permute-start(bf16[3,17,32,256]{3,2,1,0:T(8,128)(2,1)} %collective-permute-done.4.refs_2_.refs_4_), channel_id=1, source_target_pairs={{0,1},{1,0},{2,3},{3,2},{4,5},{5,4},{6,7},{7,6},{8,9},{9,8},{10,11... | collective-permute-start | bytes 2506760 | tf_op jit(solution)/shard_map/ppermute | solution.py:303
  46.5 4.2 %collective-permute-start.7 = (bf16[3,17,32,256]{3,2,1,0:T(8,128)(2,1)}, bf16[3,17,32,256]{3,2,1,0:T(8,128)(2,1)S(1)}, u32[]{:S(2)}, u32[]{:S(2)}) collective-permute-start(bf16[3,17,32,256]{3,2,1,0:T(8,128)(2,1)} %collective-permute-done.3.refs_1_.refs_2_), channel_id=1, source_target_pairs={{0,1},{1,0},{2,3},{3,2},{4,5},{5,4},{6,7},{7,6},{8,9},{9,8},{10,11... | collective-permute-start | bytes 2506760 | tf_op jit(solution)/shard_map/ppermute | solution.py:303
  47.9 2.6 %collective-permute-start.5 = (s32[12,8]{1,0:T(8,128)S(1)}, s32[12,8]{1,0:T(8,128)S(1)}, u32[]{:S(2)}, u32[]{:S(2)}) collective-permute-start(s32[12,8]{1,0:T(8,128)S(1)} %shard_map.48.mu_own), channel_id=1, source_target_pairs={{0,1},{1,0},{2,3},{3,2},{4,5},{5,4},{6,7},{7,6},{8,9},{9,8},{10,11... | collective-permute-start | bytes 1160 | tf_op jit(solution)/shard_map/ppermute | solution.py:305
  113.8 4.2 %collective-permute-start.9 = (f32[16,4,64,128]{3,2,1,0:T(8,128)S(1)}, f32[16,4,64,128]{3,2,1,0:T(8,128)S(1)}, u32[]{:S(2)}, u32[]{:S(2)}) collective-permute-start(f32[16,4,64,128]{3,2,1,0:T(8,128)S(1)} %shard_map.51), channel_id=1, source_target_pairs={{0,1},{1,0},{2,3},{3,2},{4,5},{5,4},{6,7},{7,6},{8,9},{9,8},{10,11... | collective-permute-start | bytes 6291464 | tf_op jit(solution)/shard_map/ppermute | solution.py:313

commit v6 on v5

--- a/solution.py
+++ b/solution.py
@@ -247,10 +247,10 @@
                 for z in range(NZ):
                     out_ref[i * 8 : (i + 1) * 8, z] = got[:, z * 128 : (z + 1) * 128].reshape(
                         -1, 64, 128
-                    )
-
-
-def chi_half(far, a, b):
+                    ).astype(out_ref.dtype)
+
+
+def chi_half(far, a, b, kind):
     vmem = pl.BlockSpec(memory_space=pltpu.VMEM)
     return pl.pallas_call(
         functools.partial(chi_kernel, far),
@@ -259,7 +259,7 @@
             pl.BlockSpec(memory_space=pl.ANY),
         ],
         out_specs=vmem,
-        out_shape=jax.ShapeDtypeStruct((NXY, NZ, 64, 128), F32),
+        out_shape=jax.ShapeDtypeStruct((NXY, NZ, 64, 128), kind),
         scratch_shapes=[
             pltpu.VMEM((3, 4, 2, 2, 64, 256), BF),
             pltpu.VMEM((2, 512, 512), F32),
@@ -308,8 +308,8 @@
         paired.reshape(NXY * NZ, 3, 32, 256), ("x", "y", "z"), 0, 0, tiled=True
     )
     q_side = q_side.reshape(4, 2, 2, 3, 2, 64, 256)
-    given = chi_half(1, p_side, q_side)
-    kept = chi_half(0, p_side, q_side)
+    given = chi_half(1, p_side, q_side, BF)
+    kept = chi_half(0, p_side, q_side, F32)
     chi = (kept + lax.ppermute(given, "core", other)).astype(BF)
     shares = lax.all_to_all(
         chi.reshape(NXY * NZ, 64, 128), ("x", "y", "z"), 0, 0, tiled=True

time: 144 us -> 143 us (level)
  transfers between devices with their start and end apart: 11 -> 11, of which waited for: 7 -> 6; matrix products, arithmetic and copies ran while one was open for 4% -> 4% of each run, Pallas kernels for 11% -> 11%
where the time goes in v6:
time: 143 us; the launch traced here: 142 us
  blocking collectives  73 us (51%)
  waiting for transfers between devices  23.5 us (16%)
  Pallas kernels  22.4 us (16%)
  starting transfers between devices  15.6 us (11%)
  local copies, waits for them, and re-layouts  6.36 us (4%)
    all_to_all x1, blocking collectives, shards(): lax.all_to_all(paired.reshape(NXY * NZ, 3, 32, 256), ('x', 'y', 'z'), 0,...  49 us
    all_to_all x1, blocking collectives, shards(): lax.all_to_all(chi.reshape(NXY * NZ, 64, 128), ('x', 'y', 'z'), 0, 0, til...  24 us
    ppermute x3, waiting for transfers between devices, shards(): lax.ppermute(blocks[s], 'z', around[s])  18.4 us
    pallas_call x1, Pallas kernels, make_paired(): pl.pallas_call(pair_kernel, in_specs=[smem] * 2 + [pl.BlockSpec(memory_sp...  8.53 us
    ppermute x3, starting transfers between devices, shards(): lax.ppermute(blocks[s], 'z', around[s])  7.28 us
    all_to_all x1, starting transfers between devices, shards(): lax.all_to_all(regrouped, ('x', 'y'), split_axis=0, concat_axis=0, tiled=...  7.21 us
    pallas_call x2, Pallas kernels, chi_half(): pl.pallas_call(functools.partial(chi_kernel, far), in_specs=[vmem, pl.Blo...  6.13 us
    pallas_call x1, Pallas kernels, spread(): pl.pallas_call(spread_kernel, in_specs=[anywhere] * 2, out_specs=[anywher...  4.2 us
  transfers between devices with their start and end apart: 11, of which 6 were waited for; matrix products, arithmetic and copies ran while one was open for 4% of the time, Pallas kernels for 11%

profile of v6, /device:TPU:0, one launch (start us, length us, event | category | flops | bytes accessed | tf_op | source)
XLA Modules:
  0.0 142.1 jit_solution(3322746735427879459)
XLA Ops:
  0.0 0.0 copy-start
  0.0 4.2 %shard_map.46 = (bf16[16,3,2,64,256]{4,3,2,1,0:T(8,128)(2,1)}, bf16[3,17,32,256]{3,2,1,0:T(8,128)(2,1)}, bf16[3,17,32,256]{3,2,1,0:T(8,128)(2,1)}, bf16[3,17,32,...) custom-call(s32[3,8]{1,0:T(4,128)} %mu_ref.3, bf16[3,64,32,256]{3,2,1,0:T(8,128)(2,1)} %tensor_ref.1), custom_call_target="tpu_custom_call" | custom-call | flops 1000 | bytes 1000 | tf_op jit(solution)/shard_map/pallas_call | solution.py:81
  4.2 0.1 collective-permute-start.2
  4.3 4.0 %collective-permute-start.3 = (bf16[3,17,32,256]{3,2,1,0:T(8,128)(2,1)}, bf16[3,17,32,256]{3,2,1,0:T(8,128)(2,1)}, u32[]{:S(2)}, u32[]{:S(2)}) collective-permute-start(bf16[3,17,32,256]{3,2,1,0:T(8,128)(2,1)} %get-tuple-element.15), channel_id=1, source_target_pairs={{0,4},{2,6},{4,0},{6,2},{1,5},{3,7},{5,1},{7,3},{8,12},{10,14},{12... | collective-permute-start | bytes 2506760 | tf_op jit(solution)/shard_map/ppermute | solution.py:282
  8.3 1.0 collective-permute-start
  9.4 2.2 %collective-permute-start.4 = (bf16[3,17,32,256]{3,2,1,0:T(8,128)(2,1)}, bf16[3,17,32,256]{3,2,1,0:T(8,128)(2,1)}, u32[]{:S(2)}, u32[]{:S(2)}) collective-permute-start(bf16[3,17,32,256]{3,2,1,0:T(8,128)(2,1)} %get-tuple-element.17), channel_id=1, source_target_pairs={{0,6},{2,0},{4,2},{6,4},{1,7},{3,1},{5,3},{7,5},{8,14},{10,8},{12,... | collective-permute-start | bytes 2506760 | tf_op jit(solution)/shard_map/ppermute | solution.py:282
  11.6 0.0 copy-start.2
  11.6 7.2 %all-to-all-start.1 = ((bf16[16,3,2,64,256]{4,3,2,1,0:T(8,128)(2,1)}), bf16[16,3,2,64,256]{4,3,2,1,0:T(8,128)(2,1)}, u32[]{:S(2)}, u32[]{:S(2)}) async-start(bf16[16,3,2,64,256]{4,3,2,1,0:T(8,128)(2,1)} %get-tuple-element.20), calls=%async_computation.1 | async-start | bytes 6291456 | tf_op jit(solution)/shard_map/all_to_all | solution.py:283
  18.8 0.0 copy-done.2
  18.8 0.1 collective-permute-start.1
  19.0 0.1 stack.35
  19.1 0.0 copy-done
  19.1 0.6 gather_fusion
  19.7 0.6 copy.8
  20.4 1.6 %copy.6 = bf16[768,768]{0,1:T(8,128)(2,1)S(1)} copy(bf16[768,768]{1,0:T(8,128)(2,1)} %param.6) | data formatting | bytes 2359296 | tf_op args[2]
  22.0 0.9 constant_dynamic-slice_fusion
  22.9 1.4 copy.7.occ_ref.refs_6_
  24.2 0.0 collective-permute-done.1.mu_other
  24.3 0.0 collective-permute-done.2.other
  24.3 0.0 copy-start.1
  24.3 1.1 copy-done.1
  25.4 2.6 %shard_map.47.refs_8_ = bf16[16,384,256]{2,1,0:T(8,128)(2,1)S(1)} custom-call(s32[3,8]{1,0:T(4,128)S(1)} %copy-done.2, s32[3,8]{1,0:T(4,128)S(1)} %collective-permute-done.1.mu_other, bf16[3,17,32,256]{3,2,1,0:T(8,128)(2,1)S(1)} %copy-done.1, bf16[3,17,32,256]{3,2,1,0:T(8,128)(2,1)} %collective-permute-done.2.other, bf16[768,384]{1,0:T(8,128)(2,1)S(1)} %copy.7.occ_ref.refs_6_), custom_call_target="tpu_custom_call" | custom-call | flops 1000 | bytes 1000 | tf_op jit(solution)/shard_map/pallas_call | solution.py:132
  28.1 0.1 collective-permute-done.3.refs_1_.refs_2_
  28.2 17.6 %collective-permute-done.refs_0_ = bf16[3,17,32,256]{3,2,1,0:T(8,128)(2,1)} collective-permute-done((bf16[3,17,32,256]{3,2,1,0:T(8,128)(2,1)}, bf16[3,17,32,256]{3,2,1,0:T(8,128)(2,1)}, u32[]{:S(2)}, u32[]{:S(2)}) %collective-permute-start) | collective-permute-done | bytes 835616 | tf_op jit(solution)/shard_map/ppermute | solution.py:282
  45.7 0.0 collective-permute-start.6
  45.8 0.8 collective-permute-done.4.refs_2_.refs_4_
  46.5 0.0 collective-permute-start.8
  46.5 0.5 collective-permute-start.7
  47.0 0.9 shard_map.48.mu_own
  47.9 0.3 collective-permute-start.5
  48.2 2.3 %collective-permute-done.5.mu_other = s32[12,8]{1,0:T(8,128)S(1)} collective-permute-done((s32[12,8]{1,0:T(8,128)S(1)}, s32[12,8]{1,0:T(8,128)S(1)}, u32[]{:S(2)}, u32[]{:S(2)}) %collective-permute-start.5) | collective-permute-done | bytes 416 | tf_op jit(solution)/shard_map/ppermute | solution.py:305
  50.5 0.0 collective-permute-done.6.refs_1_
  50.5 0.0 collective-permute-done.8.refs_5_
  50.5 0.2 collective-permute-done.7.refs_3_
  50.7 8.5 %shard_map.49 = bf16[16,4,3,32,256]{4,3,2,1,0:T(8,128)(2,1)} custom-call(s32[12,8]{1,0:T(8,128)S(1)} %shard_map.48.mu_own, s32[12,8]{1,0:T(8,128)S(1)} %collective-permute-done.5.mu_other, bf16[3,17,32,256]{3,2,1,0:T(8,128)(2,1)} %collective-permute-done.refs_0_, bf16[3,17,32,256]{3,2,1,0:T(8,128)(2,1)S(1)} %collective-permute-done.6.refs_1_, ...), custom_call_target="tpu_custom_call" | custom-call | flops 15000000512 | bytes 12000000 | tf_op jit(solution)/shard_map/pallas_call | solution.py:182
  59.2 2.6 %all-to-all-done.1 = bf16[16,3,2,64,256]{4,3,2,1,0:T(8,128)(2,1)} async-done(((bf16[16,3,2,64,256]{4,3,2,1,0:T(8,128)(2,1)}), bf16[16,3,2,64,256]{4,3,2,1,0:T(8,128)(2,1)}, u32[]{:S(2)}, u32[]{:S(2)}) %all-to-all-start.1) | async-done | bytes 3145760 | tf_op jit(solution)/shard_map/all_to_all | solution.py:283
  61.8 49.0 %all_to_all.15.a_ref = bf16[64,3,32,256]{3,2,1,0:T(8,128)(2,1)S(1)} all-to-all(bf16[64,3,32,256]{3,2,1,0:T(8,128)(2,1)} %bitcast.22), channel_id=1, replica_groups=mesh['x'=4,'y'=4,'z'=4,'core'=2] {'x','y','z'}, dimensions={0} | all-to-all | bytes 6291456 | tf_op jit(solution)/shard_map/all_to_all | solution.py:307
  110.8 3.1 %shard_map.51 = bf16[16,4,64,128]{3,2,1,0:T(8,128)(2,1)S(1)} custom-call(bf16[64,3,32,256]{3,2,1,0:T(8,128)(2,1)S(1)} %all_to_all.15.a_ref, bf16[4,2,2,3,2,64,256]{6,5,4,3,2,1,0:T(8,128)(2,1)} %bitcast.15.b_ref), custom_call_target="tpu_custom_call" | custom-call | flops 1700000000 | bytes 7000000 | tf_op jit(solution)/shard_map/pallas_call | solution.py:255
  113.8 0.1 collective-permute-start.9
  113.9 3.1 %shard_map.50 = f32[16,4,64,128]{3,2,1,0:T(8,128)S(1)} custom-call(bf16[64,3,32,256]{3,2,1,0:T(8,128)(2,1)S(1)} %all_to_all.15.a_ref, bf16[4,2,2,3,2,64,256]{6,5,4,3,2,1,0:T(8,128)(2,1)} %bitcast.15.b_ref), custom_call_target="tpu_custom_call" | custom-call | flops 1700000000 | bytes 7000000 | tf_op jit(solution)/shard_map/pallas_call | solution.py:255
  117.0 0.0 collective-permute-done.9
  117.0 0.3 add_convert_fusion
  117.4 24.0 %all_to_all.16 = bf16[64,64,128]{2,1,0:T(8,128)(2,1)S(1)} all-to-all(bf16[64,64,128]{2,1,0:T(8,128)(2,1)S(1)} %bitcast.21), channel_id=1, replica_groups=mesh['x'=4,'y'=4,'z'=4,'core'=2] {'x','y','z'}, dimensions={0} | all-to-all | bytes 2097152 | tf_op jit(solution)/shard_map/all_to_all | solution.py:314
  141.4 0.8 convert_reduce_fusion
  (2 shorter events, 0.0 us)
Async XLA Ops:
  0.0 19.1 %copy-start = (bf16[768,768]{1,0:T(8,128)(2,1)S(1)}, bf16[768,768]{1,0:T(8,128)(2,1)}, u32[]{:S(2)}) copy-start(bf16[768,768]{1,0:T(8,128)(2,1)} %param.7) | copy-start | bytes 3538948
  4.2 20.0 %collective-permute-start.2 = (bf16[3,17,32,256]{3,2,1,0:T(8,128)(2,1)}, bf16[3,17,32,256]{3,2,1,0:T(8,128)(2,1)}, u32[]{:S(2)}, u32[]{:S(2)}) collective-permute-start(bf16[3,17,32,256]{3,2,1,0:T(8,128)(2,1)} %get-tuple-element.14.own), channel_id=1, source_target_pairs={{0,1},{1,0},{2,3},{3,2},{4,5},{5,4},{6,7},{7,6},{8,9},{9,8},{10,11... | collective-permute-start | bytes 2506760 | tf_op jit(solution)/shard_map/ppermute | solution.py:297
  4.3 23.8 %collective-permute-start.3 = (bf16[3,17,32,256]{3,2,1,0:T(8,128)(2,1)}, bf16[3,17,32,256]{3,2,1,0:T(8,128)(2,1)}, u32[]{:S(2)}, u32[]{:S(2)}) collective-permute-start(bf16[3,17,32,256]{3,2,1,0:T(8,128)(2,1)} %get-tuple-element.15), channel_id=1, source_target_pairs={{0,4},{2,6},{4,0},{6,2},{1,5},{3,7},{5,1},{7,3},{8,12},{10,14},{12... | collective-permute-start | bytes 2506760 | tf_op jit(solution)/shard_map/ppermute | solution.py:282
  8.3 37.4 %collective-permute-start = (bf16[3,17,32,256]{3,2,1,0:T(8,128)(2,1)}, bf16[3,17,32,256]{3,2,1,0:T(8,128)(2,1)}, u32[]{:S(2)}, u32[]{:S(2)}) collective-permute-start(bf16[3,17,32,256]{3,2,1,0:T(8,128)(2,1)} %get-tuple-element.13), channel_id=1, source_target_pairs={{0,2},{2,4},{4,6},{6,0},{1,3},{3,5},{5,7},{7,1},{8,10},{10,12},{12... | collective-permute-start | bytes 2506760 | tf_op jit(solution)/shard_map/ppermute | solution.py:282
  9.4 37.2 %collective-permute-start.4 = (bf16[3,17,32,256]{3,2,1,0:T(8,128)(2,1)}, bf16[3,17,32,256]{3,2,1,0:T(8,128)(2,1)}, u32[]{:S(2)}, u32[]{:S(2)}) collective-permute-start(bf16[3,17,32,256]{3,2,1,0:T(8,128)(2,1)} %get-tuple-element.17), channel_id=1, source_target_pairs={{0,6},{2,0},{4,2},{6,4},{1,7},{3,1},{5,3},{7,5},{8,14},{10,8},{12,... | collective-permute-start | bytes 2506760 | tf_op jit(solution)/shard_map/ppermute | solution.py:282
  11.6 7.2 %copy-start.2 = (s32[3,8]{1,0:T(4,128)S(1)}, s32[3,8]{1,0:T(4,128)}, u32[]{:S(2)}) copy-start(s32[3,8]{1,0:T(4,128)} %mu_ref.3) | copy-start | bytes 292
  11.6 50.2 %all-to-all-start.1 = ((bf16[16,3,2,64,256]{4,3,2,1,0:T(8,128)(2,1)}), bf16[16,3,2,64,256]{4,3,2,1,0:T(8,128)(2,1)}, u32[]{:S(2)}, u32[]{:S(2)}) async-start(bf16[16,3,2,64,256]{4,3,2,1,0:T(8,128)(2,1)} %get-tuple-element.20), calls=%async_computation.1 | async-start | bytes 6291456 | tf_op jit(solution)/shard_map/all_to_all | solution.py:283
  18.8 5.4 %collective-permute-start.1 = (s32[3,8]{1,0:T(4,128)S(1)}, s32[3,8]{1,0:T(4,128)S(1)}, u32[]{:S(2)}, u32[]{:S(2)}) collective-permute-start(s32[3,8]{1,0:T(4,128)S(1)} %copy-done.2), channel_id=1, source_target_pairs={{0,1},{1,0},{2,3},{3,2},{4,5},{5,4},{6,7},{7,6},{8,9},{9,8},{10,11... | collective-permute-start | bytes 296 | tf_op jit(solution)/shard_map/ppermute | solution.py:295
  24.3 1.2 copy-start.1
  45.7 4.8 %collective-permute-start.6 = (bf16[3,17,32,256]{3,2,1,0:T(8,128)(2,1)}, bf16[3,17,32,256]{3,2,1,0:T(8,128)(2,1)S(1)}, u32[]{:S(2)}, u32[]{:S(2)}) collective-permute-start(bf16[3,17,32,256]{3,2,1,0:T(8,128)(2,1)} %collective-permute-done.refs_0_), channel_id=1, source_target_pairs={{0,1},{1,0},{2,3},{3,2},{4,5},{5,4},{6,7},{7,6},{8,9},{9,8},{10,11... | collective-permute-start | bytes 2506760 | tf_op jit(solution)/shard_map/ppermute | solution.py:303
  46.5 4.0 %collective-permute-start.8 = (bf16[3,17,32,256]{3,2,1,0:T(8,128)(2,1)}, bf16[3,17,32,256]{3,2,1,0:T(8,128)(2,1)S(1)}, u32[]{:S(2)}, u32[]{:S(2)}) collective-permute-start(bf16[3,17,32,256]{3,2,1,0:T(8,128)(2,1)} %collective-permute-done.4.refs_2_.refs_4_), channel_id=1, source_target_pairs={{0,1},{1,0},{2,3},{3,2},{4,5},{5,4},{6,7},{7,6},{8,9},{9,8},{10,11... | collective-permute-start | bytes 2506760 | tf_op jit(solution)/shard_map/ppermute | solution.py:303
  46.5 4.2 %collective-permute-start.7 = (bf16[3,17,32,256]{3,2,1,0:T(8,128)(2,1)}, bf16[3,17,32,256]{3,2,1,0:T(8,128)(2,1)S(1)}, u32[]{:S(2)}, u32[]{:S(2)}) collective-permute-start(bf16[3,17,32,256]{3,2,1,0:T(8,128)(2,1)} %collective-permute-done.3.refs_1_.refs_2_), channel_id=1, source_target_pairs={{0,1},{1,0},{2,3},{3,2},{4,5},{5,4},{6,7},{7,6},{8,9},{9,8},{10,11... | collective-permute-start | bytes 2506760 | tf_op jit(solution)/shard_map/ppermute | solution.py:303
  47.9 2.6 %collective-permute-start.5 = (s32[12,8]{1,0:T(8,128)S(1)}, s32[12,8]{1,0:T(8,128)S(1)}, u32[]{:S(2)}, u32[]{:S(2)}) collective-permute-start(s32[12,8]{1,0:T(8,128)S(1)} %shard_map.48.mu_own), channel_id=1, source_target_pairs={{0,1},{1,0},{2,3},{3,2},{4,5},{5,4},{6,7},{7,6},{8,9},{9,8},{10,11... | collective-permute-start | bytes 1160 | tf_op jit(solution)/shard_map/ppermute | solution.py:305
  113.8 3.2 %collective-permute-start.9 = (bf16[16,4,64,128]{3,2,1,0:T(8,128)(2,1)S(1)}, bf16[16,4,64,128]{3,2,1,0:T(8,128)(2,1)S(1)}, u32[]{:S(2)}, u32[]{:S(2)}) collective-permute-start(bf16[16,4,64,128]{3,2,1,0:T(8,128)(2,1)S(1)} %shard_map.51), channel_id=1, source_target_pairs={{0,1},{1,0},{2,3},{3,2},{4,5},{5,4},{6,7},{7,6},{8,9},{9,8},{10,11... | collective-permute-start | bytes 3145736 | tf_op jit(solution)/shard_map/ppermute | solution.py:313

commit v7 on v6

--- a/solution.py
+++ b/solution.py
@@ -142,7 +142,9 @@
 
 def pair_kernel(mu_own, mu_other, *refs):
     pieces, refs = refs[:6], refs[6:]
-    occ_ref, virt_ref, early_ref, out_ref, turned, stage, result, out_sems = refs
+    occ_ref, virt_ref, early_ref, out_ref, turned, stage, result, out_sems, early_sem = refs
+    early = pltpu.make_async_copy(early_ref, turned.at[:, :, 512:], early_sem)
+    early.start()
     per, width, pair = mu_own.shape[1], 32, 256
     z_own = lax.axis_index("z")
     for n in range(18):
@@ -153,7 +155,7 @@
         if n % 4 == 3:
             for p in range(16):
                 turned[p, :, (n - 3) * width : (n + 1) * width] = stage[p].T
-    turned[:, :, 512:] = early_ref[...]
+    early.wait()
     for p in range(16):
         turned[p, :, 512:576] = stage[p, :64].T
     stores = []
@@ -189,6 +191,7 @@
             pltpu.VMEM((16, 128, half), BF),
             pltpu.VMEM((NZ, NXY, 3, 32, 256), BF),
             pltpu.SemaphoreType.DMA((NZ,)),
+            pltpu.SemaphoreType.DMA,
         ],
         compiler_params=pltpu.CompilerParams(vmem_limit_bytes=LIMIT),
         cost_estimate=pl.CostEstimate(

time: 143 us -> 143 us (level)
  no operation moved by 1% of the time
where the time goes in v7:
time: 143 us; the launch traced here: 142 us
  blocking collectives  73 us (51%)
  waiting for transfers between devices  23.4 us (16%)
  Pallas kernels  22.5 us (16%)
  starting transfers between devices  15.6 us (11%)
  local copies, waits for them, and re-layouts  6.36 us (4%)
    all_to_all x1, blocking collectives, shards(): lax.all_to_all(paired.reshape(NXY * NZ, 3, 32, 256), ('x', 'y', 'z'), 0,...  49.1 us
    all_to_all x1, blocking collectives, shards(): lax.all_to_all(chi.reshape(NXY * NZ, 64, 128), ('x', 'y', 'z'), 0, 0, til...  23.9 us
    ppermute x3, waiting for transfers between devices, shards(): lax.ppermute(blocks[s], 'z', around[s])  18.4 us
    pallas_call x1, Pallas kernels, make_paired(): pl.pallas_call(pair_kernel, in_specs=[smem] * 2 + [pl.BlockSpec(memory_sp...  8.67 us
    ppermute x3, starting transfers between devices, shards(): lax.ppermute(blocks[s], 'z', around[s])  7.28 us
    all_to_all x1, starting transfers between devices, shards(): lax.all_to_all(regrouped, ('x', 'y'), split_axis=0, concat_axis=0, tiled=...  7.21 us
    pallas_call x2, Pallas kernels, chi_half(): pl.pallas_call(functools.partial(chi_kernel, far), in_specs=[vmem, pl.Blo...  6.13 us
    pallas_call x1, Pallas kernels, spread(): pl.pallas_call(spread_kernel, in_specs=[anywhere] * 2, out_specs=[anywher...  4.2 us
  transfers between devices with their start and end apart: 11, of which 6 were waited for; matrix products, arithmetic and copies ran while one was open for 4% of the time, Pallas kernels for 11%

profile of v7, /device:TPU:0, one launch (start us, length us, event | category | flops | bytes accessed | tf_op | source)
XLA Modules:
  0.0 142.2 jit_solution(13536399067335111987)
XLA Ops:
  0.0 0.0 copy-start
  0.0 4.2 %shard_map.46 = (bf16[16,3,2,64,256]{4,3,2,1,0:T(8,128)(2,1)}, bf16[3,17,32,256]{3,2,1,0:T(8,128)(2,1)}, bf16[3,17,32,256]{3,2,1,0:T(8,128)(2,1)}, bf16[3,17,32,...) custom-call(s32[3,8]{1,0:T(4,128)} %mu_ref.3, bf16[3,64,32,256]{3,2,1,0:T(8,128)(2,1)} %tensor_ref.1), custom_call_target="tpu_custom_call" | custom-call | flops 1000 | bytes 1000 | tf_op jit(solution)/shard_map/pallas_call | solution.py:81
  4.2 0.1 collective-permute-start.2
  4.3 4.0 %collective-permute-start.3 = (bf16[3,17,32,256]{3,2,1,0:T(8,128)(2,1)}, bf16[3,17,32,256]{3,2,1,0:T(8,128)(2,1)}, u32[]{:S(2)}, u32[]{:S(2)}) collective-permute-start(bf16[3,17,32,256]{3,2,1,0:T(8,128)(2,1)} %get-tuple-element.15), channel_id=1, source_target_pairs={{0,4},{2,6},{4,0},{6,2},{1,5},{3,7},{5,1},{7,3},{8,12},{10,14},{12... | collective-permute-start | bytes 2506760 | tf_op jit(solution)/shard_map/ppermute | solution.py:285
  8.3 1.0 collective-permute-start
  9.4 2.2 %collective-permute-start.4 = (bf16[3,17,32,256]{3,2,1,0:T(8,128)(2,1)}, bf16[3,17,32,256]{3,2,1,0:T(8,128)(2,1)}, u32[]{:S(2)}, u32[]{:S(2)}) collective-permute-start(bf16[3,17,32,256]{3,2,1,0:T(8,128)(2,1)} %get-tuple-element.17), channel_id=1, source_target_pairs={{0,6},{2,0},{4,2},{6,4},{1,7},{3,1},{5,3},{7,5},{8,14},{10,8},{12,... | collective-permute-start | bytes 2506760 | tf_op jit(solution)/shard_map/ppermute | solution.py:285
  11.6 0.0 copy-start.2
  11.6 7.2 %all-to-all-start.1 = ((bf16[16,3,2,64,256]{4,3,2,1,0:T(8,128)(2,1)}), bf16[16,3,2,64,256]{4,3,2,1,0:T(8,128)(2,1)}, u32[]{:S(2)}, u32[]{:S(2)}) async-start(bf16[16,3,2,64,256]{4,3,2,1,0:T(8,128)(2,1)} %get-tuple-element.20), calls=%async_computation.1 | async-start | bytes 6291456 | tf_op jit(solution)/shard_map/all_to_all | solution.py:286
  18.8 0.0 copy-done.2
  18.8 0.1 collective-permute-start.1
  19.0 0.1 stack.35
  19.1 0.0 copy-done
  19.1 0.6 gather_fusion
  19.7 0.6 copy.8
  20.4 1.6 %copy.6 = bf16[768,768]{0,1:T(8,128)(2,1)S(1)} copy(bf16[768,768]{1,0:T(8,128)(2,1)} %param.6) | data formatting | bytes 2359296 | tf_op args[2]
  22.0 0.9 constant_dynamic-slice_fusion
  22.9 1.4 copy.7.occ_ref.refs_6_
  24.2 0.0 collective-permute-done.1.mu_other
  24.3 0.0 collective-permute-done.2.other
  24.3 0.0 copy-start.1
  24.3 1.1 copy-done.1
  25.4 2.7 %shard_map.47.refs_8_ = bf16[16,384,256]{2,1,0:T(8,128)(2,1)S(1)} custom-call(s32[3,8]{1,0:T(4,128)S(1)} %copy-done.2, s32[3,8]{1,0:T(4,128)S(1)} %collective-permute-done.1.mu_other, bf16[3,17,32,256]{3,2,1,0:T(8,128)(2,1)S(1)} %copy-done.1, bf16[3,17,32,256]{3,2,1,0:T(8,128)(2,1)} %collective-permute-done.2.other, bf16[768,384]{1,0:T(8,128)(2,1)S(1)} %copy.7.occ_ref.refs_6_), custom_call_target="tpu_custom_call" | custom-call | flops 1000 | bytes 1000 | tf_op jit(solution)/shard_map/pallas_call | solution.py:132
  28.1 0.1 collective-permute-done.3.refs_1_.refs_2_
  28.2 17.6 %collective-permute-done.refs_0_ = bf16[3,17,32,256]{3,2,1,0:T(8,128)(2,1)} collective-permute-done((bf16[3,17,32,256]{3,2,1,0:T(8,128)(2,1)}, bf16[3,17,32,256]{3,2,1,0:T(8,128)(2,1)}, u32[]{:S(2)}, u32[]{:S(2)}) %collective-permute-start) | collective-permute-done | bytes 835616 | tf_op jit(solution)/shard_map/ppermute | solution.py:285
  45.7 0.0 collective-permute-start.6
  45.8 0.8 collective-permute-done.4.refs_2_.refs_4_
  46.5 0.0 collective-permute-start.8
  46.5 0.5 collective-permute-start.7
  47.0 0.9 shard_map.48.mu_own
  47.9 0.3 collective-permute-start.5
  48.2 2.3 %collective-permute-done.5.mu_other = s32[12,8]{1,0:T(8,128)S(1)} collective-permute-done((s32[12,8]{1,0:T(8,128)S(1)}, s32[12,8]{1,0:T(8,128)S(1)}, u32[]{:S(2)}, u32[]{:S(2)}) %collective-permute-start.5) | collective-permute-done | bytes 416 | tf_op jit(solution)/shard_map/ppermute | solution.py:308
  50.5 0.0 collective-permute-done.6.refs_1_
  50.5 0.0 collective-permute-done.8.refs_5_
  50.5 0.2 collective-permute-done.7.refs_3_
  50.7 8.7 %shard_map.49 = bf16[16,4,3,32,256]{4,3,2,1,0:T(8,128)(2,1)} custom-call(s32[12,8]{1,0:T(8,128)S(1)} %shard_map.48.mu_own, s32[12,8]{1,0:T(8,128)S(1)} %collective-permute-done.5.mu_other, bf16[3,17,32,256]{3,2,1,0:T(8,128)(2,1)} %collective-permute-done.refs_0_, bf16[3,17,32,256]{3,2,1,0:T(8,128)(2,1)S(1)} %collective-permute-done.6.refs_1_, ...), custom_call_target="tpu_custom_call" | custom-call | flops 15000000512 | bytes 12000000 | tf_op jit(solution)/shard_map/pallas_call | solution.py:184
  59.4 2.4 %all-to-all-done.1 = bf16[16,3,2,64,256]{4,3,2,1,0:T(8,128)(2,1)} async-done(((bf16[16,3,2,64,256]{4,3,2,1,0:T(8,128)(2,1)}), bf16[16,3,2,64,256]{4,3,2,1,0:T(8,128)(2,1)}, u32[]{:S(2)}, u32[]{:S(2)}) %all-to-all-start.1) | async-done | bytes 3145760 | tf_op jit(solution)/shard_map/all_to_all | solution.py:286
  61.8 49.1 %all_to_all.15.a_ref = bf16[64,3,32,256]{3,2,1,0:T(8,128)(2,1)S(1)} all-to-all(bf16[64,3,32,256]{3,2,1,0:T(8,128)(2,1)} %bitcast.22), channel_id=1, replica_groups=mesh['x'=4,'y'=4,'z'=4,'core'=2] {'x','y','z'}, dimensions={0} | all-to-all | bytes 6291456 | tf_op jit(solution)/shard_map/all_to_all | solution.py:310
  110.9 3.1 %shard_map.51 = bf16[16,4,64,128]{3,2,1,0:T(8,128)(2,1)S(1)} custom-call(bf16[64,3,32,256]{3,2,1,0:T(8,128)(2,1)S(1)} %all_to_all.15.a_ref, bf16[4,2,2,3,2,64,256]{6,5,4,3,2,1,0:T(8,128)(2,1)} %bitcast.15.b_ref), custom_call_target="tpu_custom_call" | custom-call | flops 1700000000 | bytes 7000000 | tf_op jit(solution)/shard_map/pallas_call | solution.py:258
  114.0 0.1 collective-permute-start.9
  114.1 3.1 %shard_map.50 = f32[16,4,64,128]{3,2,1,0:T(8,128)S(1)} custom-call(bf16[64,3,32,256]{3,2,1,0:T(8,128)(2,1)S(1)} %all_to_all.15.a_ref, bf16[4,2,2,3,2,64,256]{6,5,4,3,2,1,0:T(8,128)(2,1)} %bitcast.15.b_ref), custom_call_target="tpu_custom_call" | custom-call | flops 1700000000 | bytes 7000000 | tf_op jit(solution)/shard_map/pallas_call | solution.py:258
  117.2 0.0 collective-permute-done.9
  117.2 0.3 add_convert_fusion
  117.5 23.9 %all_to_all.16 = bf16[64,64,128]{2,1,0:T(8,128)(2,1)S(1)} all-to-all(bf16[64,64,128]{2,1,0:T(8,128)(2,1)S(1)} %bitcast.21), channel_id=1, replica_groups=mesh['x'=4,'y'=4,'z'=4,'core'=2] {'x','y','z'}, dimensions={0} | all-to-all | bytes 2097152 | tf_op jit(solution)/shard_map/all_to_all | solution.py:317
  141.4 0.8 convert_reduce_fusion
  (2 shorter events, 0.0 us)
Async XLA Ops:
  0.0 19.1 %copy-start = (bf16[768,768]{1,0:T(8,128)(2,1)S(1)}, bf16[768,768]{1,0:T(8,128)(2,1)}, u32[]{:S(2)}) copy-start(bf16[768,768]{1,0:T(8,128)(2,1)} %param.7) | copy-start | bytes 3538948
  4.2 20.0 %collective-permute-start.2 = (bf16[3,17,32,256]{3,2,1,0:T(8,128)(2,1)}, bf16[3,17,32,256]{3,2,1,0:T(8,128)(2,1)}, u32[]{:S(2)}, u32[]{:S(2)}) collective-permute-start(bf16[3,17,32,256]{3,2,1,0:T(8,128)(2,1)} %get-tuple-element.14.own), channel_id=1, source_target_pairs={{0,1},{1,0},{2,3},{3,2},{4,5},{5,4},{6,7},{7,6},{8,9},{9,8},{10,11... | collective-permute-start | bytes 2506760 | tf_op jit(solution)/shard_map/ppermute | solution.py:300
  4.3 23.8 %collective-permute-start.3 = (bf16[3,17,32,256]{3,2,1,0:T(8,128)(2,1)}, bf16[3,17,32,256]{3,2,1,0:T(8,128)(2,1)}, u32[]{:S(2)}, u32[]{:S(2)}) collective-permute-start(bf16[3,17,32,256]{3,2,1,0:T(8,128)(2,1)} %get-tuple-element.15), channel_id=1, source_target_pairs={{0,4},{2,6},{4,0},{6,2},{1,5},{3,7},{5,1},{7,3},{8,12},{10,14},{12... | collective-permute-start | bytes 2506760 | tf_op jit(solution)/shard_map/ppermute | solution.py:285
  8.3 37.4 %collective-permute-start = (bf16[3,17,32,256]{3,2,1,0:T(8,128)(2,1)}, bf16[3,17,32,256]{3,2,1,0:T(8,128)(2,1)}, u32[]{:S(2)}, u32[]{:S(2)}) collective-permute-start(bf16[3,17,32,256]{3,2,1,0:T(8,128)(2,1)} %get-tuple-element.13), channel_id=1, source_target_pairs={{0,2},{2,4},{4,6},{6,0},{1,3},{3,5},{5,7},{7,1},{8,10},{10,12},{12... | collective-permute-start | bytes 2506760 | tf_op jit(solution)/shard_map/ppermute | solution.py:285
  9.4 37.2 %collective-permute-start.4 = (bf16[3,17,32,256]{3,2,1,0:T(8,128)(2,1)}, bf16[3,17,32,256]{3,2,1,0:T(8,128)(2,1)}, u32[]{:S(2)}, u32[]{:S(2)}) collective-permute-start(bf16[3,17,32,256]{3,2,1,0:T(8,128)(2,1)} %get-tuple-element.17), channel_id=1, source_target_pairs={{0,6},{2,0},{4,2},{6,4},{1,7},{3,1},{5,3},{7,5},{8,14},{10,8},{12,... | collective-permute-start | bytes 2506760 | tf_op jit(solution)/shard_map/ppermute | solution.py:285
  11.6 7.2 %copy-start.2 = (s32[3,8]{1,0:T(4,128)S(1)}, s32[3,8]{1,0:T(4,128)}, u32[]{:S(2)}) copy-start(s32[3,8]{1,0:T(4,128)} %mu_ref.3) | copy-start | bytes 292
  11.6 50.2 %all-to-all-start.1 = ((bf16[16,3,2,64,256]{4,3,2,1,0:T(8,128)(2,1)}), bf16[16,3,2,64,256]{4,3,2,1,0:T(8,128)(2,1)}, u32[]{:S(2)}, u32[]{:S(2)}) async-start(bf16[16,3,2,64,256]{4,3,2,1,0:T(8,128)(2,1)} %get-tuple-element.20), calls=%async_computation.1 | async-start | bytes 6291456 | tf_op jit(solution)/shard_map/all_to_all | solution.py:286
  18.8 5.4 %collective-permute-start.1 = (s32[3,8]{1,0:T(4,128)S(1)}, s32[3,8]{1,0:T(4,128)S(1)}, u32[]{:S(2)}, u32[]{:S(2)}) collective-permute-start(s32[3,8]{1,0:T(4,128)S(1)} %copy-done.2), channel_id=1, source_target_pairs={{0,1},{1,0},{2,3},{3,2},{4,5},{5,4},{6,7},{7,6},{8,9},{9,8},{10,11... | collective-permute-start | bytes 296 | tf_op jit(solution)/shard_map/ppermute | solution.py:298
  24.3 1.2 copy-start.1
  45.7 4.8 %collective-permute-start.6 = (bf16[3,17,32,256]{3,2,1,0:T(8,128)(2,1)}, bf16[3,17,32,256]{3,2,1,0:T(8,128)(2,1)S(1)}, u32[]{:S(2)}, u32[]{:S(2)}) collective-permute-start(bf16[3,17,32,256]{3,2,1,0:T(8,128)(2,1)} %collective-permute-done.refs_0_), channel_id=1, source_target_pairs={{0,1},{1,0},{2,3},{3,2},{4,5},{5,4},{6,7},{7,6},{8,9},{9,8},{10,11... | collective-permute-start | bytes 2506760 | tf_op jit(solution)/shard_map/ppermute | solution.py:306
  46.5 4.0 %collective-permute-start.8 = (bf16[3,17,32,256]{3,2,1,0:T(8,128)(2,1)}, bf16[3,17,32,256]{3,2,1,0:T(8,128)(2,1)S(1)}, u32[]{:S(2)}, u32[]{:S(2)}) collective-permute-start(bf16[3,17,32,256]{3,2,1,0:T(8,128)(2,1)} %collective-permute-done.4.refs_2_.refs_4_), channel_id=1, source_target_pairs={{0,1},{1,0},{2,3},{3,2},{4,5},{5,4},{6,7},{7,6},{8,9},{9,8},{10,11... | collective-permute-start | bytes 2506760 | tf_op jit(solution)/shard_map/ppermute | solution.py:306
  46.5 4.2 %collective-permute-start.7 = (bf16[3,17,32,256]{3,2,1,0:T(8,128)(2,1)}, bf16[3,17,32,256]{3,2,1,0:T(8,128)(2,1)S(1)}, u32[]{:S(2)}, u32[]{:S(2)}) collective-permute-start(bf16[3,17,32,256]{3,2,1,0:T(8,128)(2,1)} %collective-permute-done.3.refs_1_.refs_2_), channel_id=1, source_target_pairs={{0,1},{1,0},{2,3},{3,2},{4,5},{5,4},{6,7},{7,6},{8,9},{9,8},{10,11... | collective-permute-start | bytes 2506760 | tf_op jit(solution)/shard_map/ppermute | solution.py:306
  47.9 2.6 %collective-permute-start.5 = (s32[12,8]{1,0:T(8,128)S(1)}, s32[12,8]{1,0:T(8,128)S(1)}, u32[]{:S(2)}, u32[]{:S(2)}) collective-permute-start(s32[12,8]{1,0:T(8,128)S(1)} %shard_map.48.mu_own), channel_id=1, source_target_pairs={{0,1},{1,0},{2,3},{3,2},{4,5},{5,4},{6,7},{7,6},{8,9},{9,8},{10,11... | collective-permute-start | bytes 1160 | tf_op jit(solution)/shard_map/ppermute | solution.py:308
  114.0 3.2 %collective-permute-start.9 = (bf16[16,4,64,128]{3,2,1,0:T(8,128)(2,1)S(1)}, bf16[16,4,64,128]{3,2,1,0:T(8,128)(2,1)S(1)}, u32[]{:S(2)}, u32[]{:S(2)}) collective-permute-start(bf16[16,4,64,128]{3,2,1,0:T(8,128)(2,1)S(1)} %shard_map.51), channel_id=1, source_target_pairs={{0,1},{1,0},{2,3},{3,2},{4,5},{5,4},{6,7},{7,6},{8,9},{9,8},{10,11... | collective-permute-start | bytes 3145736 | tf_op jit(solution)/shard_map/ppermute | solution.py:316
